TPU v7x, 32 devices: a whole 2x2x4 slice. The times are simulated.
32 devices in a mesh: group: 2 (over x), docs: 4 (over y, core), tensor: 4 (over z).
Axes of the slice: x: 2, y: 2, z: 4, core: 2. Of those that a mesh axis runs over, the one named last changes fastest.
Arguments:
- inputs: bfloat16 [8192, 8192], P(('group', 'docs'), 'tensor'), parts along dimension 0, may hold values from -6 to 6
- grads: bfloat16 [8192, 28672], P(('group', 'docs'), 'tensor'), parts along dimension 0, may hold values from -6 to 6
- proj_in: bfloat16 [8192, 64], P('tensor'), may hold values from -0.0625 to 0.0625
- proj_out: bfloat16 [28672, 64], P('tensor'), may hold values from -0.03125 to 0.03125
- queries: bfloat16 [4096, 4096], P(('group', 'docs'), 'tensor'), parts along dimension 0, may hold values from -3 to 3
- segment_ids: int32 [8, 1024], P(('group', 'docs')), parts along dimension 0, may hold values from 0 to 7, never falling along the last dimension, each value on 1 to 256 neighbouring positions
Outputs:
- scores: float32 [64, 4, 512], P(('group', 'docs'), None, 'tensor'), parts along dimension 0
There are 2 independent parts, one for each index of `group`. A program takes and returns all parts, laid end to end along the dimension named above; an argument that names none is the same for every part. Nothing has to cross between parts.
Inputs may be any that keep to these rules, and one draw needn't show every extreme that they name: `segment_ids`: within each row the ids never fall, and each of the 8 ids names between 1 and 256 tokens, one exactly 256.
All inputs are finite; a program needn't handle non-finite values.
Results may differ from a plain program's by a relative error of at most 0.0029.
Values may be sent and summed in bfloat16 or wider, within the bound.
No kernel may reach another device: no remote copies, remote signals or barrier semaphores. Data moves between devices by JAX's collectives and lax.ppermute only.
A program may use at most 64 MiB of HBM per device.

v0:
```python
import jax
import jax.numpy as jnp
from jax import lax
from jax.sharding import PartitionSpec as P

DOC_DEV = 8


def passed_along(block, axis, distance):
    devices = range(lax.axis_size(axis))
    route = [((i - distance) % len(devices), i) for i in devices]
    return lax.ppermute(block, axis, route)


def per_device(inputs, grads, proj_in, proj_out, queries, segment_ids):
    shares = lax.axis_size("tensor")
    rank = proj_in.shape[1]
    rows_share = rank // shares
    part_in = jnp.dot(inputs, proj_in, preferred_element_type=jnp.float32)
    part_out = jnp.dot(grads, proj_out, preferred_element_type=jnp.float32)
    proj_x, proj_g = lax.psum((part_in, part_out), "tensor")
    proj_rows = lax.dynamic_slice_in_dim(
        proj_g, lax.axis_index("tensor") * rows_share, rows_share, 1
    )
    doc_count = DOC_DEV
    tok_count = inputs.shape[0]
    ids = segment_ids[0]
    onehot = (ids[:, None] == jnp.arange(doc_count, dtype=jnp.int32)[None, :]).astype(jnp.float32)
    counts = jnp.sum(onehot, axis=0)
    weighted = (onehot[:, :, None] * proj_rows[:, None, :]).reshape(
        tok_count, doc_count * rows_share
    )
    summed = jnp.dot(weighted.T, proj_x, precision=lax.Precision.HIGHEST)
    summed = summed.reshape(doc_count, rows_share * rank)
    train = (summed / counts[:, None]).astype(jnp.bfloat16)
    ndev = lax.axis_size("docs")
    myself = lax.axis_index("docs")
    qrows = queries.shape[0]

    def score_block(block):
        return jnp.einsum("dk,qk->dq", train, block, preferred_element_type=jnp.float32)

    start = jnp.zeros((doc_count, ndev, qrows), jnp.float32)
    start = start.at[:, myself, :].set(score_block(queries))

    def turn_query(step, carry):
        block, totals = carry
        block = passed_along(block, "docs", 1)
        source = (myself - step) % ndev
        totals = totals.at[:, source, :].set(score_block(block))
        return (block, totals)

    block, totals = lax.fori_loop(1, ndev, turn_query, (queries, start))
    reduced = lax.psum_scatter(totals, "tensor", scatter_dimension=2, tiled=True)
    return reduced


def solution(mesh):
    in_specs = (
        P(("group", "docs"), "tensor"),
        P(("group", "docs"), "tensor"),
        P("tensor", None),
        P("tensor", None),
        P(("group", "docs"), "tensor"),
        P(("group", "docs"), None),
    )
    out_specs = P(("group", "docs"), None, "tensor")
    return jax.shard_map(
        per_device, mesh=mesh, in_specs=in_specs, out_specs=out_specs, check_vma=False
    )
```

profile of v0, /device:TPU:0, one launch (start us, length us, event | category | flops | bytes accessed | tf_op | source)
XLA Modules:
  0.0 143.8 jit_solution(13278955340444775666)
XLA Ops:
  6.5 1.3 copy.31
  7.8 4.3 %fusion.7 = f32[1024,64]{0,1:T(8,128)} fusion(bf16[1024,2048]{1,0:T(8,128)(2,1)} %param.12, bf16[2048,64]{0,1:T(8,128)(2,1)} %param.14), kind=kOutput, calls=%fused_computation.15 | convolution fusion | flops 268435456 | bytes 4718592 | tf_op jit(solution)/shard_map/dot_general | solution.py:19
  12.2 10.5 %fusion.6 = f32[1024,64]{0,1:T(8,128)} fusion(bf16[1024,7168]{1,0:T(8,128)(2,1)} %param.13, bf16[7168,64]{0,1:T(8,128)(2,1)S(1)} %copy-done), kind=kOutput, calls=%fused_computation.14 | convolution fusion | flops 939524096 | bytes 15859712 | tf_op jit(solution)/shard_map/dot_general | solution.py:20
  22.6 0.0 all-reduce.3.cloned.1.call-update
  22.7 0.0 reduce-scatter.4.cloned.1.call-start
  22.7 0.7 and_reduce_fusion.1
  23.5 0.1 fusion.5
  23.6 40.4 %all-reduce.3.cloned.1.call-done = (f32[1024,64]{0,1:T(8,128)}, f32[1024,64]{0,1:T(8,128)}) async-done(((f32[1024,64]{0,1:T(8,128)}, f32[1024,64]{0,1:T(8,128)}), (f32[1024,64]{0,1:T(8,128)}, f32[1024,64]{0,1:T(8,128)})) %all-reduce.3.cloned.1.call-update) | async-done | bytes 524304 | tf_op jit(solution)/shard_map/psum | solution.py:21
  64.0 0.8 constant_dynamic-slice_fusion
  64.9 1.5 %fusion.8 = f32[128,64]{1,0:T(8,128)S(1)} fusion(f32[1024,128]{0,1:T(8,128)S(1)} %bitcast.35, f32[1024,64]{0,1:T(8,128)} %get-tuple-element.184), kind=kOutput, calls=%fused_computation.16 | convolution fusion | flops 100663296 | bytes 819200 | tf_op jit(solution)/shard_map/dot_general | solution.py:33
  66.4 0.1 reshape.135
  66.5 0.1 divide_convert_fusion
  66.6 1.0 fusion.3
  67.6 45.7 %while.19 = (s32[]{:T(128)}, bf16[512,1024]{1,0:T(8,128)(2,1)S(1)}, f32[8,4,512]{2,0,1:T(8,128)S(1)}, s32[]{:T(128)}, bf16[8,1024]{1,0:T(8,128)(2,1)S(1)}, /*ind...) while((s32[]{:T(128)}, bf16[512,1024]{1,0:T(8,128)(2,1)S(1)}, ...), condition=%wide.region_6.7_spmd, body=%wide.region_4.6_spmd.sunk | while | flops 8392738 | bytes 7389514 | solution.py:53
  67.6 0.7 and_reduce_fusion.3
  68.3 13.5 %collective-permute-done = bf16[512,1024]{1,0:T(8,128)(2,1)S(1)} collective-permute-done((bf16[512,1024]{1,0:T(8,128)(2,1)S(1)}, bf16[512,1024]{1,0:T(8,128)(2,1)S(1)}, u32[]{:S(2)}, u32[]{:S(2)}) %collective-permute-start) | collective-permute-done | bytes 1048608 | tf_op jit(solution)/shard_map/while/body/eval_jaxpr/ppermute | solution.py:12
  81.9 0.1 copy.28
  81.9 0.9 fusion.24
  82.9 0.7 and_reduce_fusion.3
  83.6 13.5 %collective-permute-done = bf16[512,1024]{1,0:T(8,128)(2,1)S(1)} collective-permute-done((bf16[512,1024]{1,0:T(8,128)(2,1)S(1)}, bf16[512,1024]{1,0:T(8,128)(2,1)S(1)}, u32[]{:S(2)}, u32[]{:S(2)}) %collective-permute-start) | collective-permute-done | bytes 1048608 | tf_op jit(solution)/shard_map/while/body/eval_jaxpr/ppermute | solution.py:12
  97.1 0.1 copy.28
  97.2 0.9 fusion.24
  98.1 0.7 and_reduce_fusion.3
  98.8 13.5 %collective-permute-done = bf16[512,1024]{1,0:T(8,128)(2,1)S(1)} collective-permute-done((bf16[512,1024]{1,0:T(8,128)(2,1)S(1)}, bf16[512,1024]{1,0:T(8,128)(2,1)S(1)}, u32[]{:S(2)}, u32[]{:S(2)}) %collective-permute-start) | collective-permute-done | bytes 1048608 | tf_op jit(solution)/shard_map/while/body/eval_jaxpr/ppermute | solution.py:12
  112.3 0.1 copy.28
  112.4 0.9 fusion.24
  113.4 0.8 copy.14
  114.2 1.2 reshape.137
  115.4 0.0 reduce-scatter.4.cloned.1.call-update
  115.5 19.6 %reduce-scatter.4.cloned.1.call-done = f32[128,32]{1,0:T(8,128)} async-done(((f32[512,32]{1,0:T(8,128)}), f32[128,32]{1,0:T(8,128)}) %reduce-scatter.4.cloned.1.call-update) | async-done | bytes 16400
  135.1 1.0 reshape.138
  136.1 0.8 copy.15
  (13 shorter events, 0.1 us)
Async XLA Ops:
  6.5 5.6 %copy-start = (bf16[7168,64]{0,1:T(8,128)(2,1)S(1)}, bf16[7168,64]{0,1:T(8,128)(2,1)}, u32[]{:S(2)}) copy-start(bf16[7168,64]{0,1:T(8,128)(2,1)} %param.15) | copy-start | bytes 2752516
  6.5 57.5 %all-reduce.3.cloned.1.call-start = ((), (), s32[]{:S(2)}) async-start(), calls=%async_computation.2 | async-start | bytes 1048576 | tf_op jit(solution)/shard_map/psum | solution.py:21
  12.2 10.5 %copy-start.1 = (s32[3]{0:T(128)S(1)}, s32[3]{0:T(128)}, u32[]{:S(2)}) copy-start(s32[3]{0:T(128)} %constant.138.clone.1) | copy-start | bytes 40
  12.2 11.3 %copy-start.2 = (s32[1,1024]{1,0:T(1,128)S(1)}, s32[1,1024]{1,0:T(1,128)}, u32[]{:S(2)}) copy-start(s32[1,1024]{1,0:T(1,128)} %param.17) | copy-start | bytes 12292
  22.7 112.4 %reduce-scatter.4.cloned.1.call-start = ((), (), s32[]{:S(2)}) async-start(), calls=%async_computation.1 | async-start | bytes 327680
  67.6 14.2 %collective-permute-start = (bf16[512,1024]{1,0:T(8,128)(2,1)S(1)}, bf16[512,1024]{1,0:T(8,128)(2,1)S(1)}, u32[]{:S(2)}, u32[]{:S(2)}) collective-permute-start(bf16[512,1024]{1,0:T(8,128)(2,1)S(1)} %get-tuple-element.228), channel_id=1, source_target_pairs={{12,0},{0,4},{4,8},{8,12},{13,1},{1,5},{5,9},{9,13},{14,2},{2,6},{... | collective-permute-start | bytes 3145736 | tf_op jit(solution)/shard_map/while/body/eval_jaxpr/ppermute | solution.py:12
  82.9 14.2 %collective-permute-start = (bf16[512,1024]{1,0:T(8,128)(2,1)S(1)}, bf16[512,1024]{1,0:T(8,128)(2,1)S(1)}, u32[]{:S(2)}, u32[]{:S(2)}) collective-permute-start(bf16[512,1024]{1,0:T(8,128)(2,1)S(1)} %get-tuple-element.228), channel_id=1, source_target_pairs={{12,0},{0,4},{4,8},{8,12},{13,1},{1,5},{5,9},{9,13},{14,2},{2,6},{... | collective-permute-start | bytes 3145736 | tf_op jit(solution)/shard_map/while/body/eval_jaxpr/ppermute | solution.py:12
  98.1 14.2 %collective-permute-start = (bf16[512,1024]{1,0:T(8,128)(2,1)S(1)}, bf16[512,1024]{1,0:T(8,128)(2,1)S(1)}, u32[]{:S(2)}, u32[]{:S(2)}) collective-permute-start(bf16[512,1024]{1,0:T(8,128)(2,1)S(1)} %get-tuple-element.228), channel_id=1, source_target_pairs={{12,0},{0,4},{4,8},{8,12},{13,1},{1,5},{5,9},{9,13},{14,2},{2,6},{... | collective-permute-start | bytes 3145736 | tf_op jit(solution)/shard_map/while/body/eval_jaxpr/ppermute | solution.py:12
Sparse Core Ops, SparseCore 0:
  22.8 41.2 all-reduce.2
  115.6 19.4 reduce-scatter.3
where the time goes:
time: 144 us
  waiting for transfers between devices  101 us (70%)
  matrix products  20.1 us (14%)
  between operations  13.5 us (9%)
  local copies, waits for them, and re-layouts  6.37 us (4%)
  other arithmetic  3.14 us (2%)
    ppermute x3, waiting for transfers between devices, passed_along(): return lax.ppermute(block, axis, route)  40.6 us
    psum x1, waiting for transfers between devices, per_device(): proj_x, proj_g = lax.psum((part_in, part_out), 'tensor')  40.4 us
    unnamed x3, waiting for transfers between devices  19.7 us
    dot_general x1, matrix products, per_device(): part_out = jnp.dot(grads, proj_out, preferred_element_type=jnp.float32)  10.5 us
    unnamed x11, local copies, waits for them, and re-layouts  5.24 us
    dot_general x1, matrix products, per_device(): part_in = jnp.dot(inputs, proj_in, preferred_element_type=jnp.float32)  4.32 us
    dot_general x4, matrix products, score_block(): jnp.einsum('dk,qk->dq', train, block, preferred_element_type=jnp.float32)  3.79 us
    another operation x4, other arithmetic  2.89 us
  transfers between devices with their start and end apart: 5, of which 5 were waited for; matrix products, arithmetic and copies ran while one was open for 2% of the time, Pallas kernels for 0%

commit v1 on v0

v1 whole, which is shorter than its diff:
```python
import functools

import jax
import jax.numpy as jnp
from jax import lax
from jax.experimental import pallas as pl
from jax.experimental.pallas import tpu as pltpu
from jax.sharding import PartitionSpec as P

DOC_DEV = 8
F32 = jnp.float32
BF16 = jnp.bfloat16
NT = (((1,), (1,)), ((), ()))
VMEM = pl.BlockSpec(memory_space=pltpu.VMEM)
ANY = pl.BlockSpec(memory_space=pl.ANY)
PIECES = 2


def swapped(block, axis, flip):
    return lax.ppermute(block, axis, [(i, i ^ flip) for i in range(lax.axis_size(axis))])


def project_kernel(flips, x_hbm, g_hbm, px_hbm, pg_hbm, *rest):
    outs, (xb, gb, px, pg, sems, wsems) = rest[: len(flips)], rest[len(flips) :]
    me = lax.axis_index("tensor")
    rank, chunk = px.shape[0], xb.shape[1]
    kx, kg = xb.shape[2], gb.shape[2]
    total = len(flips) * PIECES

    def copies(p):
        row = pl.multiple_of((me ^ flips[p // PIECES]) * chunk, chunk)
        i = p % PIECES
        return (
            pltpu.make_async_copy(x_hbm.at[pl.ds(row, chunk), pl.ds(i * kx, kx)], xb.at[p], sems.at[0, p]),
            pltpu.make_async_copy(g_hbm.at[pl.ds(row, chunk), pl.ds(i * kg, kg)], gb.at[p], sems.at[1, p]),
        )

    weights = (
        pltpu.make_async_copy(px_hbm, px, wsems.at[0]),
        pltpu.make_async_copy(pg_hbm, pg, wsems.at[1]),
    )
    for c in weights:
        c.start()
    ahead = min(2, total)
    for p in range(ahead):
        for c in copies(p):
            c.start()
    for c in weights:
        c.wait()
    for p in range(total):
        i, out = p % PIECES, outs[p // PIECES]
        for c in copies(p):
            c.wait()
        if p + ahead < total:
            for c in copies(p + ahead):
                c.start()

        @pl.when(me >= 0)
        def _():
            dx = lax.dot_general(xb[p], px[:, i * kx : (i + 1) * kx], NT, preferred_element_type=F32).T
            dg = lax.dot_general(gb[p], pg[:, i * kg : (i + 1) * kg], NT, preferred_element_type=F32).T
            if i == 0:
                out[:rank, :] = dx
                out[rank:, :] = dg
            else:
                out[:rank, :] += dx
                out[rank:, :] += dg


def project(flips, inputs, grads, proj_in_t, proj_out_t, chunk):
    rank = proj_in_t.shape[0]
    total = len(flips) * PIECES
    kx, kg = inputs.shape[1] // PIECES, grads.shape[1] // PIECES
    return pl.pallas_call(
        functools.partial(project_kernel, flips),
        out_shape=[jax.ShapeDtypeStruct((2 * rank, chunk), F32)] * len(flips),
        in_specs=[ANY] * 4,
        out_specs=[VMEM] * len(flips),
        scratch_shapes=[
            pltpu.VMEM((total, chunk, kx), BF16),
            pltpu.VMEM((total, chunk, kg), BF16),
            pltpu.VMEM(proj_in_t.shape, BF16),
            pltpu.VMEM(proj_out_t.shape, BF16),
            pltpu.SemaphoreType.DMA((2, total)),
            pltpu.SemaphoreType.DMA((2,)),
        ],
        compiler_params=pltpu.CompilerParams(vmem_limit_bytes=32 * 2**20),
        name="project",
    )(inputs, grads, proj_in_t, proj_out_t)


def outer_kernel(shares, ids, *refs):
    parts, outs, (prod,) = refs[:shares], refs[shares : 2 * shares], refs[2 * shares :]
    me = lax.axis_index("tensor")
    rank, chunk = parts[0].shape[0] // 2, parts[0].shape[1]
    both = parts[0][...]
    for part in parts[1:]:
        both = both + part[...]
    x, g = both[:rank], both[rank:]
    own = ids[:, pl.ds(pl.multiple_of(me * chunk, chunk), chunk)]
    mask = own == lax.broadcasted_iota(jnp.int32, (DOC_DEV, chunk), 0)
    rows = jnp.concatenate([jnp.where(mask, g[i : i + 1], 0.0) for i in range(rank)], axis=0)
    rows_hi = rows.astype(BF16)
    rows_lo = (rows - rows_hi.astype(F32)).astype(BF16)
    x_hi = x.astype(BF16)
    x_lo = (x - x_hi.astype(F32)).astype(BF16)
    dot = functools.partial(lax.dot_general, dimension_numbers=NT, preferred_element_type=F32)
    total = dot(rows_hi, x_hi) + (dot(rows_hi, x_lo) + dot(rows_lo, x_hi))
    prod[...] = total.reshape(rank, DOC_DEV, rank)
    share = rank // shares
    for k in range(shares):
        first = (me ^ k) * share
        outs[k][...] = jnp.concatenate([prod[first + r] for r in range(share)], axis=1)


def outer(parts, ids):
    shares = len(parts)
    rank = parts[0].shape[0] // 2
    return pl.pallas_call(
        functools.partial(outer_kernel, shares),
        out_shape=[jax.ShapeDtypeStruct((DOC_DEV, rank * rank // shares), F32)] * shares,
        in_specs=[VMEM] * (1 + shares),
        out_specs=[VMEM] * shares,
        scratch_shapes=[pltpu.VMEM((rank, DOC_DEV, rank), F32)],
        name="outer",
    )(ids, *parts)


def train_kernel(ids, *refs):
    parts, out = refs[:-1], refs[-1]
    total = parts[0][...]
    for part in parts[1:]:
        total = total + part[...]
    hits = ids[...] == lax.broadcasted_iota(jnp.int32, (DOC_DEV, ids.shape[1]), 0)
    counts = jnp.sum(hits.astype(F32), axis=1, keepdims=True)
    train = total / counts
    half = train.shape[1] // 2
    out[...] = jnp.concatenate([train[:, :half], train[:, half:]], axis=0).astype(BF16)


def mean_gradients(parts, ids):
    width = parts[0].shape[1]
    return pl.pallas_call(
        train_kernel,
        out_shape=jax.ShapeDtypeStruct((2 * DOC_DEV, width // 2), BF16),
        in_specs=[VMEM] * (1 + len(parts)),
        out_specs=VMEM,
        name="train",
    )(ids, *parts)


def score_kernel(shares, near, far, *refs):
    trains, outs, (held,) = refs[: -shares - 1], refs[-shares - 1 : -1], refs[-1:]
    me = lax.axis_index("tensor")
    rows = []
    for train in trains:
        t = train[...].astype(F32)
        rows.append(jnp.concatenate([t[:DOC_DEV], t[DOC_DEV:]], axis=1))
    docs = jnp.concatenate(rows, axis=0).astype(BF16)
    count = docs.shape[0]
    width = near.shape[0] // shares
    for at, queries in enumerate((near, far)):
        scores = lax.dot_general(docs, queries[...], NT, preferred_element_type=F32)
        for j in range(shares):
            held[j, at * count : (at + 1) * count, :] = scores[:, j * width : (j + 1) * width]
    for k in range(shares):
        outs[k][...] = held[me ^ k]


def score(trains, near, far, shares):
    shape = (2 * DOC_DEV * len(trains), near.shape[0] // shares)
    return pl.pallas_call(
        functools.partial(score_kernel, shares),
        out_shape=[jax.ShapeDtypeStruct(shape, F32)] * shares,
        in_specs=[VMEM] * (2 + len(trains)),
        out_specs=[VMEM] * shares,
        scratch_shapes=[pltpu.VMEM((shares, *shape), F32)],
        name="score",
    )(near, far, *trains)


def add_kernel(shares, *refs):
    parts, outs = refs[:shares], refs[shares:]
    total = parts[0][...]
    for part in parts[1:]:
        total = total + part[...]
    count = total.shape[0] // 2
    for m, out in enumerate(outs):
        a = m * DOC_DEV
        out[...] = jnp.concatenate([total[a : a + DOC_DEV], total[count + a : count + a + DOC_DEV]], axis=0)


def add(parts, chips):
    return pl.pallas_call(
        functools.partial(add_kernel, len(parts)),
        out_shape=[jax.ShapeDtypeStruct((2 * DOC_DEV, parts[0].shape[1]), F32)] * chips,
        in_specs=[VMEM] * len(parts),
        out_specs=[VMEM] * chips,
        name="add",
    )(*parts)


def place_kernel(*refs):
    parts, out = refs[:-1], refs[-1]
    me = lax.axis_index("docs")
    for m, part in enumerate(parts):
        block = me ^ (2 * m)
        out[:, pl.ds(block, 1), :] = part[:DOC_DEV, :][:, None, :]
        out[:, pl.ds(block ^ 1, 1), :] = part[DOC_DEV:, :][:, None, :]


def place(parts):
    return pl.pallas_call(
        place_kernel,
        out_shape=jax.ShapeDtypeStruct((DOC_DEV, 2 * len(parts), parts[0].shape[1]), F32),
        in_specs=[VMEM] * len(parts),
        out_specs=VMEM,
        name="place",
    )(*parts)


def per_device(inputs, grads, proj_in, proj_out, queries, ids):
    shares, ndev = lax.axis_size("tensor"), lax.axis_size("docs")
    chips = ndev // 2
    chunk = inputs.shape[0] // shares
    sibling = swapped(queries, "docs", 1)
    flips = list(range(shares - 1, 0, -1))
    parts = project(flips, inputs, grads, proj_in.T, proj_out.T, chunk)
    arrived = [swapped(p, "tensor", k) for k, p in zip(flips, parts)]
    (own,) = project([0], inputs, grads, proj_in.T, proj_out.T, chunk)
    sums = outer([own] + arrived, ids)
    arrived = [swapped(sums[k], "tensor", k) for k in flips]
    train = mean_gradients([sums[0]] + arrived, ids)
    trains = [train] + [swapped(train, "docs", 2 * m) for m in range(1, chips)]
    scores = score(trains, queries, sibling, shares)
    arrived = [swapped(scores[k], "tensor", k) for k in flips]
    mine = add([scores[0]] + arrived, chips)
    return place([mine[0]] + [swapped(mine[m], "docs", 2 * m) for m in range(1, chips)])


def solution(mesh):
    in_specs = (
        P(("group", "docs"), "tensor"),
        P(("group", "docs"), "tensor"),
        P("tensor", None),
        P("tensor", None),
        P(("group", "docs"), "tensor"),
        P(("group", "docs"), None),
    )
    out_specs = P(("group", "docs"), None, "tensor")
    return jax.shard_map(
        per_device, mesh=mesh, in_specs=in_specs, out_specs=out_specs, check_vma=False
    )
```

time: 144 us -> 69 us (0.48)
  waiting for transfers between devices: 101 us -> 18.3 us
  matrix products: 20.1 us -> 0 us
  Pallas kernels: 0 us -> 17.8 us
  starting transfers between devices: 0.05 us -> 17.6 us
  between operations: 13.5 us -> 0.07 us
  local copies, waits for them, and re-layouts: 6.37 us -> 14.8 us
  other arithmetic: 3.14 us -> 0 us
    psum x1 -> x0, waiting for transfers between devices: 40.4 us -> none  [per_device(): proj_x, proj_g = lax.psum((part_in, part_out), 'tensor')]
    ppermute x3 -> x12, waiting for transfers between devices: 40.6 us -> 18.3 us  [swapped(): lax.ppermute(block, axis, [(i, i ^ flip) for i in range(lax.axis_size(axi...]
    dot_general x7 -> x0, matrix products: 20.1 us -> none  [the longest x1 10.5 us: per_device(): part_out = jnp.dot(grads, proj_out, preferred_element_type=jnp.float32)]
    unnamed x3 -> x0, waiting for transfers between devices: 19.7 us -> none
    pallas_call x0 -> x7, Pallas kernels: none -> 17.8 us  [the longest x2 8.5 us: project(): pl.pallas_call(functools.partial(project_kernel, flips), out_shape=[jax.S...]
    ppermute x3 -> x12, starting transfers between devices: 0.01 us -> 17.6 us  [swapped(): lax.ppermute(block, axis, [(i, i ^ flip) for i in range(lax.axis_size(axi...]
    unnamed x11 -> x34, local copies, waits for them, and re-layouts: 5.24 us -> 14.8 us
    another operation x4 -> x0, other arithmetic: 2.89 us -> none
  transfers between devices with their start and end apart: 5 -> 12, of which waited for: 5 -> 8; matrix products, arithmetic and copies ran while one was open for 2% -> 0% of each run, Pallas kernels for 0% -> 18%
where the time goes in v1:
time: 69 us; the launch traced here: 68.6 us
  waiting for transfers between devices  18.3 us (27%)
  Pallas kernels  17.8 us (26%)
  starting transfers between devices  17.6 us (26%)
  local copies, waits for them, and re-layouts  14.8 us (21%)
    ppermute x12, waiting for transfers between devices, swapped(): lax.ppermute(block, axis, [(i, i ^ flip) for i in range(lax.axis_size(axi...  18.3 us
    ppermute x12, starting transfers between devices, swapped(): lax.ppermute(block, axis, [(i, i ^ flip) for i in range(lax.axis_size(axi...  17.6 us
    unnamed x34, local copies, waits for them, and re-layouts  14.8 us
    pallas_call x2, Pallas kernels, project(): pl.pallas_call(functools.partial(project_kernel, flips), out_shape=[jax.S...  8.5 us
    pallas_call x1, Pallas kernels, score(): pl.pallas_call(functools.partial(score_kernel, shares), out_shape=[jax.Sh...  2.83 us
    pallas_call x1, Pallas kernels, outer(): pl.pallas_call(functools.partial(outer_kernel, shares), out_shape=[jax.Sh...  2.22 us
    pallas_call x1, Pallas kernels, mean_gradients(): pl.pallas_call(train_kernel, out_shape=jax.ShapeDtypeStruct((2 * DOC_DEV,...  1.52 us
  transfers between devices with their start and end apart: 12, of which 8 were waited for; matrix products, arithmetic and copies ran while one was open for 0% of the time, Pallas kernels for 18%

profile of v1, /device:TPU:0, one launch (start us, length us, event | category | flops | bytes accessed | tf_op | source)
XLA Modules:
  0.0 68.6 jit_solution(17935462101338913022)
XLA Ops:
  0.5 5.2 %copy-done = bf16[1024,7168]{1,0:T(8,128)(2,1)S(1)} copy-done((bf16[1024,7168]{1,0:T(8,128)(2,1)S(1)}, bf16[1024,7168]{1,0:T(8,128)(2,1)}, u32[]{:S(2)}) %copy-start) | copy-done | bytes 14680088
  5.6 2.2 %copy-done.1 = bf16[1024,2048]{1,0:T(8,128)(2,1)S(1)} copy-done((bf16[1024,2048]{1,0:T(8,128)(2,1)S(1)}, bf16[1024,2048]{1,0:T(8,128)(2,1)}, u32[]{:S(2)}) %copy-start.1) | copy-done | bytes 4194328
  7.8 1.2 %copy-done.2 = bf16[7168,64]{0,1:T(8,128)(2,1)S(1)} copy-done((bf16[7168,64]{0,1:T(8,128)(2,1)S(1)}, bf16[7168,64]{0,1:T(8,128)(2,1)}, u32[]{:S(2)}) %copy-start.2) | copy-done | bytes 917528
  9.0 0.9 %copy-done.3 = bf16[2048,64]{0,1:T(8,128)(2,1)S(1)} copy-done((bf16[2048,64]{0,1:T(8,128)(2,1)S(1)}, bf16[2048,64]{0,1:T(8,128)(2,1)}, u32[]{:S(2)}) %copy-start.3) | copy-done | bytes 262168
  9.9 6.2 %project.3 = (f32[128,256]{1,0:T(8,128)S(1)}, f32[128,256]{1,0:T(8,128)S(1)}, f32[128,256]{1,0:T(8,128)S(1)}) custom-call(bf16[1024,2048]{1,0:T(8,128)(2,1)S(1)} %copy-done.1, bf16[1024,7168]{1,0:T(8,128)(2,1)S(1)} %copy-done, bf16[64,2048]{1,0:T(8,128)(2,1)S(1)} %bitcast.4, bf16[64,7168]{1,0:T(8,128)(2,1)S(1)} %bitcast.2), custom_call_target="tpu_custom_call" | custom-call | tf_op jit(solution)/shard_map/project/pallas_call | solution.py:74
  16.2 4.7 %collective-permute-start.1 = (f32[128,256]{1,0:T(8,128)S(1)}, f32[128,256]{1,0:T(8,128)S(1)}, u32[]{:S(2)}, u32[]{:S(2)}) collective-permute-start(f32[128,256]{1,0:T(8,128)S(1)} %get-tuple-element.18), channel_id=1, source_target_pairs={{0,3},{1,2},{2,1},{3,0},{4,7},{5,6},{6,5},{7,4},{8,11},{9,10},{10,... | collective-permute-start | bytes 393224 | tf_op jit(solution)/shard_map/ppermute | solution.py:20
  20.9 0.6 collective-permute-start.3
  21.5 2.3 %project.2.refs_0_ = f32[128,256]{1,0:T(8,128)S(1)} custom-call(bf16[1024,2048]{1,0:T(8,128)(2,1)S(1)} %copy-done.1, bf16[1024,7168]{1,0:T(8,128)(2,1)S(1)} %copy-done, bf16[64,2048]{1,0:T(8,128)(2,1)S(1)} %bitcast.5, bf16[64,7168]{1,0:T(8,128)(2,1)S(1)} %bitcast.3), custom_call_target="tpu_custom_call" | custom-call | tf_op jit(solution)/shard_map/project/pallas_call | solution.py:74
  23.8 0.6 copy-done.4
  24.4 0.9 %collective-permute-done.1.refs_1_ = f32[128,256]{1,0:T(8,128)S(1)} collective-permute-done((f32[128,256]{1,0:T(8,128)S(1)}, f32[128,256]{1,0:T(8,128)S(1)}, u32[]{:S(2)}, u32[]{:S(2)}) %collective-permute-start.1) | collective-permute-done | bytes 131104 | tf_op jit(solution)/shard_map/ppermute | solution.py:20
  25.3 7.3 %collective-permute-done.2.refs_2_ = f32[128,256]{1,0:T(8,128)S(1)} collective-permute-done((f32[128,256]{1,0:T(8,128)S(1)}, f32[128,256]{1,0:T(8,128)S(1)}, u32[]{:S(2)}, u32[]{:S(2)}) %collective-permute-start.2) | collective-permute-done | bytes 131104 | tf_op jit(solution)/shard_map/ppermute | solution.py:20
  32.6 0.7 copy-done.7
  33.3 0.7 copy-done.8
  33.9 2.2 %outer.1 = (f32[8,1024]{1,0:T(8,128)}, f32[8,1024]{1,0:T(8,128)}, f32[8,1024]{1,0:T(8,128)}, f32[8,1024]{1,0:T(8,128)}) custom-call(s32[1,1024]{1,0:T(1,128)} %ids.3, f32[128,256]{1,0:T(8,128)} %copy-done.4, f32[128,256]{1,0:T(8,128)} %copy-done.6, f32[128,256]{1,0:T(8,128)} %copy-done.7, f32[128,256]{1,0:T(8,128)} %copy-done.8), custom_call_target="tpu_custom_call" | custom-call | tf_op jit(solution)/shard_map/outer/pallas_call | solution.py:119
  36.1 2.5 %collective-permute-start.4 = (f32[8,1024]{1,0:T(8,128)}, f32[8,1024]{1,0:T(8,128)S(1)}, u32[]{:S(2)}, u32[]{:S(2)}) collective-permute-start(f32[8,1024]{1,0:T(8,128)} %get-tuple-element.22), channel_id=1, source_target_pairs={{0,3},{1,2},{2,1},{3,0},{4,7},{5,6},{6,5},{7,4},{8,11},{9,10},{10,... | collective-permute-start | bytes 98312 | tf_op jit(solution)/shard_map/ppermute | solution.py:20
  38.6 1.9 %collective-permute-start.6 = (f32[8,1024]{1,0:T(8,128)}, f32[8,1024]{1,0:T(8,128)S(1)}, u32[]{:S(2)}, u32[]{:S(2)}) collective-permute-start(f32[8,1024]{1,0:T(8,128)} %get-tuple-element.24), channel_id=1, source_target_pairs={{0,1},{1,0},{2,3},{3,2},{4,5},{5,4},{6,7},{7,6},{8,9},{9,8},{10,11... | collective-permute-start | bytes 98312 | tf_op jit(solution)/shard_map/ppermute | solution.py:20
  40.5 1.6 %collective-permute-done.4.refs_1_ = f32[8,1024]{1,0:T(8,128)S(1)} collective-permute-done((f32[8,1024]{1,0:T(8,128)}, f32[8,1024]{1,0:T(8,128)S(1)}, u32[]{:S(2)}, u32[]{:S(2)}) %collective-permute-start.4) | collective-permute-done | bytes 32800 | tf_op jit(solution)/shard_map/ppermute | solution.py:20
  42.1 1.6 %collective-permute-done.5.refs_2_ = f32[8,1024]{1,0:T(8,128)S(1)} collective-permute-done((f32[8,1024]{1,0:T(8,128)}, f32[8,1024]{1,0:T(8,128)S(1)}, u32[]{:S(2)}, u32[]{:S(2)}) %collective-permute-start.5) | collective-permute-done | bytes 32800 | tf_op jit(solution)/shard_map/ppermute | solution.py:20
  44.3 1.5 %train.1.refs_0_ = bf16[16,512]{1,0:T(8,128)(2,1)} custom-call(s32[1,1024]{1,0:T(1,128)} %ids.3, f32[8,1024]{1,0:T(8,128)} %get-tuple-element.21.refs_0_, f32[8,1024]{1,0:T(8,128)} %copy-done.9, f32[8,1024]{1,0:T(8,128)} %copy-done.10, f32[8,1024]{1,0:T(8,128)} %copy-done.11), custom_call_target="tpu_custom_call" | custom-call | tf_op jit(solution)/shard_map/train/pallas_call | solution.py:143
  45.8 1.5 %collective-permute-start.7 = (bf16[16,512]{1,0:T(8,128)(2,1)}, bf16[16,512]{1,0:T(8,128)(2,1)S(1)}, u32[]{:S(2)}, u32[]{:S(2)}) collective-permute-start(bf16[16,512]{1,0:T(8,128)(2,1)} %train.1.refs_0_), channel_id=1, source_target_pairs={{0,8},{4,12},{8,0},{12,4},{1,9},{5,13},{9,1},{13,5},{2,10},{6,14},... | collective-permute-start | bytes 49160 | tf_op jit(solution)/shard_map/ppermute | solution.py:20
  47.3 2.4 %collective-permute-done.7.refs_1_ = bf16[16,512]{1,0:T(8,128)(2,1)S(1)} collective-permute-done((bf16[16,512]{1,0:T(8,128)(2,1)}, bf16[16,512]{1,0:T(8,128)(2,1)S(1)}, u32[]{:S(2)}, u32[]{:S(2)}) %collective-permute-start.7) | collective-permute-done | bytes 16416 | tf_op jit(solution)/shard_map/ppermute | solution.py:20
  50.4 1.0 %copy-done.5 = bf16[512,1024]{1,0:T(8,128)(2,1)} copy-done((bf16[512,1024]{1,0:T(8,128)(2,1)}, bf16[512,1024]{1,0:T(8,128)(2,1)S(1)}, u32[]{:S(2)}) %copy-start.5) | copy-done | bytes 1048600
  51.3 2.8 %score.1 = (f32[32,128]{1,0:T(8,128)}, f32[32,128]{1,0:T(8,128)}, f32[32,128]{1,0:T(8,128)}, f32[32,128]{1,0:T(8,128)}) custom-call(bf16[512,1024]{1,0:T(8,128)(2,1)} %near.1, bf16[512,1024]{1,0:T(8,128)(2,1)} %copy-done.5, bf16[16,512]{1,0:T(8,128)(2,1)} %train.1.refs_0_, bf16[16,512]{1,0:T(8,128)(2,1)} %copy-done.12), custom_call_target="tpu_custom_call" | custom-call | tf_op jit(solution)/shard_map/score/pallas_call | solution.py:172
  54.2 1.8 %collective-permute-start.8 = (f32[32,128]{1,0:T(8,128)}, f32[32,128]{1,0:T(8,128)S(1)}, u32[]{:S(2)}, u32[]{:S(2)}) collective-permute-start(f32[32,128]{1,0:T(8,128)} %get-tuple-element.26), channel_id=1, source_target_pairs={{0,3},{1,2},{2,1},{3,0},{4,7},{5,6},{6,5},{7,4},{8,11},{9,10},{10,... | collective-permute-start | bytes 49160 | tf_op jit(solution)/shard_map/ppermute | solution.py:20
  55.9 0.7 collective-permute-start.9
  56.6 1.9 %collective-permute-start.10 = (f32[32,128]{1,0:T(8,128)}, f32[32,128]{1,0:T(8,128)S(1)}, u32[]{:S(2)}, u32[]{:S(2)}) collective-permute-start(f32[32,128]{1,0:T(8,128)} %get-tuple-element.28), channel_id=1, source_target_pairs={{0,1},{1,0},{2,3},{3,2},{4,5},{5,4},{6,7},{7,6},{8,9},{9,8},{10,11... | collective-permute-start | bytes 49160 | tf_op jit(solution)/shard_map/ppermute | solution.py:20
  58.5 1.4 %collective-permute-done.8.refs_1_ = f32[32,128]{1,0:T(8,128)S(1)} collective-permute-done((f32[32,128]{1,0:T(8,128)}, f32[32,128]{1,0:T(8,128)S(1)}, u32[]{:S(2)}, u32[]{:S(2)}) %collective-permute-start.8) | collective-permute-done | bytes 16416 | tf_op jit(solution)/shard_map/ppermute | solution.py:20
  59.9 0.9 %collective-permute-done.9.refs_2_ = f32[32,128]{1,0:T(8,128)S(1)} collective-permute-done((f32[32,128]{1,0:T(8,128)}, f32[32,128]{1,0:T(8,128)S(1)}, u32[]{:S(2)}, u32[]{:S(2)}) %collective-permute-start.9) | collective-permute-done | bytes 16416 | tf_op jit(solution)/shard_map/ppermute | solution.py:20
  61.4 1.4 %add.1 = (f32[16,128]{1,0:T(8,128)}, f32[16,128]{1,0:T(8,128)}) custom-call(f32[32,128]{1,0:T(8,128)} %get-tuple-element.25.refs_0_, f32[32,128]{1,0:T(8,128)} %copy-done.13, f32[32,128]{1,0:T(8,128)} %copy-done.14, f32[32,128]{1,0:T(8,128)} %copy-done.15), custom_call_target="tpu_custom_call" | custom-call | tf_op jit(solution)/shard_map/add/pallas_call | solution.py:194
  62.8 1.5 %collective-permute-start.11 = (f32[16,128]{1,0:T(8,128)}, f32[16,128]{1,0:T(8,128)S(1)}, u32[]{:S(2)}, u32[]{:S(2)}) collective-permute-start(f32[16,128]{1,0:T(8,128)} %get-tuple-element.30), channel_id=1, source_target_pairs={{0,8},{4,12},{8,0},{12,4},{1,9},{5,13},{9,1},{13,5},{2,10},{6,14},... | collective-permute-start | bytes 24584 | tf_op jit(solution)/shard_map/ppermute | solution.py:20
  64.3 2.3 %collective-permute-done.11.refs_1_ = f32[16,128]{1,0:T(8,128)S(1)} collective-permute-done((f32[16,128]{1,0:T(8,128)}, f32[16,128]{1,0:T(8,128)S(1)}, u32[]{:S(2)}, u32[]{:S(2)}) %collective-permute-start.11) | collective-permute-done | bytes 8224 | tf_op jit(solution)/shard_map/ppermute | solution.py:20
  67.2 1.3 %place.1 = f32[8,4,128]{2,1,0:T(4,128)} custom-call(f32[16,128]{1,0:T(8,128)} %get-tuple-element.29.refs_0_, f32[16,128]{1,0:T(8,128)} %copy-done.16), custom_call_target="tpu_custom_call" | custom-call | tf_op jit(solution)/shard_map/place/pallas_call | solution.py:213
  (33 shorter events, 2.9 us)
Async XLA Ops:
  0.0 49.8 %collective-permute-start = (bf16[512,1024]{1,0:T(8,128)(2,1)}, bf16[512,1024]{1,0:T(8,128)(2,1)S(1)}, u32[]{:S(2)}, u32[]{:S(2)}) collective-permute-start(bf16[512,1024]{1,0:T(8,128)(2,1)} %near.1), channel_id=1, source_target_pairs={{0,4},{4,0},{8,12},{12,8},{1,5},{5,1},{9,13},{13,9},{2,6},{6,2},{1... | collective-permute-start | bytes 3145736 | tf_op jit(solution)/shard_map/ppermute | solution.py:20
  0.5 5.2 %copy-start = (bf16[1024,7168]{1,0:T(8,128)(2,1)S(1)}, bf16[1024,7168]{1,0:T(8,128)(2,1)}, u32[]{:S(2)}) copy-start(bf16[1024,7168]{1,0:T(8,128)(2,1)} %g_hbm.3) | copy-start | bytes 44040196
  5.6 2.2 %copy-start.1 = (bf16[1024,2048]{1,0:T(8,128)(2,1)S(1)}, bf16[1024,2048]{1,0:T(8,128)(2,1)}, u32[]{:S(2)}) copy-start(bf16[1024,2048]{1,0:T(8,128)(2,1)} %x_hbm.3) | copy-start | bytes 12582916
  7.8 1.2 %copy-start.2 = (bf16[7168,64]{0,1:T(8,128)(2,1)S(1)}, bf16[7168,64]{0,1:T(8,128)(2,1)}, u32[]{:S(2)}) copy-start(bf16[7168,64]{0,1:T(8,128)(2,1)} %param.9) | copy-start | bytes 2752516
  9.0 0.9 %copy-start.3 = (bf16[2048,64]{0,1:T(8,128)(2,1)S(1)}, bf16[2048,64]{0,1:T(8,128)(2,1)}, u32[]{:S(2)}) copy-start(bf16[2048,64]{0,1:T(8,128)(2,1)} %param.8) | copy-start | bytes 786436
  16.2 9.1 %collective-permute-start.1 = (f32[128,256]{1,0:T(8,128)S(1)}, f32[128,256]{1,0:T(8,128)S(1)}, u32[]{:S(2)}, u32[]{:S(2)}) collective-permute-start(f32[128,256]{1,0:T(8,128)S(1)} %get-tuple-element.18), channel_id=1, source_target_pairs={{0,3},{1,2},{2,1},{3,0},{4,7},{5,6},{6,5},{7,4},{8,11},{9,10},{10,... | collective-permute-start | bytes 393224 | tf_op jit(solution)/shard_map/ppermute | solution.py:20
  20.9 11.7 %collective-permute-start.2 = (f32[128,256]{1,0:T(8,128)S(1)}, f32[128,256]{1,0:T(8,128)S(1)}, u32[]{:S(2)}, u32[]{:S(2)}) collective-permute-start(f32[128,256]{1,0:T(8,128)S(1)} %get-tuple-element.19), channel_id=1, source_target_pairs={{0,2},{1,3},{2,0},{3,1},{4,6},{5,7},{6,4},{7,5},{8,10},{9,11},{10,... | collective-permute-start | bytes 393224 | tf_op jit(solution)/shard_map/ppermute | solution.py:20
  20.9 11.7 %collective-permute-start.3 = (f32[128,256]{1,0:T(8,128)S(1)}, f32[128,256]{1,0:T(8,128)S(1)}, u32[]{:S(2)}, u32[]{:S(2)}) collective-permute-start(f32[128,256]{1,0:T(8,128)S(1)} %get-tuple-element.20), channel_id=1, source_target_pairs={{0,1},{1,0},{2,3},{3,2},{4,5},{5,4},{6,7},{7,6},{8,9},{9,8},{10,11... | collective-permute-start | bytes 393224 | tf_op jit(solution)/shard_map/ppermute | solution.py:20
  23.8 0.7 copy-start.4
  25.3 7.3 %copy-start.6 = (f32[128,256]{1,0:T(8,128)}, f32[128,256]{1,0:T(8,128)S(1)}, u32[]{:S(2)}) copy-start(f32[128,256]{1,0:T(8,128)S(1)} %collective-permute-done.1.refs_1_) | copy-start | bytes 393220
  32.6 0.7 copy-start.7
  33.3 0.7 copy-start.8
  36.1 6.0 %collective-permute-start.4 = (f32[8,1024]{1,0:T(8,128)}, f32[8,1024]{1,0:T(8,128)S(1)}, u32[]{:S(2)}, u32[]{:S(2)}) collective-permute-start(f32[8,1024]{1,0:T(8,128)} %get-tuple-element.22), channel_id=1, source_target_pairs={{0,3},{1,2},{2,1},{3,0},{4,7},{5,6},{6,5},{7,4},{8,11},{9,10},{10,... | collective-permute-start | bytes 98312 | tf_op jit(solution)/shard_map/ppermute | solution.py:20
  38.6 5.0 %collective-permute-start.5 = (f32[8,1024]{1,0:T(8,128)}, f32[8,1024]{1,0:T(8,128)S(1)}, u32[]{:S(2)}, u32[]{:S(2)}) collective-permute-start(f32[8,1024]{1,0:T(8,128)} %get-tuple-element.23), channel_id=1, source_target_pairs={{0,2},{1,3},{2,0},{3,1},{4,6},{5,7},{6,4},{7,5},{8,10},{9,11},{10,... | collective-permute-start | bytes 98312 | tf_op jit(solution)/shard_map/ppermute | solution.py:20
  38.6 5.0 %collective-permute-start.6 = (f32[8,1024]{1,0:T(8,128)}, f32[8,1024]{1,0:T(8,128)S(1)}, u32[]{:S(2)}, u32[]{:S(2)}) collective-permute-start(f32[8,1024]{1,0:T(8,128)} %get-tuple-element.24), channel_id=1, source_target_pairs={{0,1},{1,0},{2,3},{3,2},{4,5},{5,4},{6,7},{7,6},{8,9},{9,8},{10,11... | collective-permute-start | bytes 98312 | tf_op jit(solution)/shard_map/ppermute | solution.py:20
  42.1 1.6 %copy-start.9 = (f32[8,1024]{1,0:T(8,128)}, f32[8,1024]{1,0:T(8,128)S(1)}, u32[]{:S(2)}) copy-start(f32[8,1024]{1,0:T(8,128)S(1)} %collective-permute-done.4.refs_1_) | copy-start | bytes 98308
  43.7 0.6 copy-start.10
  43.7 0.6 copy-start.11
  45.8 3.9 %collective-permute-start.7 = (bf16[16,512]{1,0:T(8,128)(2,1)}, bf16[16,512]{1,0:T(8,128)(2,1)S(1)}, u32[]{:S(2)}, u32[]{:S(2)}) collective-permute-start(bf16[16,512]{1,0:T(8,128)(2,1)} %train.1.refs_0_), channel_id=1, source_target_pairs={{0,8},{4,12},{8,0},{12,4},{1,9},{5,13},{9,1},{13,5},{2,10},{6,14},... | collective-permute-start | bytes 49160 | tf_op jit(solution)/shard_map/ppermute | solution.py:20
  49.8 0.6 copy-start.12
  50.4 1.0 %copy-start.5 = (bf16[512,1024]{1,0:T(8,128)(2,1)}, bf16[512,1024]{1,0:T(8,128)(2,1)S(1)}, u32[]{:S(2)}) copy-start(bf16[512,1024]{1,0:T(8,128)(2,1)S(1)} %collective-permute-done.far) | copy-start | bytes 3145732
  54.2 5.7 %collective-permute-start.8 = (f32[32,128]{1,0:T(8,128)}, f32[32,128]{1,0:T(8,128)S(1)}, u32[]{:S(2)}, u32[]{:S(2)}) collective-permute-start(f32[32,128]{1,0:T(8,128)} %get-tuple-element.26), channel_id=1, source_target_pairs={{0,3},{1,2},{2,1},{3,0},{4,7},{5,6},{6,5},{7,4},{8,11},{9,10},{10,... | collective-permute-start | bytes 49160 | tf_op jit(solution)/shard_map/ppermute | solution.py:20
  55.9 4.8 %collective-permute-start.9 = (f32[32,128]{1,0:T(8,128)}, f32[32,128]{1,0:T(8,128)S(1)}, u32[]{:S(2)}, u32[]{:S(2)}) collective-permute-start(f32[32,128]{1,0:T(8,128)} %get-tuple-element.27), channel_id=1, source_target_pairs={{0,2},{1,3},{2,0},{3,1},{4,6},{5,7},{6,4},{7,5},{8,10},{9,11},{10,... | collective-permute-start | bytes 49160 | tf_op jit(solution)/shard_map/ppermute | solution.py:20
  56.6 4.2 %collective-permute-start.10 = (f32[32,128]{1,0:T(8,128)}, f32[32,128]{1,0:T(8,128)S(1)}, u32[]{:S(2)}, u32[]{:S(2)}) collective-permute-start(f32[32,128]{1,0:T(8,128)} %get-tuple-element.28), channel_id=1, source_target_pairs={{0,1},{1,0},{2,3},{3,2},{4,5},{5,4},{6,7},{7,6},{8,9},{9,8},{10,11... | collective-permute-start | bytes 49160 | tf_op jit(solution)/shard_map/ppermute | solution.py:20
  59.9 0.9 %copy-start.13 = (f32[32,128]{1,0:T(8,128)}, f32[32,128]{1,0:T(8,128)S(1)}, u32[]{:S(2)}) copy-start(f32[32,128]{1,0:T(8,128)S(1)} %collective-permute-done.8.refs_1_) | copy-start | bytes 49156
  60.8 0.6 copy-start.14
  60.8 0.6 copy-start.15
  62.8 3.9 %collective-permute-start.11 = (f32[16,128]{1,0:T(8,128)}, f32[16,128]{1,0:T(8,128)S(1)}, u32[]{:S(2)}, u32[]{:S(2)}) collective-permute-start(f32[16,128]{1,0:T(8,128)} %get-tuple-element.30), channel_id=1, source_target_pairs={{0,8},{4,12},{8,0},{12,4},{1,9},{5,13},{9,1},{13,5},{2,10},{6,14},... | collective-permute-start | bytes 24584 | tf_op jit(solution)/shard_map/ppermute | solution.py:20
  66.6 0.6 copy-start.16

commit v2 on v1

--- a/solution.py
+++ b/solution.py
@@ -12,16 +12,38 @@
 BF16 = jnp.bfloat16
 NT = (((1,), (1,)), ((), ()))
 VMEM = pl.BlockSpec(memory_space=pltpu.VMEM)
-ANY = pl.BlockSpec(memory_space=pl.ANY)
+HBM = pl.BlockSpec(memory_space=pltpu.HBM)
+SMALL = pltpu.CompilerParams(vmem_limit_bytes=8 * 2**20)
 PIECES = 2
+STEPS = 32000.0
+TAIL = 16
 
 
 def swapped(block, axis, flip):
     return lax.ppermute(block, axis, [(i, i ^ flip) for i in range(lax.axis_size(axis))])
 
 
+def encode(out, dx, dg):
+    rank, chunk = dx.shape
+    exponents = []
+    for at, v in ((0, dx), (rank, dg)):
+        top = jnp.maximum(jnp.max(jnp.abs(v), axis=0, keepdims=True), 1e-30)
+        e = jnp.floor(jnp.log2(top)) + 1.0
+        scaled = jnp.clip(jnp.round(v * (jnp.exp2(-e) * STEPS)), -32767.0, 32767.0)
+        out[at : at + rank, :] = scaled.astype(jnp.int32).astype(jnp.int16)
+        exponents.append(e.astype(jnp.int32))
+    row = lax.broadcasted_iota(jnp.int32, (TAIL, chunk), 0)
+    out[2 * rank :, :] = jnp.where(row == 0, exponents[0], jnp.where(row == 1, exponents[1], 0)).astype(jnp.int16)
+
+
+def decode(part, rank):
+    v = part[...].astype(jnp.int32).astype(F32)
+    unit = jnp.exp2(v[2 * rank : 2 * rank + 2]) * (1.0 / STEPS)
+    return v[:rank] * unit[0:1], v[rank : 2 * rank] * unit[1:2]
+
+
 def project_kernel(flips, x_hbm, g_hbm, px_hbm, pg_hbm, *rest):
-    outs, (xb, gb, px, pg, sems, wsems) = rest[: len(flips)], rest[len(flips) :]
+    outs, (xb, gb, px, pg, accx, accg, sems, wsems) = rest[: len(flips)], rest[len(flips) :]
     me = lax.axis_index("tensor")
     rank, chunk = px.shape[0], xb.shape[1]
     kx, kg = xb.shape[2], gb.shape[2]
@@ -57,14 +79,18 @@
 
         @pl.when(me >= 0)
         def _():
-            dx = lax.dot_general(xb[p], px[:, i * kx : (i + 1) * kx], NT, preferred_element_type=F32).T
-            dg = lax.dot_general(gb[p], pg[:, i * kg : (i + 1) * kg], NT, preferred_element_type=F32).T
-            if i == 0:
-                out[:rank, :] = dx
-                out[rank:, :] = dg
+            dx = lax.dot_general(xb[p], px[:, i * kx : (i + 1) * kx], NT, preferred_element_type=F32)
+            dg = lax.dot_general(gb[p], pg[:, i * kg : (i + 1) * kg], NT, preferred_element_type=F32)
+            if i > 0:
+                dx, dg = dx + accx[...], dg + accg[...]
+            if i < PIECES - 1:
+                accx[...], accg[...] = dx, dg
             else:
-                out[:rank, :] += dx
-                out[rank:, :] += dg
+                dx, dg = dx.T, dg.T
+                if flips[p // PIECES]:
+                    encode(out, dx, dg)
+                else:
+                    out[:rank, :], out[rank:, :] = dx, dg
 
 
 def project(flips, inputs, grads, proj_in_t, proj_out_t, chunk):
@@ -73,18 +99,25 @@
     kx, kg = inputs.shape[1] // PIECES, grads.shape[1] // PIECES
     return pl.pallas_call(
         functools.partial(project_kernel, flips),
-        out_shape=[jax.ShapeDtypeStruct((2 * rank, chunk), F32)] * len(flips),
-        in_specs=[ANY] * 4,
+        out_shape=[
+            jax.ShapeDtypeStruct((2 * rank + TAIL, chunk), jnp.int16)
+            if k
+            else jax.ShapeDtypeStruct((2 * rank, chunk), F32)
+            for k in flips
+        ],
+        in_specs=[HBM] * 4,
         out_specs=[VMEM] * len(flips),
         scratch_shapes=[
             pltpu.VMEM((total, chunk, kx), BF16),
             pltpu.VMEM((total, chunk, kg), BF16),
             pltpu.VMEM(proj_in_t.shape, BF16),
             pltpu.VMEM(proj_out_t.shape, BF16),
+            pltpu.VMEM((chunk, rank), F32),
+            pltpu.VMEM((chunk, rank), F32),
             pltpu.SemaphoreType.DMA((2, total)),
             pltpu.SemaphoreType.DMA((2,)),
         ],
-        compiler_params=pltpu.CompilerParams(vmem_limit_bytes=32 * 2**20),
+        compiler_params=pltpu.CompilerParams(vmem_limit_bytes=60 * 2**20),
         name="project",
     )(inputs, grads, proj_in_t, proj_out_t)
 
@@ -93,10 +126,10 @@
     parts, outs, (prod,) = refs[:shares], refs[shares : 2 * shares], refs[2 * shares :]
     me = lax.axis_index("tensor")
     rank, chunk = parts[0].shape[0] // 2, parts[0].shape[1]
-    both = parts[0][...]
+    x, g = parts[0][:rank], parts[0][rank:]
     for part in parts[1:]:
-        both = both + part[...]
-    x, g = both[:rank], both[rank:]
+        more_x, more_g = decode(part, rank)
+        x, g = x + more_x, g + more_g
     own = ids[:, pl.ds(pl.multiple_of(me * chunk, chunk), chunk)]
     mask = own == lax.broadcasted_iota(jnp.int32, (DOC_DEV, chunk), 0)
     rows = jnp.concatenate([jnp.where(mask, g[i : i + 1], 0.0) for i in range(rank)], axis=0)
@@ -122,6 +155,7 @@
         in_specs=[VMEM] * (1 + shares),
         out_specs=[VMEM] * shares,
         scratch_shapes=[pltpu.VMEM((rank, DOC_DEV, rank), F32)],
+        compiler_params=SMALL,
         name="outer",
     )(ids, *parts)
 
@@ -145,6 +179,7 @@
         out_shape=jax.ShapeDtypeStruct((2 * DOC_DEV, width // 2), BF16),
         in_specs=[VMEM] * (1 + len(parts)),
         out_specs=VMEM,
+        compiler_params=SMALL,
         name="train",
     )(ids, *parts)
 
@@ -175,6 +210,7 @@
         in_specs=[VMEM] * (2 + len(trains)),
         out_specs=[VMEM] * shares,
         scratch_shapes=[pltpu.VMEM((shares, *shape), F32)],
+        compiler_params=SMALL,
         name="score",
     )(near, far, *trains)
 
@@ -196,6 +232,7 @@
         out_shape=[jax.ShapeDtypeStruct((2 * DOC_DEV, parts[0].shape[1]), F32)] * chips,
         in_specs=[VMEM] * len(parts),
         out_specs=[VMEM] * chips,
+        compiler_params=SMALL,
         name="add",
     )(*parts)
 
@@ -215,8 +252,14 @@
         out_shape=jax.ShapeDtypeStruct((DOC_DEV, 2 * len(parts), parts[0].shape[1]), F32),
         in_specs=[VMEM] * len(parts),
         out_specs=VMEM,
+        compiler_params=SMALL,
         name="place",
     )(*parts)
+
+
+def groups_of(shares):
+    flips = list(range(shares - 1, -1, -1))
+    return [flips[:-1], flips[-1:]]
 
 
 def per_device(inputs, grads, proj_in, proj_out, queries, ids):
@@ -225,10 +268,12 @@
     chunk = inputs.shape[0] // shares
     sibling = swapped(queries, "docs", 1)
     flips = list(range(shares - 1, 0, -1))
-    parts = project(flips, inputs, grads, proj_in.T, proj_out.T, chunk)
-    arrived = [swapped(p, "tensor", k) for k, p in zip(flips, parts)]
-    (own,) = project([0], inputs, grads, proj_in.T, proj_out.T, chunk)
-    sums = outer([own] + arrived, ids)
+    parts = {}
+    for group in groups_of(shares):
+        made = project(group, inputs, grads, proj_in.T, proj_out.T, chunk)
+        for k, part in zip(group, made):
+            parts[k] = swapped(part, "tensor", k) if k else part
+    sums = outer([parts[k] for k in range(shares)], ids)
     arrived = [swapped(sums[k], "tensor", k) for k in flips]
     train = mean_gradients([sums[0]] + arrived, ids)
     trains = [train] + [swapped(train, "docs", 2 * m) for m in range(1, chips)]

time: 69 us -> 45.3 us (0.66)
  local copies, waits for them, and re-layouts: 14.8 us -> 0.92 us
  waiting for transfers between devices: 18.3 us -> 12 us
  Pallas kernels: 17.8 us -> 14.4 us
    unnamed x34 -> x6, local copies, waits for them, and re-layouts: 14.8 us -> 0.92 us
    ppermute x12, waiting for transfers between devices: 18.3 us -> 12 us  [swapped(): lax.ppermute(block, axis, [(i, i ^ flip) for i in range(lax.axis_size(axi...]
    pallas_call x2, Pallas kernels: 8.5 us -> 12.6 us  [project(): pl.pallas_call(functools.partial(project_kernel, flips), out_shape=[jax.S...]
    pallas_call x1, Pallas kernels: 2.83 us -> 0.65 us  [score(): pl.pallas_call(functools.partial(score_kernel, shares), out_shape=[jax.Sh...]
    pallas_call x1, Pallas kernels: 2.22 us -> 0.49 us  [outer(): pl.pallas_call(functools.partial(outer_kernel, shares), out_shape=[jax.Sh...]
    pallas_call x1, Pallas kernels: 1.52 us -> 0.09 us  [mean_gradients(): pl.pallas_call(train_kernel, out_shape=jax.ShapeDtypeStruct((2 * DOC_DEV,...]
    pallas_call x1, Pallas kernels: 1.37 us -> 0.01 us  [add(): pl.pallas_call(functools.partial(add_kernel, len(parts)), out_shape=[jax....]
    pallas_call x1, Pallas kernels: 1.34 us -> 0.62 us  [place(): pl.pallas_call(place_kernel, out_shape=jax.ShapeDtypeStruct((DOC_DEV, 2 *...]
  transfers between devices with their start and end apart: 12 -> 12, of which waited for: 8 -> 7; matrix products, arithmetic and copies ran while one was open for 0% -> 0% of each run, Pallas kernels for 18% -> 29%
where the time goes in v2:
time: 45.3 us; the launch traced here: 45.1 us
  starting transfers between devices  17.6 us (39%)
  Pallas kernels  14.4 us (32%)
  waiting for transfers between devices  12 us (26%)
  local copies, waits for them, and re-layouts  0.92 us (2%)
    ppermute x12, starting transfers between devices, swapped(): lax.ppermute(block, axis, [(i, i ^ flip) for i in range(lax.axis_size(axi...  17.6 us
    pallas_call x2, Pallas kernels, project(): pl.pallas_call(functools.partial(project_kernel, flips), out_shape=[jax.S...  12.6 us
    ppermute x12, waiting for transfers between devices, swapped(): lax.ppermute(block, axis, [(i, i ^ flip) for i in range(lax.axis_size(axi...  12 us
    unnamed x6, local copies, waits for them, and re-layouts  0.92 us
  transfers between devices with their start and end apart: 12, of which 7 were waited for; matrix products, arithmetic and copies ran while one was open for 0% of the time, Pallas kernels for 29%

profile of v2, /device:TPU:0, one launch (start us, length us, event | category | flops | bytes accessed | tf_op | source)
XLA Modules:
  0.0 45.1 jit_solution(7356430266872471316)
XLA Ops:
  0.0 0.5 %collective-permute-start = (bf16[512,1024]{1,0:T(8,128)(2,1)}, bf16[512,1024]{1,0:T(8,128)(2,1)S(1)}, u32[]{:S(2)}, u32[]{:S(2)}) collective-permute-start(bf16[512,1024]{1,0:T(8,128)(2,1)} %near.1), channel_id=1, source_target_pairs={{0,4},{4,0},{8,12},{12,8},{1,5},{5,1},{9,13},{13,9},{2,6},{6,2},{1... | collective-permute-start | bytes 3145736 | tf_op jit(solution)/shard_map/ppermute | solution.py:23
  0.5 8.2 %project.3 = (s16[144,256]{1,0:T(8,128)(2,1)}, s16[144,256]{1,0:T(8,128)(2,1)}, s16[144,256]{1,0:T(8,128)(2,1)}) custom-call(bf16[1024,2048]{1,0:T(8,128)(2,1)} %x_hbm.3, bf16[1024,7168]{1,0:T(8,128)(2,1)} %g_hbm.3, bf16[64,2048]{1,0:T(8,128)(2,1)} %bitcast.4, bf16[64,7168]{1,0:T(8,128)(2,1)} %bitcast.2), custom_call_target="tpu_custom_call" | custom-call | tf_op jit(solution)/shard_map/project/pallas_call | solution.py:100
  8.6 0.0 copy-start.2
  8.6 0.0 copy-start
  8.6 2.6 %collective-permute-start.1 = (s16[144,256]{1,0:T(8,128)(2,1)}, s16[144,256]{1,0:T(8,128)(2,1)S(1)}, u32[]{:S(2)}, u32[]{:S(2)}) collective-permute-start(s16[144,256]{1,0:T(8,128)(2,1)} %get-tuple-element.18), channel_id=1, source_target_pairs={{0,1},{1,0},{2,3},{3,2},{4,5},{5,4},{6,7},{7,6},{8,9},{9,8},{10,11... | collective-permute-start | bytes 221192 | tf_op jit(solution)/shard_map/ppermute | solution.py:23
  11.3 2.6 %collective-permute-start.2 = (s16[144,256]{1,0:T(8,128)(2,1)}, s16[144,256]{1,0:T(8,128)(2,1)S(1)}, u32[]{:S(2)}, u32[]{:S(2)}) collective-permute-start(s16[144,256]{1,0:T(8,128)(2,1)} %get-tuple-element.19), channel_id=1, source_target_pairs={{0,2},{1,3},{2,0},{3,1},{4,6},{5,7},{6,4},{7,5},{8,10},{9,11},{10,... | collective-permute-start | bytes 221192 | tf_op jit(solution)/shard_map/ppermute | solution.py:23
  13.9 0.0 collective-permute-start.3
  13.9 4.4 %project.2.refs_0_ = f32[128,256]{1,0:T(8,128)} custom-call(bf16[1024,2048]{1,0:T(8,128)(2,1)} %x_hbm.3, bf16[1024,7168]{1,0:T(8,128)(2,1)} %g_hbm.3, bf16[64,2048]{1,0:T(8,128)(2,1)} %bitcast.5, bf16[64,7168]{1,0:T(8,128)(2,1)} %bitcast.3), custom_call_target="tpu_custom_call" | custom-call | tf_op jit(solution)/shard_map/project/pallas_call | solution.py:100
  18.3 0.0 collective-permute-done.1.refs_1_
  18.3 2.1 %collective-permute-done.2.refs_2_ = s16[144,256]{1,0:T(8,128)(2,1)S(1)} collective-permute-done((s16[144,256]{1,0:T(8,128)(2,1)}, s16[144,256]{1,0:T(8,128)(2,1)S(1)}, u32[]{:S(2)}, u32[]{:S(2)}) %collective-permute-start.2) | collective-permute-done | bytes 73760 | tf_op jit(solution)/shard_map/ppermute | solution.py:23
  20.4 0.0 collective-permute-done.3.refs_3_
  20.5 0.9 %copy-done.1 = f32[128,256]{1,0:T(8,128)S(1)} copy-done((f32[128,256]{1,0:T(8,128)S(1)}, f32[128,256]{1,0:T(8,128)}, u32[]{:S(2)}) %copy-start.1) | copy-done | bytes 131096
  21.4 0.5 %outer.1 = (f32[8,1024]{1,0:T(8,128)S(1)}, f32[8,1024]{1,0:T(8,128)S(1)}, f32[8,1024]{1,0:T(8,128)S(1)}, f32[8,1024]{1,0:T(8,128)S(1)}) custom-call(s32[1,1024]{1,0:T(1,128)S(1)} %copy-done.2, f32[128,256]{1,0:T(8,128)S(1)} %copy-done.1, s16[144,256]{1,0:T(8,128)(2,1)S(1)} %collective-permute-done.1.refs_1_, ...), custom_call_target="tpu_custom_call" | custom-call | tf_op jit(solution)/shard_map/outer/pallas_call | solution.py:152
  21.9 2.8 %collective-permute-start.4 = (f32[8,1024]{1,0:T(8,128)S(1)}, f32[8,1024]{1,0:T(8,128)S(1)}, u32[]{:S(2)}, u32[]{:S(2)}) collective-permute-start(f32[8,1024]{1,0:T(8,128)S(1)} %get-tuple-element.22), channel_id=1, source_target_pairs={{0,3},{1,2},{2,1},{3,0},{4,7},{5,6},{6,5},{7,4},{8,11},{9,10},{10,... | collective-permute-start | bytes 98312 | tf_op jit(solution)/shard_map/ppermute | solution.py:23
  24.6 0.4 collective-permute-start.5
  25.0 1.3 %collective-permute-start.6 = (f32[8,1024]{1,0:T(8,128)S(1)}, f32[8,1024]{1,0:T(8,128)S(1)}, u32[]{:S(2)}, u32[]{:S(2)}) collective-permute-start(f32[8,1024]{1,0:T(8,128)S(1)} %get-tuple-element.24), channel_id=1, source_target_pairs={{0,1},{1,0},{2,3},{3,2},{4,5},{5,4},{6,7},{7,6},{8,9},{9,8},{10,11... | collective-permute-start | bytes 98312 | tf_op jit(solution)/shard_map/ppermute | solution.py:23
  26.3 1.7 %collective-permute-done.4.refs_1_ = f32[8,1024]{1,0:T(8,128)S(1)} collective-permute-done((f32[8,1024]{1,0:T(8,128)S(1)}, f32[8,1024]{1,0:T(8,128)S(1)}, u32[]{:S(2)}, u32[]{:S(2)}) %collective-permute-start.4) | collective-permute-done | bytes 32800 | tf_op jit(solution)/shard_map/ppermute | solution.py:23
  28.0 1.8 %collective-permute-done.5.refs_2_ = f32[8,1024]{1,0:T(8,128)S(1)} collective-permute-done((f32[8,1024]{1,0:T(8,128)S(1)}, f32[8,1024]{1,0:T(8,128)S(1)}, u32[]{:S(2)}, u32[]{:S(2)}) %collective-permute-start.5) | collective-permute-done | bytes 32800 | tf_op jit(solution)/shard_map/ppermute | solution.py:23
  29.8 0.0 collective-permute-done.6.refs_3_
  29.8 0.1 train.1.refs_0_
  29.8 1.5 %collective-permute-start.7 = (bf16[16,512]{1,0:T(8,128)(2,1)S(1)}, bf16[16,512]{1,0:T(8,128)(2,1)S(1)}, u32[]{:S(2)}, u32[]{:S(2)}) collective-permute-start(bf16[16,512]{1,0:T(8,128)(2,1)S(1)} %train.1.refs_0_), channel_id=1, source_target_pairs={{0,8},{4,12},{8,0},{12,4},{1,9},{5,13},{9,1},{13,5},{2,10},{6,14},... | collective-permute-start | bytes 49160 | tf_op jit(solution)/shard_map/ppermute | solution.py:23
  31.4 2.2 %collective-permute-done.7.refs_1_ = bf16[16,512]{1,0:T(8,128)(2,1)S(1)} collective-permute-done((bf16[16,512]{1,0:T(8,128)(2,1)S(1)}, bf16[16,512]{1,0:T(8,128)(2,1)S(1)}, u32[]{:S(2)}, u32[]{:S(2)}) %collective-permute-start.7) | collective-permute-done | bytes 16416 | tf_op jit(solution)/shard_map/ppermute | solution.py:23
  33.6 0.0 collective-permute-done.far
  33.6 0.7 %score.1 = (f32[32,128]{1,0:T(8,128)S(1)}, f32[32,128]{1,0:T(8,128)S(1)}, f32[32,128]{1,0:T(8,128)S(1)}, f32[32,128]{1,0:T(8,128)S(1)}) custom-call(bf16[512,1024]{1,0:T(8,128)(2,1)S(1)} %copy-done, bf16[512,1024]{1,0:T(8,128)(2,1)S(1)} %collective-permute-done.far, bf16[16,512]{1,0:T(8,128)(2,1)S(1)} %train.1.refs_0_, ...), custom_call_target="tpu_custom_call" | custom-call | tf_op jit(solution)/shard_map/score/pallas_call | solution.py:207
  34.2 1.7 %collective-permute-start.8 = (f32[32,128]{1,0:T(8,128)S(1)}, f32[32,128]{1,0:T(8,128)S(1)}, u32[]{:S(2)}, u32[]{:S(2)}) collective-permute-start(f32[32,128]{1,0:T(8,128)S(1)} %get-tuple-element.26), channel_id=1, source_target_pairs={{0,3},{1,2},{2,1},{3,0},{4,7},{5,6},{6,5},{7,4},{8,11},{9,10},{10,... | collective-permute-start | bytes 49160 | tf_op jit(solution)/shard_map/ppermute | solution.py:23
  35.9 0.3 collective-permute-start.9
  36.2 2.5 %collective-permute-start.10 = (f32[32,128]{1,0:T(8,128)S(1)}, f32[32,128]{1,0:T(8,128)S(1)}, u32[]{:S(2)}, u32[]{:S(2)}) collective-permute-start(f32[32,128]{1,0:T(8,128)S(1)} %get-tuple-element.28), channel_id=1, source_target_pairs={{0,1},{1,0},{2,3},{3,2},{4,5},{5,4},{6,7},{7,6},{8,9},{9,8},{10,11... | collective-permute-start | bytes 49160 | tf_op jit(solution)/shard_map/ppermute | solution.py:23
  38.7 1.1 %collective-permute-done.8.refs_1_ = f32[32,128]{1,0:T(8,128)S(1)} collective-permute-done((f32[32,128]{1,0:T(8,128)S(1)}, f32[32,128]{1,0:T(8,128)S(1)}, u32[]{:S(2)}, u32[]{:S(2)}) %collective-permute-start.8) | collective-permute-done | bytes 16416 | tf_op jit(solution)/shard_map/ppermute | solution.py:23
  39.8 1.0 %collective-permute-done.9.refs_2_ = f32[32,128]{1,0:T(8,128)S(1)} collective-permute-done((f32[32,128]{1,0:T(8,128)S(1)}, f32[32,128]{1,0:T(8,128)S(1)}, u32[]{:S(2)}, u32[]{:S(2)}) %collective-permute-start.9) | collective-permute-done | bytes 16416 | tf_op jit(solution)/shard_map/ppermute | solution.py:23
  40.8 1.6 %collective-permute-start.11 = (f32[16,128]{1,0:T(8,128)S(1)}, f32[16,128]{1,0:T(8,128)S(1)}, u32[]{:S(2)}, u32[]{:S(2)}) collective-permute-start(f32[16,128]{1,0:T(8,128)S(1)} %get-tuple-element.30), channel_id=1, source_target_pairs={{0,8},{4,12},{8,0},{12,4},{1,9},{5,13},{9,1},{13,5},{2,10},{6,14},... | collective-permute-start | bytes 24584 | tf_op jit(solution)/shard_map/ppermute | solution.py:23
  42.4 2.1 %collective-permute-done.11.refs_1_ = f32[16,128]{1,0:T(8,128)S(1)} collective-permute-done((f32[16,128]{1,0:T(8,128)S(1)}, f32[16,128]{1,0:T(8,128)S(1)}, u32[]{:S(2)}, u32[]{:S(2)}) %collective-permute-start.11) | collective-permute-done | bytes 8224 | tf_op jit(solution)/shard_map/ppermute | solution.py:23
  44.5 0.6 %place.1 = f32[8,4,128]{2,1,0:T(4,128)} custom-call(f32[16,128]{1,0:T(8,128)S(1)} %get-tuple-element.29.refs_0_, f32[16,128]{1,0:T(8,128)S(1)} %collective-permute-done.11.refs_1_), custom_call_target="tpu_custom_call" | custom-call | tf_op jit(solution)/shard_map/place/pallas_call | solution.py:250
  (5 shorter events, 0.0 us)
Async XLA Ops:
  0.0 33.6 %collective-permute-start = (bf16[512,1024]{1,0:T(8,128)(2,1)}, bf16[512,1024]{1,0:T(8,128)(2,1)S(1)}, u32[]{:S(2)}, u32[]{:S(2)}) collective-permute-start(bf16[512,1024]{1,0:T(8,128)(2,1)} %near.1), channel_id=1, source_target_pairs={{0,4},{4,0},{8,12},{12,8},{1,5},{5,1},{9,13},{13,9},{2,6},{6,2},{1... | collective-permute-start | bytes 3145736 | tf_op jit(solution)/shard_map/ppermute | solution.py:23
  8.6 11.8 %copy-start.2 = (s32[1,1024]{1,0:T(1,128)S(1)}, s32[1,1024]{1,0:T(1,128)}, u32[]{:S(2)}) copy-start(s32[1,1024]{1,0:T(1,128)} %ids.3) | copy-start | bytes 12292
  8.6 25.0 %copy-start = (bf16[512,1024]{1,0:T(8,128)(2,1)S(1)}, bf16[512,1024]{1,0:T(8,128)(2,1)}, u32[]{:S(2)}) copy-start(bf16[512,1024]{1,0:T(8,128)(2,1)} %near.1) | copy-start | bytes 3145732
  8.6 9.7 %collective-permute-start.1 = (s16[144,256]{1,0:T(8,128)(2,1)}, s16[144,256]{1,0:T(8,128)(2,1)S(1)}, u32[]{:S(2)}, u32[]{:S(2)}) collective-permute-start(s16[144,256]{1,0:T(8,128)(2,1)} %get-tuple-element.18), channel_id=1, source_target_pairs={{0,1},{1,0},{2,3},{3,2},{4,5},{5,4},{6,7},{7,6},{8,9},{9,8},{10,11... | collective-permute-start | bytes 221192 | tf_op jit(solution)/shard_map/ppermute | solution.py:23
  11.3 9.2 %collective-permute-start.2 = (s16[144,256]{1,0:T(8,128)(2,1)}, s16[144,256]{1,0:T(8,128)(2,1)S(1)}, u32[]{:S(2)}, u32[]{:S(2)}) collective-permute-start(s16[144,256]{1,0:T(8,128)(2,1)} %get-tuple-element.19), channel_id=1, source_target_pairs={{0,2},{1,3},{2,0},{3,1},{4,6},{5,7},{6,4},{7,5},{8,10},{9,11},{10,... | collective-permute-start | bytes 221192 | tf_op jit(solution)/shard_map/ppermute | solution.py:23
  13.9 6.6 %collective-permute-start.3 = (s16[144,256]{1,0:T(8,128)(2,1)}, s16[144,256]{1,0:T(8,128)(2,1)S(1)}, u32[]{:S(2)}, u32[]{:S(2)}) collective-permute-start(s16[144,256]{1,0:T(8,128)(2,1)} %get-tuple-element.20), channel_id=1, source_target_pairs={{0,3},{1,2},{2,1},{3,0},{4,7},{5,6},{6,5},{7,4},{8,11},{9,10},{10,... | collective-permute-start | bytes 221192 | tf_op jit(solution)/shard_map/ppermute | solution.py:23
  20.4 0.9 %copy-start.1 = (f32[128,256]{1,0:T(8,128)S(1)}, f32[128,256]{1,0:T(8,128)}, u32[]{:S(2)}) copy-start(f32[128,256]{1,0:T(8,128)} %project.2.refs_0_) | copy-start | bytes 393220
  21.9 6.1 %collective-permute-start.4 = (f32[8,1024]{1,0:T(8,128)S(1)}, f32[8,1024]{1,0:T(8,128)S(1)}, u32[]{:S(2)}, u32[]{:S(2)}) collective-permute-start(f32[8,1024]{1,0:T(8,128)S(1)} %get-tuple-element.22), channel_id=1, source_target_pairs={{0,3},{1,2},{2,1},{3,0},{4,7},{5,6},{6,5},{7,4},{8,11},{9,10},{10,... | collective-permute-start | bytes 98312 | tf_op jit(solution)/shard_map/ppermute | solution.py:23
  24.6 5.1 %collective-permute-start.5 = (f32[8,1024]{1,0:T(8,128)S(1)}, f32[8,1024]{1,0:T(8,128)S(1)}, u32[]{:S(2)}, u32[]{:S(2)}) collective-permute-start(f32[8,1024]{1,0:T(8,128)S(1)} %get-tuple-element.23), channel_id=1, source_target_pairs={{0,2},{1,3},{2,0},{3,1},{4,6},{5,7},{6,4},{7,5},{8,10},{9,11},{10,... | collective-permute-start | bytes 98312 | tf_op jit(solution)/shard_map/ppermute | solution.py:23
  25.0 4.7 %collective-permute-start.6 = (f32[8,1024]{1,0:T(8,128)S(1)}, f32[8,1024]{1,0:T(8,128)S(1)}, u32[]{:S(2)}, u32[]{:S(2)}) collective-permute-start(f32[8,1024]{1,0:T(8,128)S(1)} %get-tuple-element.24), channel_id=1, source_target_pairs={{0,1},{1,0},{2,3},{3,2},{4,5},{5,4},{6,7},{7,6},{8,9},{9,8},{10,11... | collective-permute-start | bytes 98312 | tf_op jit(solution)/shard_map/ppermute | solution.py:23
  29.8 3.7 %collective-permute-start.7 = (bf16[16,512]{1,0:T(8,128)(2,1)S(1)}, bf16[16,512]{1,0:T(8,128)(2,1)S(1)}, u32[]{:S(2)}, u32[]{:S(2)}) collective-permute-start(bf16[16,512]{1,0:T(8,128)(2,1)S(1)} %train.1.refs_0_), channel_id=1, source_target_pairs={{0,8},{4,12},{8,0},{12,4},{1,9},{5,13},{9,1},{13,5},{2,10},{6,14},... | collective-permute-start | bytes 49160 | tf_op jit(solution)/shard_map/ppermute | solution.py:23
  34.2 5.6 %collective-permute-start.8 = (f32[32,128]{1,0:T(8,128)S(1)}, f32[32,128]{1,0:T(8,128)S(1)}, u32[]{:S(2)}, u32[]{:S(2)}) collective-permute-start(f32[32,128]{1,0:T(8,128)S(1)} %get-tuple-element.26), channel_id=1, source_target_pairs={{0,3},{1,2},{2,1},{3,0},{4,7},{5,6},{6,5},{7,4},{8,11},{9,10},{10,... | collective-permute-start | bytes 49160 | tf_op jit(solution)/shard_map/ppermute | solution.py:23
  35.9 4.8 %collective-permute-start.9 = (f32[32,128]{1,0:T(8,128)S(1)}, f32[32,128]{1,0:T(8,128)S(1)}, u32[]{:S(2)}, u32[]{:S(2)}) collective-permute-start(f32[32,128]{1,0:T(8,128)S(1)} %get-tuple-element.27), channel_id=1, source_target_pairs={{0,2},{1,3},{2,0},{3,1},{4,6},{5,7},{6,4},{7,5},{8,10},{9,11},{10,... | collective-permute-start | bytes 49160 | tf_op jit(solution)/shard_map/ppermute | solution.py:23
  36.2 4.6 %collective-permute-start.10 = (f32[32,128]{1,0:T(8,128)S(1)}, f32[32,128]{1,0:T(8,128)S(1)}, u32[]{:S(2)}, u32[]{:S(2)}) collective-permute-start(f32[32,128]{1,0:T(8,128)S(1)} %get-tuple-element.28), channel_id=1, source_target_pairs={{0,1},{1,0},{2,3},{3,2},{4,5},{5,4},{6,7},{7,6},{8,9},{9,8},{10,11... | collective-permute-start | bytes 49160 | tf_op jit(solution)/shard_map/ppermute | solution.py:23
  40.8 3.7 %collective-permute-start.11 = (f32[16,128]{1,0:T(8,128)S(1)}, f32[16,128]{1,0:T(8,128)S(1)}, u32[]{:S(2)}, u32[]{:S(2)}) collective-permute-start(f32[16,128]{1,0:T(8,128)S(1)} %get-tuple-element.30), channel_id=1, source_target_pairs={{0,8},{4,12},{8,0},{12,4},{1,9},{5,13},{9,1},{13,5},{2,10},{6,14},... | collective-permute-start | bytes 24584 | tf_op jit(solution)/shard_map/ppermute | solution.py:23

commit v3 on v2

--- a/solution.py
+++ b/solution.py
@@ -117,7 +117,7 @@
             pltpu.SemaphoreType.DMA((2, total)),
             pltpu.SemaphoreType.DMA((2,)),
         ],
-        compiler_params=pltpu.CompilerParams(vmem_limit_bytes=60 * 2**20),
+        compiler_params=pltpu.CompilerParams(vmem_limit_bytes=int(53.5 * 2**20)),
         name="project",
     )(inputs, grads, proj_in_t, proj_out_t)
 
@@ -184,8 +184,8 @@
     )(ids, *parts)
 
 
-def score_kernel(shares, near, far, *refs):
-    trains, outs, (held,) = refs[: -shares - 1], refs[-shares - 1 : -1], refs[-1:]
+def score_kernel(shares, chips, *refs):
+    blocks, trains, outs, (held,) = refs[:chips], refs[chips : chips + 2], refs[chips + 2 : -1], refs[-1:]
     me = lax.axis_index("tensor")
     rows = []
     for train in trains:
@@ -193,26 +193,26 @@
         rows.append(jnp.concatenate([t[:DOC_DEV], t[DOC_DEV:]], axis=1))
     docs = jnp.concatenate(rows, axis=0).astype(BF16)
     count = docs.shape[0]
-    width = near.shape[0] // shares
-    for at, queries in enumerate((near, far)):
+    width = blocks[0].shape[0] // shares
+    for m, queries in enumerate(blocks):
         scores = lax.dot_general(docs, queries[...], NT, preferred_element_type=F32)
         for j in range(shares):
-            held[j, at * count : (at + 1) * count, :] = scores[:, j * width : (j + 1) * width]
+            held[j, m * count : (m + 1) * count, :] = scores[:, j * width : (j + 1) * width]
     for k in range(shares):
         outs[k][...] = held[me ^ k]
 
 
-def score(trains, near, far, shares):
-    shape = (2 * DOC_DEV * len(trains), near.shape[0] // shares)
-    return pl.pallas_call(
-        functools.partial(score_kernel, shares),
+def score(trains, blocks, shares):
+    shape = (2 * DOC_DEV * len(blocks), blocks[0].shape[0] // shares)
+    return pl.pallas_call(
+        functools.partial(score_kernel, shares, len(blocks)),
         out_shape=[jax.ShapeDtypeStruct(shape, F32)] * shares,
-        in_specs=[VMEM] * (2 + len(trains)),
+        in_specs=[VMEM] * (len(blocks) + len(trains)),
         out_specs=[VMEM] * shares,
         scratch_shapes=[pltpu.VMEM((shares, *shape), F32)],
         compiler_params=SMALL,
         name="score",
-    )(near, far, *trains)
+    )(*blocks, *trains)
 
 
 def add_kernel(shares, *refs):
@@ -220,41 +220,40 @@
     total = parts[0][...]
     for part in parts[1:]:
         total = total + part[...]
-    count = total.shape[0] // 2
-    for m, out in enumerate(outs):
-        a = m * DOC_DEV
-        out[...] = jnp.concatenate([total[a : a + DOC_DEV], total[count + a : count + a + DOC_DEV]], axis=0)
-
-
-def add(parts, chips):
+    both = total.reshape(-1, 2, DOC_DEV, total.shape[1])
+    for core, out in enumerate(outs):
+        out[...] = both[:, core]
+
+
+def add(parts):
+    rows, width = parts[0].shape
     return pl.pallas_call(
         functools.partial(add_kernel, len(parts)),
-        out_shape=[jax.ShapeDtypeStruct((2 * DOC_DEV, parts[0].shape[1]), F32)] * chips,
+        out_shape=[jax.ShapeDtypeStruct((rows // (2 * DOC_DEV), DOC_DEV, width), F32)] * 2,
         in_specs=[VMEM] * len(parts),
-        out_specs=[VMEM] * chips,
+        out_specs=[VMEM] * 2,
         compiler_params=SMALL,
         name="add",
     )(*parts)
 
 
-def place_kernel(*refs):
-    parts, out = refs[:-1], refs[-1]
+def place_kernel(near, far, out):
     me = lax.axis_index("docs")
-    for m, part in enumerate(parts):
-        block = me ^ (2 * m)
-        out[:, pl.ds(block, 1), :] = part[:DOC_DEV, :][:, None, :]
-        out[:, pl.ds(block ^ 1, 1), :] = part[DOC_DEV:, :][:, None, :]
-
-
-def place(parts):
+    for m in range(near.shape[0]):
+        out[:, pl.ds(me ^ (2 * m), 1), :] = near[m][:, None, :]
+        out[:, pl.ds(me ^ (2 * m + 1), 1), :] = far[m][:, None, :]
+
+
+def place(near, far):
+    chips, docs, width = near.shape
     return pl.pallas_call(
         place_kernel,
-        out_shape=jax.ShapeDtypeStruct((DOC_DEV, 2 * len(parts), parts[0].shape[1]), F32),
-        in_specs=[VMEM] * len(parts),
+        out_shape=jax.ShapeDtypeStruct((docs, 2 * chips, width), F32),
+        in_specs=[VMEM] * 2,
         out_specs=VMEM,
         compiler_params=SMALL,
         name="place",
-    )(*parts)
+    )(near, far)
 
 
 def groups_of(shares):
@@ -266,7 +265,7 @@
     shares, ndev = lax.axis_size("tensor"), lax.axis_size("docs")
     chips = ndev // 2
     chunk = inputs.shape[0] // shares
-    sibling = swapped(queries, "docs", 1)
+    blocks = [queries] + [swapped(queries, "docs", 2 * m) for m in range(1, chips)]
     flips = list(range(shares - 1, 0, -1))
     parts = {}
     for group in groups_of(shares):
@@ -276,11 +275,10 @@
     sums = outer([parts[k] for k in range(shares)], ids)
     arrived = [swapped(sums[k], "tensor", k) for k in flips]
     train = mean_gradients([sums[0]] + arrived, ids)
-    trains = [train] + [swapped(train, "docs", 2 * m) for m in range(1, chips)]
-    scores = score(trains, queries, sibling, shares)
+    scores = score([train, swapped(train, "docs", 1)], blocks, shares)
     arrived = [swapped(scores[k], "tensor", k) for k in flips]
-    mine = add([scores[0]] + arrived, chips)
-    return place([mine[0]] + [swapped(mine[m], "docs", 2 * m) for m in range(1, chips)])
+    mine, sibling = add([scores[0]] + arrived)
+    return place(mine, swapped(sibling, "docs", 1))
 
 
 def solution(mesh):

time: 45.3 us -> 39.2 us (0.87)
  waiting for transfers between devices: 12 us -> 9.56 us
  Pallas kernels: 14.4 us -> 13 us
  starting transfers between devices: 17.6 us -> 16.3 us
  local copies, waits for them, and re-layouts: 0.92 us -> 0.02 us
    ppermute x12, waiting for transfers between devices: 12 us -> 9.56 us  [swapped(): lax.ppermute(block, axis, [(i, i ^ flip) for i in range(lax.axis_size(axi...]
    pallas_call x2, Pallas kernels: 12.6 us -> 11.2 us  [project(): pl.pallas_call(functools.partial(project_kernel, flips), out_shape=[jax.S...]
    ppermute x12, starting transfers between devices: 17.6 us -> 16.3 us  [swapped(): lax.ppermute(block, axis, [(i, i ^ flip) for i in range(lax.axis_size(axi...]
    unnamed x6, local copies, waits for them, and re-layouts: 0.92 us -> 0.02 us
  transfers between devices with their start and end apart: 12 -> 12, of which waited for: 7 -> 8; matrix products, arithmetic and copies ran while one was open for 0% -> 0% of each run, Pallas kernels for 29% -> 30%
where the time goes in v3:
time: 39.2 us; the launch traced here: 39 us
  starting transfers between devices  16.3 us (42%)
  Pallas kernels  13 us (33%)
  waiting for transfers between devices  9.56 us (24%)
    ppermute x12, starting transfers between devices, swapped(): lax.ppermute(block, axis, [(i, i ^ flip) for i in range(lax.axis_size(axi...  16.3 us
    pallas_call x2, Pallas kernels, project(): pl.pallas_call(functools.partial(project_kernel, flips), out_shape=[jax.S...  11.2 us
    ppermute x12, waiting for transfers between devices, swapped(): lax.ppermute(block, axis, [(i, i ^ flip) for i in range(lax.axis_size(axi...  9.56 us
  transfers between devices with their start and end apart: 12, of which 8 were waited for; matrix products, arithmetic and copies ran while one was open for 0% of the time, Pallas kernels for 30%

profile of v3, /device:TPU:0, one launch (start us, length us, event | category | flops | bytes accessed | tf_op | source)
XLA Modules:
  0.0 39.0 jit_solution(5709871134406215047)
XLA Ops:
  0.0 3.0 %collective-permute-start = (bf16[512,1024]{1,0:T(8,128)(2,1)}, bf16[512,1024]{1,0:T(8,128)(2,1)S(1)}, u32[]{:S(2)}, u32[]{:S(2)}) collective-permute-start(bf16[512,1024]{1,0:T(8,128)(2,1)} %refs_0_.1), channel_id=1, source_target_pairs={{0,8},{4,12},{8,0},{12,4},{1,9},{5,13},{9,1},{13,5},{2,10},{6,14},... | collective-permute-start | bytes 3145736 | tf_op jit(solution)/shard_map/ppermute | solution.py:23
  3.0 7.5 %project.3 = (s16[144,256]{1,0:T(8,128)(2,1)S(1)}, s16[144,256]{1,0:T(8,128)(2,1)S(1)}, s16[144,256]{1,0:T(8,128)(2,1)S(1)}) custom-call(bf16[1024,2048]{1,0:T(8,128)(2,1)} %x_hbm.3, bf16[1024,7168]{1,0:T(8,128)(2,1)} %g_hbm.3, bf16[64,2048]{1,0:T(8,128)(2,1)} %bitcast.2, bf16[64,7168]{1,0:T(8,128)(2,1)} %bitcast.4), custom_call_target="tpu_custom_call" | custom-call | tf_op jit(solution)/shard_map/project/pallas_call | solution.py:100
  10.5 0.0 copy-start.2
  10.5 0.0 copy-start.1
  10.5 1.6 %collective-permute-start.1 = (s16[144,256]{1,0:T(8,128)(2,1)S(1)}, s16[144,256]{1,0:T(8,128)(2,1)S(1)}, u32[]{:S(2)}, u32[]{:S(2)}) collective-permute-start(s16[144,256]{1,0:T(8,128)(2,1)S(1)} %get-tuple-element.18), channel_id=1, source_target_pairs={{0,1},{1,0},{2,3},{3,2},{4,5},{5,4},{6,7},{7,6},{8,9},{9,8},{10,11... | collective-permute-start | bytes 221192 | tf_op jit(solution)/shard_map/ppermute | solution.py:23
  12.1 2.6 %collective-permute-start.2 = (s16[144,256]{1,0:T(8,128)(2,1)S(1)}, s16[144,256]{1,0:T(8,128)(2,1)S(1)}, u32[]{:S(2)}, u32[]{:S(2)}) collective-permute-start(s16[144,256]{1,0:T(8,128)(2,1)S(1)} %get-tuple-element.19), channel_id=1, source_target_pairs={{0,2},{1,3},{2,0},{3,1},{4,6},{5,7},{6,4},{7,5},{8,10},{9,11},{10,... | collective-permute-start | bytes 221192 | tf_op jit(solution)/shard_map/ppermute | solution.py:23
  14.7 0.2 collective-permute-start.3
  14.9 3.7 %project.2.refs_0_ = f32[128,256]{1,0:T(8,128)S(1)} custom-call(bf16[1024,2048]{1,0:T(8,128)(2,1)} %x_hbm.3, bf16[1024,7168]{1,0:T(8,128)(2,1)} %g_hbm.3, bf16[64,2048]{1,0:T(8,128)(2,1)S(1)} %bitcast.3, bf16[64,7168]{1,0:T(8,128)(2,1)} %bitcast.5), custom_call_target="tpu_custom_call" | custom-call | tf_op jit(solution)/shard_map/project/pallas_call | solution.py:100
  18.7 0.0 collective-permute-done.1.refs_1_
  18.7 1.0 %collective-permute-done.2.refs_2_ = s16[144,256]{1,0:T(8,128)(2,1)S(1)} collective-permute-done((s16[144,256]{1,0:T(8,128)(2,1)S(1)}, s16[144,256]{1,0:T(8,128)(2,1)S(1)}, u32[]{:S(2)}, u32[]{:S(2)}) %collective-permute-start.2) | collective-permute-done | bytes 73760 | tf_op jit(solution)/shard_map/ppermute | solution.py:23
  19.6 1.3 %collective-permute-done.3.refs_3_ = s16[144,256]{1,0:T(8,128)(2,1)S(1)} collective-permute-done((s16[144,256]{1,0:T(8,128)(2,1)S(1)}, s16[144,256]{1,0:T(8,128)(2,1)S(1)}, u32[]{:S(2)}, u32[]{:S(2)}) %collective-permute-start.3) | collective-permute-done | bytes 73760 | tf_op jit(solution)/shard_map/ppermute | solution.py:23
  21.0 0.5 %outer.1 = (f32[8,1024]{1,0:T(8,128)S(1)}, f32[8,1024]{1,0:T(8,128)S(1)}, f32[8,1024]{1,0:T(8,128)S(1)}, f32[8,1024]{1,0:T(8,128)S(1)}) custom-call(s32[1,1024]{1,0:T(1,128)S(1)} %copy-done.2, f32[128,256]{1,0:T(8,128)S(1)} %project.2.refs_0_, s16[144,256]{1,0:T(8,128)(2,1)S(1)} %collective-permute-done.1.refs_1_, ...), custom_call_target="tpu_custom_call" | custom-call | tf_op jit(solution)/shard_map/outer/pallas_call | solution.py:152
  21.5 2.0 %collective-permute-start.4 = (f32[8,1024]{1,0:T(8,128)S(1)}, f32[8,1024]{1,0:T(8,128)S(1)}, u32[]{:S(2)}, u32[]{:S(2)}) collective-permute-start(f32[8,1024]{1,0:T(8,128)S(1)} %get-tuple-element.22), channel_id=1, source_target_pairs={{0,3},{1,2},{2,1},{3,0},{4,7},{5,6},{6,5},{7,4},{8,11},{9,10},{10,... | collective-permute-start | bytes 98312 | tf_op jit(solution)/shard_map/ppermute | solution.py:23
  23.5 0.3 collective-permute-start.5
  23.8 2.1 %collective-permute-start.6 = (f32[8,1024]{1,0:T(8,128)S(1)}, f32[8,1024]{1,0:T(8,128)S(1)}, u32[]{:S(2)}, u32[]{:S(2)}) collective-permute-start(f32[8,1024]{1,0:T(8,128)S(1)} %get-tuple-element.24), channel_id=1, source_target_pairs={{0,1},{1,0},{2,3},{3,2},{4,5},{5,4},{6,7},{7,6},{8,9},{9,8},{10,11... | collective-permute-start | bytes 98312 | tf_op jit(solution)/shard_map/ppermute | solution.py:23
  25.9 1.3 %collective-permute-done.4.refs_1_ = f32[8,1024]{1,0:T(8,128)S(1)} collective-permute-done((f32[8,1024]{1,0:T(8,128)S(1)}, f32[8,1024]{1,0:T(8,128)S(1)}, u32[]{:S(2)}, u32[]{:S(2)}) %collective-permute-start.4) | collective-permute-done | bytes 32800 | tf_op jit(solution)/shard_map/ppermute | solution.py:23
  27.2 1.3 %collective-permute-done.5.refs_2_ = f32[8,1024]{1,0:T(8,128)S(1)} collective-permute-done((f32[8,1024]{1,0:T(8,128)S(1)}, f32[8,1024]{1,0:T(8,128)S(1)}, u32[]{:S(2)}, u32[]{:S(2)}) %collective-permute-start.5) | collective-permute-done | bytes 32800 | tf_op jit(solution)/shard_map/ppermute | solution.py:23
  28.5 0.0 collective-permute-done.6.refs_3_
  28.5 0.1 train.1.refs_2_
  28.6 0.0 collective-permute-start.7
  28.6 1.2 %collective-permute-done.7.refs_3_ = bf16[16,512]{1,0:T(8,128)(2,1)S(1)} collective-permute-done((bf16[16,512]{1,0:T(8,128)(2,1)S(1)}, bf16[16,512]{1,0:T(8,128)(2,1)S(1)}, u32[]{:S(2)}, u32[]{:S(2)}) %collective-permute-start.7) | collective-permute-done | bytes 16416 | tf_op jit(solution)/shard_map/ppermute | solution.py:23
  29.8 0.0 collective-permute-done.refs_1_
  29.8 0.7 %score.1 = (f32[32,128]{1,0:T(8,128)S(1)}, f32[32,128]{1,0:T(8,128)S(1)}, f32[32,128]{1,0:T(8,128)S(1)}, f32[32,128]{1,0:T(8,128)S(1)}) custom-call(bf16[512,1024]{1,0:T(8,128)(2,1)S(1)} %copy-done.1, bf16[512,1024]{1,0:T(8,128)(2,1)S(1)} %collective-permute-done.refs_1_, bf16[16,512]{1,0:T(8,128)(2,1)S(1)} %train.1.refs_2_, ...), custom_call_target="tpu_custom_call" | custom-call | tf_op jit(solution)/shard_map/score/pallas_call | solution.py:207
  30.5 2.0 %collective-permute-start.8 = (f32[32,128]{1,0:T(8,128)S(1)}, f32[32,128]{1,0:T(8,128)S(1)}, u32[]{:S(2)}, u32[]{:S(2)}) collective-permute-start(f32[32,128]{1,0:T(8,128)S(1)} %get-tuple-element.26), channel_id=1, source_target_pairs={{0,3},{1,2},{2,1},{3,0},{4,7},{5,6},{6,5},{7,4},{8,11},{9,10},{10,... | collective-permute-start | bytes 49160 | tf_op jit(solution)/shard_map/ppermute | solution.py:23
  32.5 0.8 %collective-permute-start.9 = (f32[32,128]{1,0:T(8,128)S(1)}, f32[32,128]{1,0:T(8,128)S(1)}, u32[]{:S(2)}, u32[]{:S(2)}) collective-permute-start(f32[32,128]{1,0:T(8,128)S(1)} %get-tuple-element.27), channel_id=1, source_target_pairs={{0,2},{1,3},{2,0},{3,1},{4,6},{5,7},{6,4},{7,5},{8,10},{9,11},{10,... | collective-permute-start | bytes 49160 | tf_op jit(solution)/shard_map/ppermute | solution.py:23
  33.3 1.6 %collective-permute-start.10 = (f32[32,128]{1,0:T(8,128)S(1)}, f32[32,128]{1,0:T(8,128)S(1)}, u32[]{:S(2)}, u32[]{:S(2)}) collective-permute-start(f32[32,128]{1,0:T(8,128)S(1)} %get-tuple-element.28), channel_id=1, source_target_pairs={{0,1},{1,0},{2,3},{3,2},{4,5},{5,4},{6,7},{7,6},{8,9},{9,8},{10,11... | collective-permute-start | bytes 49160 | tf_op jit(solution)/shard_map/ppermute | solution.py:23
  34.9 1.2 %collective-permute-done.8.refs_1_ = f32[32,128]{1,0:T(8,128)S(1)} collective-permute-done((f32[32,128]{1,0:T(8,128)S(1)}, f32[32,128]{1,0:T(8,128)S(1)}, u32[]{:S(2)}, u32[]{:S(2)}) %collective-permute-start.8) | collective-permute-done | bytes 16416 | tf_op jit(solution)/shard_map/ppermute | solution.py:23
  36.0 1.2 %collective-permute-done.9.refs_2_ = f32[32,128]{1,0:T(8,128)S(1)} collective-permute-done((f32[32,128]{1,0:T(8,128)S(1)}, f32[32,128]{1,0:T(8,128)S(1)}, u32[]{:S(2)}, u32[]{:S(2)}) %collective-permute-start.9) | collective-permute-done | bytes 16416 | tf_op jit(solution)/shard_map/ppermute | solution.py:23
  37.2 0.0 collective-permute-done.10.refs_3_
  37.2 0.1 collective-permute-start.11
  37.3 1.2 %collective-permute-done.11.far = f32[2,8,128]{2,1,0:T(8,128)S(1)} collective-permute-done((f32[2,8,128]{2,1,0:T(8,128)S(1)}, f32[2,8,128]{2,1,0:T(8,128)S(1)}, u32[]{:S(2)}, u32[]{:S(2)}) %collective-permute-start.11) | collective-permute-done | bytes 8224 | tf_op jit(solution)/shard_map/ppermute | solution.py:23
  38.4 0.6 %place.1 = f32[8,4,128]{2,1,0:T(4,128)} custom-call(f32[2,8,128]{2,1,0:T(8,128)S(1)} %get-tuple-element.29.near, f32[2,8,128]{2,1,0:T(8,128)S(1)} %collective-permute-done.11.far), custom_call_target="tpu_custom_call" | custom-call | tf_op jit(solution)/shard_map/place/pallas_call | solution.py:249
  (5 shorter events, 0.0 us)
Async XLA Ops:
  0.0 14.9 %copy-start = (bf16[2048,64]{0,1:T(8,128)(2,1)S(1)}, bf16[2048,64]{0,1:T(8,128)(2,1)}, u32[]{:S(2)}) copy-start(bf16[2048,64]{0,1:T(8,128)(2,1)} %param.8) | copy-start | bytes 786436
  0.0 29.8 %collective-permute-start = (bf16[512,1024]{1,0:T(8,128)(2,1)}, bf16[512,1024]{1,0:T(8,128)(2,1)S(1)}, u32[]{:S(2)}, u32[]{:S(2)}) collective-permute-start(bf16[512,1024]{1,0:T(8,128)(2,1)} %refs_0_.1), channel_id=1, source_target_pairs={{0,8},{4,12},{8,0},{12,4},{1,9},{5,13},{9,1},{13,5},{2,10},{6,14},... | collective-permute-start | bytes 3145736 | tf_op jit(solution)/shard_map/ppermute | solution.py:23
  10.5 10.5 %copy-start.2 = (s32[1,1024]{1,0:T(1,128)S(1)}, s32[1,1024]{1,0:T(1,128)}, u32[]{:S(2)}) copy-start(s32[1,1024]{1,0:T(1,128)} %ids.3) | copy-start | bytes 12292
  10.5 19.3 %copy-start.1 = (bf16[512,1024]{1,0:T(8,128)(2,1)S(1)}, bf16[512,1024]{1,0:T(8,128)(2,1)}, u32[]{:S(2)}) copy-start(bf16[512,1024]{1,0:T(8,128)(2,1)} %refs_0_.1) | copy-start | bytes 3145732
  10.5 8.2 %collective-permute-start.1 = (s16[144,256]{1,0:T(8,128)(2,1)S(1)}, s16[144,256]{1,0:T(8,128)(2,1)S(1)}, u32[]{:S(2)}, u32[]{:S(2)}) collective-permute-start(s16[144,256]{1,0:T(8,128)(2,1)S(1)} %get-tuple-element.18), channel_id=1, source_target_pairs={{0,1},{1,0},{2,3},{3,2},{4,5},{5,4},{6,7},{7,6},{8,9},{9,8},{10,11... | collective-permute-start | bytes 221192 | tf_op jit(solution)/shard_map/ppermute | solution.py:23
  12.1 7.5 %collective-permute-start.2 = (s16[144,256]{1,0:T(8,128)(2,1)S(1)}, s16[144,256]{1,0:T(8,128)(2,1)S(1)}, u32[]{:S(2)}, u32[]{:S(2)}) collective-permute-start(s16[144,256]{1,0:T(8,128)(2,1)S(1)} %get-tuple-element.19), channel_id=1, source_target_pairs={{0,2},{1,3},{2,0},{3,1},{4,6},{5,7},{6,4},{7,5},{8,10},{9,11},{10,... | collective-permute-start | bytes 221192 | tf_op jit(solution)/shard_map/ppermute | solution.py:23
  14.7 6.3 %collective-permute-start.3 = (s16[144,256]{1,0:T(8,128)(2,1)S(1)}, s16[144,256]{1,0:T(8,128)(2,1)S(1)}, u32[]{:S(2)}, u32[]{:S(2)}) collective-permute-start(s16[144,256]{1,0:T(8,128)(2,1)S(1)} %get-tuple-element.20), channel_id=1, source_target_pairs={{0,3},{1,2},{2,1},{3,0},{4,7},{5,6},{6,5},{7,4},{8,11},{9,10},{10,... | collective-permute-start | bytes 221192 | tf_op jit(solution)/shard_map/ppermute | solution.py:23
  21.5 5.8 %collective-permute-start.4 = (f32[8,1024]{1,0:T(8,128)S(1)}, f32[8,1024]{1,0:T(8,128)S(1)}, u32[]{:S(2)}, u32[]{:S(2)}) collective-permute-start(f32[8,1024]{1,0:T(8,128)S(1)} %get-tuple-element.22), channel_id=1, source_target_pairs={{0,3},{1,2},{2,1},{3,0},{4,7},{5,6},{6,5},{7,4},{8,11},{9,10},{10,... | collective-permute-start | bytes 98312 | tf_op jit(solution)/shard_map/ppermute | solution.py:23
  23.5 5.0 %collective-permute-start.5 = (f32[8,1024]{1,0:T(8,128)S(1)}, f32[8,1024]{1,0:T(8,128)S(1)}, u32[]{:S(2)}, u32[]{:S(2)}) collective-permute-start(f32[8,1024]{1,0:T(8,128)S(1)} %get-tuple-element.23), channel_id=1, source_target_pairs={{0,2},{1,3},{2,0},{3,1},{4,6},{5,7},{6,4},{7,5},{8,10},{9,11},{10,... | collective-permute-start | bytes 98312 | tf_op jit(solution)/shard_map/ppermute | solution.py:23
  23.8 4.7 %collective-permute-start.6 = (f32[8,1024]{1,0:T(8,128)S(1)}, f32[8,1024]{1,0:T(8,128)S(1)}, u32[]{:S(2)}, u32[]{:S(2)}) collective-permute-start(f32[8,1024]{1,0:T(8,128)S(1)} %get-tuple-element.24), channel_id=1, source_target_pairs={{0,1},{1,0},{2,3},{3,2},{4,5},{5,4},{6,7},{7,6},{8,9},{9,8},{10,11... | collective-permute-start | bytes 98312 | tf_op jit(solution)/shard_map/ppermute | solution.py:23
  28.6 1.2 %collective-permute-start.7 = (bf16[16,512]{1,0:T(8,128)(2,1)S(1)}, bf16[16,512]{1,0:T(8,128)(2,1)S(1)}, u32[]{:S(2)}, u32[]{:S(2)}) collective-permute-start(bf16[16,512]{1,0:T(8,128)(2,1)S(1)} %train.1.refs_2_), channel_id=1, source_target_pairs={{0,4},{4,0},{8,12},{12,8},{1,5},{5,1},{9,13},{13,9},{2,6},{6,2},{1... | collective-permute-start | bytes 49160 | tf_op jit(solution)/shard_map/ppermute | solution.py:23
  30.5 5.6 %collective-permute-start.8 = (f32[32,128]{1,0:T(8,128)S(1)}, f32[32,128]{1,0:T(8,128)S(1)}, u32[]{:S(2)}, u32[]{:S(2)}) collective-permute-start(f32[32,128]{1,0:T(8,128)S(1)} %get-tuple-element.26), channel_id=1, source_target_pairs={{0,3},{1,2},{2,1},{3,0},{4,7},{5,6},{6,5},{7,4},{8,11},{9,10},{10,... | collective-permute-start | bytes 49160 | tf_op jit(solution)/shard_map/ppermute | solution.py:23
  32.5 4.7 %collective-permute-start.9 = (f32[32,128]{1,0:T(8,128)S(1)}, f32[32,128]{1,0:T(8,128)S(1)}, u32[]{:S(2)}, u32[]{:S(2)}) collective-permute-start(f32[32,128]{1,0:T(8,128)S(1)} %get-tuple-element.27), channel_id=1, source_target_pairs={{0,2},{1,3},{2,0},{3,1},{4,6},{5,7},{6,4},{7,5},{8,10},{9,11},{10,... | collective-permute-start | bytes 49160 | tf_op jit(solution)/shard_map/ppermute | solution.py:23
  33.3 3.9 %collective-permute-start.10 = (f32[32,128]{1,0:T(8,128)S(1)}, f32[32,128]{1,0:T(8,128)S(1)}, u32[]{:S(2)}, u32[]{:S(2)}) collective-permute-start(f32[32,128]{1,0:T(8,128)S(1)} %get-tuple-element.28), channel_id=1, source_target_pairs={{0,1},{1,0},{2,3},{3,2},{4,5},{5,4},{6,7},{7,6},{8,9},{9,8},{10,11... | collective-permute-start | bytes 49160 | tf_op jit(solution)/shard_map/ppermute | solution.py:23
  37.2 1.2 %collective-permute-start.11 = (f32[2,8,128]{2,1,0:T(8,128)S(1)}, f32[2,8,128]{2,1,0:T(8,128)S(1)}, u32[]{:S(2)}, u32[]{:S(2)}) collective-permute-start(f32[2,8,128]{2,1,0:T(8,128)S(1)} %get-tuple-element.30), channel_id=1, source_target_pairs={{0,4},{4,0},{8,12},{12,8},{1,5},{5,1},{9,13},{13,9},{2,6},{6,2},{1... | collective-permute-start | bytes 24584 | tf_op jit(solution)/shard_map/ppermute | solution.py:23

commit v4 on v0

v4 whole, which is shorter than its diff:
```python
import functools

import jax
import jax.numpy as jnp
from jax import lax
from jax.experimental import pallas as pl
from jax.experimental.pallas import tpu as pltpu
from jax.sharding import PartitionSpec as P

DOC_DEV = 8
F32 = jnp.float32
BF16 = jnp.bfloat16
NT = (((1,), (1,)), ((), ()))
VMEM = pl.BlockSpec(memory_space=pltpu.VMEM)
SMALL = pltpu.CompilerParams(vmem_limit_bytes=8 * 2**20)
STEPS = 32000.0
LANES = 128


def swapped(block, axis, flip):
    return lax.ppermute(block, axis, [(i, i ^ flip) for i in range(lax.axis_size(axis))])


def crossed(block, core, flip):
    shares, ndev = lax.axis_size("tensor"), lax.axis_size("docs")
    pairs = [(d * shares + s, (d ^ core) * shares + (s ^ flip)) for d in range(ndev) for s in range(shares)]
    return lax.ppermute(block, ("docs", "tensor"), pairs)


def coded(v):
    top = jnp.maximum(jnp.max(jnp.abs(v), axis=0, keepdims=True), 1e-30)
    e = jnp.floor(jnp.log2(top)) + 1.0
    steps = jnp.clip(jnp.round(v * (jnp.exp2(-e) * STEPS)), -32767.0, 32767.0)
    return steps.astype(jnp.int32), e.astype(jnp.int32)


def decoded(steps, e):
    return steps.astype(jnp.int32).astype(F32) * (jnp.exp2(e.astype(F32)) * (1.0 / STEPS))


def folded(e):
    return jnp.concatenate([e[:, a : a + LANES] for a in range(0, e.shape[1], LANES)], axis=0)


def unfolded(e):
    return jnp.concatenate([e[a : a + 1] for a in range(e.shape[0])], axis=1)


def projected(rows, weights):
    step = 256
    parts = [
        lax.dot_general(rows[a : a + step, :], weights[...], NT, preferred_element_type=F32).T
        for a in range(0, rows.shape[0], step)
    ]
    return jnp.concatenate(parts, axis=1)


def write_message(sent, v):
    steps, e = coded(v)
    tokens = v.shape[1]
    sent[:, :tokens] = steps.astype(jnp.int16)
    tail = folded(e)
    blank = jnp.zeros((v.shape[0] - tail.shape[0], LANES), jnp.int32)
    sent[:, tokens:] = jnp.concatenate([tail, blank], axis=0).astype(jnp.int16)


def read_message(sent):
    tokens = sent.shape[1] - LANES
    tail = sent[:, tokens:].astype(jnp.int32)
    return decoded(sent[:, :tokens], unfolded(tail[: tokens // LANES]))


def inputs_kernel(x, px, own, sent):
    v = projected(x, px)
    own[...] = v
    write_message(sent, v)


def fold_in_kernel(own, arrived, total, sent):
    v = own[...] + read_message(arrived)
    total[...] = v
    write_message(sent, v)


def fold_in(own, arrived):
    return pl.pallas_call(
        fold_in_kernel,
        out_shape=[jax.ShapeDtypeStruct(own.shape, F32), jax.ShapeDtypeStruct(arrived.shape, jnp.int16)],
        in_specs=[VMEM] * 2,
        out_specs=[VMEM] * 2,
        compiler_params=SMALL,
        name="fold_in",
    )(own, arrived)


def project_inputs(inputs, proj_t):
    rank, tokens = proj_t.shape[0], inputs.shape[0]
    return pl.pallas_call(
        inputs_kernel,
        out_shape=[
            jax.ShapeDtypeStruct((rank, tokens), F32),
            jax.ShapeDtypeStruct((rank, tokens + LANES), jnp.int16),
        ],
        in_specs=[VMEM] * 2,
        out_specs=[VMEM] * 2,
        compiler_params=SMALL,
        cost_estimate=pl.CostEstimate(flops=20_000_000_000, bytes_accessed=4_000_000, transcendentals=0),
        name="inputs",
    )(inputs, proj_t)


def grads_kernel(shares, g, pg, own, *rest):
    outs, held = rest[:-1], rest[-1]
    me = lax.axis_index("tensor")
    v = projected(g, pg)
    rank, tokens = v.shape
    rows = rank // shares
    steps, e = coded(v)
    tail = folded(e)
    if rows > tail.shape[0]:
        tail = jnp.concatenate([tail, jnp.zeros((rows - tail.shape[0], LANES), jnp.int32)], axis=0)
    tail = tail.astype(jnp.int16)
    held[...] = v.reshape(shares, rows, tokens)
    own[...] = held[me]
    held[...] = steps.astype(F32).reshape(shares, rows, tokens)
    for k, out in enumerate(outs):
        out[:, :tokens] = held[me ^ (len(outs) - k)].astype(jnp.int32).astype(jnp.int16)
        out[:, tokens:] = tail


def project_grads(grads, proj_t, shares):
    rank, tokens = proj_t.shape[0], grads.shape[0]
    rows = rank // shares
    return pl.pallas_call(
        functools.partial(grads_kernel, shares),
        out_shape=[jax.ShapeDtypeStruct((rows, tokens), F32)]
        + [jax.ShapeDtypeStruct((rows, tokens + LANES), jnp.int16)] * (shares - 1),
        in_specs=[VMEM] * 2,
        out_specs=[VMEM] * shares,
        scratch_shapes=[pltpu.VMEM((shares, rows, tokens), F32)],
        compiler_params=SMALL,
        name="grads",
    )(grads, proj_t)


def train_kernel(ids, x_own, x_sent, g_own, *refs):
    g_sent, out = refs[:-1], refs[-1]
    x, g = x_own[...] + read_message(x_sent), g_own[...]
    for sent in g_sent:
        g = g + read_message(sent)
    rows, tokens = g.shape
    mask = ids[...] == lax.broadcasted_iota(jnp.int32, (DOC_DEV, tokens), 0)
    counts = jnp.sum(mask.astype(F32), axis=1, keepdims=True)
    picked = jnp.concatenate([jnp.where(mask, g[i : i + 1], 0.0) for i in range(rows)], axis=0)
    picked_hi = picked.astype(BF16)
    picked_lo = (picked - picked_hi.astype(F32)).astype(BF16)
    x_hi = x.astype(BF16)
    x_lo = (x - x_hi.astype(F32)).astype(BF16)
    dot = functools.partial(lax.dot_general, dimension_numbers=NT, preferred_element_type=F32)
    total = dot(picked_hi, x_hi) + (dot(picked_hi, x_lo) + dot(picked_lo, x_hi))
    train = jnp.concatenate([total[i * DOC_DEV : (i + 1) * DOC_DEV] for i in range(rows)], axis=1) / counts
    half = train.shape[1] // 2
    out[...] = jnp.concatenate([train[:, :half], train[:, half:]], axis=0).astype(BF16)


def mean_gradients(ids, x_own, x_sent, g_own, g_sent):
    width = g_own.shape[0] * x_own.shape[0]
    return pl.pallas_call(
        train_kernel,
        out_shape=jax.ShapeDtypeStruct((2 * DOC_DEV, width // 2), BF16),
        in_specs=[VMEM] * (4 + len(g_sent)),
        out_specs=VMEM,
        compiler_params=SMALL,
        name="train",
    )(ids, x_own, x_sent, g_own, *g_sent)


def scores_of(trains, queries):
    rows = []
    for train in trains:
        t = train[...].astype(F32)
        rows.append(jnp.concatenate([t[:DOC_DEV], t[DOC_DEV:]], axis=1))
    docs = jnp.concatenate(rows, axis=0).astype(BF16)
    return lax.dot_general(docs, queries[...], NT, preferred_element_type=F32)


def near_kernel(mine, sibling, queries, out):
    out[...] = scores_of((mine, sibling), queries)


def score_kernel(shares, mine, sibling, near, *refs):
    blocks, outs, held = refs[: -shares - 1], refs[-shares - 1 : -1], refs[-1]
    me = lax.axis_index("tensor")
    count, width = near.shape[0], near.shape[1] // shares
    for m in range(len(blocks) + 1):
        scores = scores_of((mine, sibling), blocks[m - 1]) if m else near[...]
        for j in range(shares):
            held[j, m * count : (m + 1) * count, :] = scores[:, j * width : (j + 1) * width]
    for k in range(shares):
        outs[k][...] = held[me ^ k]


def score(mine, sibling, blocks, shares):
    rows, width = 2 * DOC_DEV, blocks[0].shape[0]
    near = pl.pallas_call(
        near_kernel,
        out_shape=jax.ShapeDtypeStruct((rows, width), F32),
        in_specs=[VMEM] * 3,
        out_specs=VMEM,
        compiler_params=SMALL,
        name="near",
    )(mine, sibling, blocks[0])
    shape = (rows * len(blocks), width // shares)
    return pl.pallas_call(
        functools.partial(score_kernel, shares),
        out_shape=[jax.ShapeDtypeStruct(shape, F32)] * shares,
        in_specs=[VMEM] * (2 + len(blocks)),
        out_specs=[VMEM] * shares,
        scratch_shapes=[pltpu.VMEM((shares, *shape), F32)],
        compiler_params=SMALL,
        name="score",
    )(mine, sibling, near, *blocks[1:])


def add_kernel(shares, *refs):
    parts, outs = refs[:shares], refs[shares:]
    total = parts[0][...]
    for part in parts[1:]:
        total = total + part[...]
    both = total.reshape(-1, 2, DOC_DEV, total.shape[1])
    for core, out in enumerate(outs):
        out[...] = both[:, 1 - core]


def add(parts):
    rows, width = parts[0].shape
    return pl.pallas_call(
        functools.partial(add_kernel, len(parts)),
        out_shape=[jax.ShapeDtypeStruct((rows // (2 * DOC_DEV), DOC_DEV, width), F32)] * 2,
        in_specs=[VMEM] * len(parts),
        out_specs=[VMEM] * 2,
        compiler_params=SMALL,
        name="add",
    )(*parts)


def place_kernel(near, far, out):
    me = lax.axis_index("docs")
    for m in range(near.shape[0]):
        out[:, pl.ds(me ^ (2 * m + 1), 1), :] = near[m][:, None, :]
        out[:, pl.ds(me ^ (2 * m), 1), :] = far[m][:, None, :]


def place(near, far):
    chips, docs, width = near.shape
    return pl.pallas_call(
        place_kernel,
        out_shape=jax.ShapeDtypeStruct((docs, 2 * chips, width), F32),
        in_specs=[VMEM] * 2,
        out_specs=VMEM,
        compiler_params=SMALL,
        name="place",
    )(near, far)


def per_device(inputs, grads, proj_in, proj_out, queries, ids):
    shares, ndev = lax.axis_size("tensor"), lax.axis_size("docs")
    blocks = [queries] + [swapped(queries, "docs", 2 * m) for m in range(1, ndev // 2)]
    flips = list(range(shares - 1, 0, -1))
    x, x_sent = project_inputs(inputs, proj_in.T)
    flip = shares // 2
    x_sent = swapped(x_sent, "tensor", flip)
    g_own, *g_coded = project_grads(grads, proj_out.T, shares)
    x_sent, g_own = lax.optimization_barrier((x_sent, g_own))
    while flip > 1:
        flip //= 2
        x, x_sent = fold_in(x, x_sent)
        x_sent = swapped(x_sent, "tensor", flip)
    g_sent = [swapped(g, "tensor", k) for k, g in zip(flips, g_coded)]
    train = mean_gradients(ids, x, x_sent, g_own, g_sent)
    scores = score(train, swapped(train, "docs", 1), blocks, shares)
    mine, sibling = add([crossed(scores[k], 1, k) for k in flips + [0]])
    return place(mine, swapped(sibling, "docs", 1))


def solution(mesh):
    in_specs = (
        P(("group", "docs"), "tensor"),
        P(("group", "docs"), "tensor"),
        P("tensor", None),
        P("tensor", None),
        P(("group", "docs"), "tensor"),
        P(("group", "docs"), None),
    )
    out_specs = P(("group", "docs"), None, "tensor")
    return jax.shard_map(
        per_device, mesh=mesh, in_specs=in_specs, out_specs=out_specs, check_vma=False
    )
```

time: 144 us -> 37.2 us (0.26)
  waiting for transfers between devices: 101 us -> 9.56 us
  matrix products: 20.1 us -> 0 us
  starting transfers between devices: 0.05 us -> 15.5 us
  between operations: 13.5 us -> 0.07 us
  Pallas kernels: 0 us -> 7.43 us
  other arithmetic: 3.14 us -> 0 us
  local copies, waits for them, and re-layouts: 6.37 us -> 4.49 us
    psum x1 -> x0, waiting for transfers between devices: 40.4 us -> none  [per_device(): proj_x, proj_g = lax.psum((part_in, part_out), 'tensor')]
    ppermute x3 -> x12, waiting for transfers between devices: 40.6 us -> 9.56 us  [the longest x8 7.48 us: swapped(): lax.ppermute(block, axis, [(i, i ^ flip) for i in range(lax.axis_size(axi...]
    dot_general x7 -> x0, matrix products: 20.1 us -> none  [the longest x1 10.5 us: per_device(): part_out = jnp.dot(grads, proj_out, preferred_element_type=jnp.float32)]
    unnamed x3 -> x0, waiting for transfers between devices: 19.7 us -> none
    ppermute x3 -> x12, starting transfers between devices: 0.01 us -> 15.5 us  [the longest x8 11.2 us: swapped(): lax.ppermute(block, axis, [(i, i ^ flip) for i in range(lax.axis_size(axi...]
    pallas_call x0 -> x8, Pallas kernels: none -> 7.43 us  [the longest x1 4.06 us: project_grads(): pl.pallas_call(functools.partial(grads_kernel, shares), out_shape=[jax.Sh...]
    another operation x4 -> x0, other arithmetic: 2.89 us -> none
    unnamed x11 -> x12, local copies, waits for them, and re-layouts: 5.24 us -> 4.49 us
  transfers between devices with their start and end apart: 5 -> 12, of which waited for: 5 -> 7; matrix products, arithmetic and copies ran while one was open for 2% -> 0% of each run, Pallas kernels for 0% -> 17%
where the time goes in v4:
time: 37.2 us; the launch traced here: 37 us
  starting transfers between devices  15.5 us (42%)
  waiting for transfers between devices  9.56 us (26%)
  Pallas kernels  7.43 us (20%)
  local copies, waits for them, and re-layouts  4.49 us (12%)
    ppermute x8, starting transfers between devices, swapped(): lax.ppermute(block, axis, [(i, i ^ flip) for i in range(lax.axis_size(axi...  11.2 us
    ppermute x8, waiting for transfers between devices, swapped(): lax.ppermute(block, axis, [(i, i ^ flip) for i in range(lax.axis_size(axi...  7.48 us
    unnamed x12, local copies, waits for them, and re-layouts  4.49 us
    ppermute x4, starting transfers between devices, crossed(): return lax.ppermute(block, ('docs', 'tensor'), pairs)  4.24 us
    pallas_call x1, Pallas kernels, project_grads(): pl.pallas_call(functools.partial(grads_kernel, shares), out_shape=[jax.Sh...  4.06 us
    ppermute x4, waiting for transfers between devices, crossed(): return lax.ppermute(block, ('docs', 'tensor'), pairs)  2.08 us
    pallas_call x1, Pallas kernels, project_inputs(): pl.pallas_call(inputs_kernel, out_shape=[jax.ShapeDtypeStruct((rank, toke...  1.34 us
  transfers between devices with their start and end apart: 12, of which 7 were waited for; matrix products, arithmetic and copies ran while one was open for 0% of the time, Pallas kernels for 17%

profile of v4, /device:TPU:0, one launch (start us, length us, event | category | flops | bytes accessed | tf_op | source)
XLA Modules:
  0.0 37.0 jit_solution(4760236784865111247)
XLA Ops:
  0.0 3.0 %collective-permute-start.6 = (bf16[512,1024]{1,0:T(8,128)(2,1)}, bf16[512,1024]{1,0:T(8,128)(2,1)S(1)}, u32[]{:S(2)}, u32[]{:S(2)}) collective-permute-start(bf16[512,1024]{1,0:T(8,128)(2,1)} %queries.1), channel_id=1, source_target_pairs={{0,8},{4,12},{8,0},{12,4},{1,9},{5,13},{9,1},{13,5},{2,10},{6,14},... | collective-permute-start | bytes 3145736 | tf_op jit(solution)/shard_map/ppermute | solution.py:21
  3.0 2.2 %copy-done.4 = bf16[1024,2048]{1,0:T(8,128)(2,1)S(1)} copy-done((bf16[1024,2048]{1,0:T(8,128)(2,1)S(1)}, bf16[1024,2048]{1,0:T(8,128)(2,1)}, u32[]{:S(2)}) %copy-start.4) | copy-done | bytes 4194328
  5.2 0.9 %copy-done.5 = bf16[2048,64]{0,1:T(8,128)(2,1)S(1)} copy-done((bf16[2048,64]{0,1:T(8,128)(2,1)S(1)}, bf16[2048,64]{0,1:T(8,128)(2,1)}, u32[]{:S(2)}) %copy-start.5) | copy-done | bytes 262168
  6.1 1.3 %inputs.1 = (f32[64,1024]{1,0:T(8,128)S(1)}, s16[64,1152]{1,0:T(8,128)(2,1)S(1)}) custom-call(bf16[1024,2048]{1,0:T(8,128)(2,1)S(1)} %copy-done.4, bf16[64,2048]{1,0:T(8,128)(2,1)S(1)} %bitcast.3), custom_call_target="tpu_custom_call" | custom-call | flops 20000000000 | bytes 4000000 | tf_op jit(solution)/shard_map/inputs/pallas_call | solution.py:98
  7.5 0.0 copy-start.3
  7.5 0.0 copy-start.1
  7.5 2.6 %collective-permute-start = (s16[64,1152]{1,0:T(8,128)(2,1)S(1)}, s16[64,1152]{1,0:T(8,128)(2,1)S(1)}, u32[]{:S(2)}, u32[]{:S(2)}) collective-permute-start(s16[64,1152]{1,0:T(8,128)(2,1)S(1)} %get-tuple-element.22), channel_id=1, source_target_pairs={{0,2},{1,3},{2,0},{3,1},{4,6},{5,7},{6,4},{7,5},{8,10},{9,11},{10,... | collective-permute-start | bytes 442376 | tf_op jit(solution)/shard_map/ppermute | solution.py:21
  10.1 1.2 %copy-done = bf16[1024,7168]{1,0:T(8,128)(2,1)S(1)} copy-done((bf16[1024,7168]{1,0:T(8,128)(2,1)S(1)}, bf16[1024,7168]{1,0:T(8,128)(2,1)}, u32[]{:S(2)}) %copy-start) | copy-done | bytes 14680088
  11.3 0.2 copy-done.2
  11.5 4.1 %grads.1 = (f32[16,1024]{1,0:T(8,128)S(1)}, s16[16,1152]{1,0:T(8,128)(2,1)S(1)}, s16[16,1152]{1,0:T(8,128)(2,1)S(1)}, s16[16,1152]{1,0:T(8,128)(2,1)S(1)}) custom-call(bf16[1024,7168]{1,0:T(8,128)(2,1)S(1)} %copy-done, bf16[64,7168]{1,0:T(8,128)(2,1)S(1)} %bitcast.2), custom_call_target="tpu_custom_call" | custom-call | tf_op jit(solution)/shard_map/grads/pallas_call | solution.py:134
  15.5 1.4 %collective-permute-done.arrived = s16[64,1152]{1,0:T(8,128)(2,1)S(1)} collective-permute-done((s16[64,1152]{1,0:T(8,128)(2,1)S(1)}, s16[64,1152]{1,0:T(8,128)(2,1)S(1)}, u32[]{:S(2)}, u32[]{:S(2)}) %collective-permute-start) | collective-permute-done | bytes 147488 | tf_op jit(solution)/shard_map/ppermute | solution.py:21
  16.9 0.1 fold_in.1
  17.0 0.7 %collective-permute-start.1 = (s16[64,1152]{1,0:T(8,128)(2,1)S(1)}, s16[64,1152]{1,0:T(8,128)(2,1)S(1)}, u32[]{:S(2)}, u32[]{:S(2)}) collective-permute-start(s16[64,1152]{1,0:T(8,128)(2,1)S(1)} %get-tuple-element.26), channel_id=1, source_target_pairs={{0,1},{1,0},{2,3},{3,2},{4,5},{5,4},{6,7},{7,6},{8,9},{9,8},{10,11... | collective-permute-start | bytes 442376 | tf_op jit(solution)/shard_map/ppermute | solution.py:21
  17.8 2.9 %collective-permute-start.2 = (s16[16,1152]{1,0:T(8,128)(2,1)S(1)}, s16[16,1152]{1,0:T(8,128)(2,1)S(1)}, u32[]{:S(2)}, u32[]{:S(2)}) collective-permute-start(s16[16,1152]{1,0:T(8,128)(2,1)S(1)} %get-tuple-element.28), channel_id=1, source_target_pairs={{0,3},{1,2},{2,1},{3,0},{4,7},{5,6},{6,5},{7,4},{8,11},{9,10},{10,... | collective-permute-start | bytes 110600 | tf_op jit(solution)/shard_map/ppermute | solution.py:21
  20.7 0.5 %collective-permute-start.3 = (s16[16,1152]{1,0:T(8,128)(2,1)S(1)}, s16[16,1152]{1,0:T(8,128)(2,1)S(1)}, u32[]{:S(2)}, u32[]{:S(2)}) collective-permute-start(s16[16,1152]{1,0:T(8,128)(2,1)S(1)} %get-tuple-element.29), channel_id=1, source_target_pairs={{0,2},{1,3},{2,0},{3,1},{4,6},{5,7},{6,4},{7,5},{8,10},{9,11},{10,... | collective-permute-start | bytes 110600 | tf_op jit(solution)/shard_map/ppermute | solution.py:21
  21.1 1.0 %collective-permute-start.4 = (s16[16,1152]{1,0:T(8,128)(2,1)S(1)}, s16[16,1152]{1,0:T(8,128)(2,1)S(1)}, u32[]{:S(2)}, u32[]{:S(2)}) collective-permute-start(s16[16,1152]{1,0:T(8,128)(2,1)S(1)} %get-tuple-element.30), channel_id=1, source_target_pairs={{0,1},{1,0},{2,3},{3,2},{4,5},{5,4},{6,7},{7,6},{8,9},{9,8},{10,11... | collective-permute-start | bytes 110600 | tf_op jit(solution)/shard_map/ppermute | solution.py:21
  22.2 3.9 %collective-permute-done.2.refs_0_ = s16[16,1152]{1,0:T(8,128)(2,1)S(1)} collective-permute-done((s16[16,1152]{1,0:T(8,128)(2,1)S(1)}, s16[16,1152]{1,0:T(8,128)(2,1)S(1)}, u32[]{:S(2)}, u32[]{:S(2)}) %collective-permute-start.2) | collective-permute-done | bytes 36896 | tf_op jit(solution)/shard_map/ppermute | solution.py:21
  26.0 0.2 collective-permute-done.3.refs_1_
  26.2 0.0 collective-permute-done.4.refs_2_
  26.3 0.5 %train.1.mine = bf16[16,512]{1,0:T(8,128)(2,1)S(1)} custom-call(s32[1,1024]{1,0:T(1,128)S(1)} %copy-done.3, f32[64,1024]{1,0:T(8,128)S(1)} %get-tuple-element.25.x_own, s16[64,1152]{1,0:T(8,128)(2,1)S(1)} %collective-permute-done.1.x_sent, f32[16,1024]{1,0:T(8,128)S(1)} %get-tuple-element.27.g_own, s16[16,1152]{1,0:T(8,128)(2,1)S(1)} %collective-permute-done.2.refs_0_, ...), custom_call_target="tpu_custom_call" | custom-call | tf_op jit(solution)/shard_map/train/pallas_call | solution.py:168
  26.8 0.1 collective-permute-start.5
  26.9 1.2 %collective-permute-done.5.sibling = bf16[16,512]{1,0:T(8,128)(2,1)S(1)} collective-permute-done((bf16[16,512]{1,0:T(8,128)(2,1)S(1)}, bf16[16,512]{1,0:T(8,128)(2,1)S(1)}, u32[]{:S(2)}, u32[]{:S(2)}) %collective-permute-start.5) | collective-permute-done | bytes 16416 | tf_op jit(solution)/shard_map/ppermute | solution.py:21
  28.0 0.4 %near.1 = f32[16,512]{1,0:T(8,128)S(1)} custom-call(bf16[16,512]{1,0:T(8,128)(2,1)S(1)} %train.1.mine, bf16[16,512]{1,0:T(8,128)(2,1)S(1)} %collective-permute-done.5.sibling, bf16[512,1024]{1,0:T(8,128)(2,1)S(1)} %copy-done.1), custom_call_target="tpu_custom_call" | custom-call | tf_op jit(solution)/shard_map/near/pallas_call | solution.py:205
  28.4 0.4 %score.1 = (f32[32,128]{1,0:T(8,128)S(1)}, f32[32,128]{1,0:T(8,128)S(1)}, f32[32,128]{1,0:T(8,128)S(1)}, f32[32,128]{1,0:T(8,128)S(1)}) custom-call(bf16[16,512]{1,0:T(8,128)(2,1)S(1)} %train.1.mine, bf16[16,512]{1,0:T(8,128)(2,1)S(1)} %collective-permute-done.5.sibling, f32[16,512]{1,0:T(8,128)S(1)} %near.1, ...), custom_call_target="tpu_custom_call" | custom-call | tf_op jit(solution)/shard_map/score/pallas_call | solution.py:214
  28.8 2.3 %collective-permute-start.7 = (f32[32,128]{1,0:T(8,128)S(1)}, f32[32,128]{1,0:T(8,128)S(1)}, u32[]{:S(2)}, u32[]{:S(2)}) collective-permute-start(f32[32,128]{1,0:T(8,128)S(1)} %get-tuple-element.31), channel_id=1, source_target_pairs={{0,7},{1,6},{2,5},{3,4},{4,3},{5,2},{6,1},{7,0},{8,15},{9,14},{10,... | collective-permute-start | bytes 49160 | tf_op jit(solution)/shard_map/ppermute | solution.py:27
  31.1 1.6 %collective-permute-start.9 = (f32[32,128]{1,0:T(8,128)S(1)}, f32[32,128]{1,0:T(8,128)S(1)}, u32[]{:S(2)}, u32[]{:S(2)}) collective-permute-start(f32[32,128]{1,0:T(8,128)S(1)} %get-tuple-element.33), channel_id=1, source_target_pairs={{0,5},{1,4},{2,7},{3,6},{4,1},{5,0},{6,3},{7,2},{8,13},{9,12},{10,... | collective-permute-start | bytes 49160 | tf_op jit(solution)/shard_map/ppermute | solution.py:27
  32.7 0.3 collective-permute-start.10
  33.0 0.7 %collective-permute-done.7.refs_0_ = f32[32,128]{1,0:T(8,128)S(1)} collective-permute-done((f32[32,128]{1,0:T(8,128)S(1)}, f32[32,128]{1,0:T(8,128)S(1)}, u32[]{:S(2)}, u32[]{:S(2)}) %collective-permute-start.7) | collective-permute-done | bytes 16416 | tf_op jit(solution)/shard_map/ppermute | solution.py:27
  33.8 1.3 %collective-permute-done.8.refs_1_ = f32[32,128]{1,0:T(8,128)S(1)} collective-permute-done((f32[32,128]{1,0:T(8,128)S(1)}, f32[32,128]{1,0:T(8,128)S(1)}, u32[]{:S(2)}, u32[]{:S(2)}) %collective-permute-start.8) | collective-permute-done | bytes 16416 | tf_op jit(solution)/shard_map/ppermute | solution.py:27
  35.1 0.4 %collective-permute-start.11 = (f32[2,8,128]{2,1,0:T(8,128)S(1)}, f32[2,8,128]{2,1,0:T(8,128)S(1)}, u32[]{:S(2)}, u32[]{:S(2)}) collective-permute-start(f32[2,8,128]{2,1,0:T(8,128)S(1)} %get-tuple-element.36), channel_id=1, source_target_pairs={{0,4},{4,0},{8,12},{12,8},{1,5},{5,1},{9,13},{13,9},{2,6},{6,2},{1... | collective-permute-start | bytes 24584 | tf_op jit(solution)/shard_map/ppermute | solution.py:21
  35.6 0.8 %collective-permute-done.11.far = f32[2,8,128]{2,1,0:T(8,128)S(1)} collective-permute-done((f32[2,8,128]{2,1,0:T(8,128)S(1)}, f32[2,8,128]{2,1,0:T(8,128)S(1)}, u32[]{:S(2)}, u32[]{:S(2)}) %collective-permute-start.11) | collective-permute-done | bytes 8224 | tf_op jit(solution)/shard_map/ppermute | solution.py:21
  36.4 0.6 %place.1 = f32[8,4,128]{2,1,0:T(4,128)} custom-call(f32[2,8,128]{2,1,0:T(8,128)S(1)} %get-tuple-element.35.near, f32[2,8,128]{2,1,0:T(8,128)S(1)} %collective-permute-done.11.far), custom_call_target="tpu_custom_call" | custom-call | tf_op jit(solution)/shard_map/place/pallas_call | solution.py:256
  (12 shorter events, 0.0 us)
Async XLA Ops:
  0.0 28.4 %collective-permute-start.6 = (bf16[512,1024]{1,0:T(8,128)(2,1)}, bf16[512,1024]{1,0:T(8,128)(2,1)S(1)}, u32[]{:S(2)}, u32[]{:S(2)}) collective-permute-start(bf16[512,1024]{1,0:T(8,128)(2,1)} %queries.1), channel_id=1, source_target_pairs={{0,8},{4,12},{8,0},{12,4},{1,9},{5,13},{9,1},{13,5},{2,10},{6,14},... | collective-permute-start | bytes 3145736 | tf_op jit(solution)/shard_map/ppermute | solution.py:21
  3.0 2.2 %copy-start.4 = (bf16[1024,2048]{1,0:T(8,128)(2,1)S(1)}, bf16[1024,2048]{1,0:T(8,128)(2,1)}, u32[]{:S(2)}) copy-start(bf16[1024,2048]{1,0:T(8,128)(2,1)} %x.1) | copy-start | bytes 12582916
  5.2 0.9 %copy-start.5 = (bf16[2048,64]{0,1:T(8,128)(2,1)S(1)}, bf16[2048,64]{0,1:T(8,128)(2,1)}, u32[]{:S(2)}) copy-start(bf16[2048,64]{0,1:T(8,128)(2,1)} %param.8) | copy-start | bytes 786436
  6.1 5.2 %copy-start = (bf16[1024,7168]{1,0:T(8,128)(2,1)S(1)}, bf16[1024,7168]{1,0:T(8,128)(2,1)}, u32[]{:S(2)}) copy-start(bf16[1024,7168]{1,0:T(8,128)(2,1)} %g.1) | copy-start | bytes 44040196
  6.1 5.4 %copy-start.2 = (bf16[7168,64]{0,1:T(8,128)(2,1)S(1)}, bf16[7168,64]{0,1:T(8,128)(2,1)}, u32[]{:S(2)}) copy-start(bf16[7168,64]{0,1:T(8,128)(2,1)} %param.9) | copy-start | bytes 2752516
  7.5 18.8 %copy-start.3 = (s32[1,1024]{1,0:T(1,128)S(1)}, s32[1,1024]{1,0:T(1,128)}, u32[]{:S(2)}) copy-start(s32[1,1024]{1,0:T(1,128)} %ids.1) | copy-start | bytes 12292
  7.5 20.6 %copy-start.1 = (bf16[512,1024]{1,0:T(8,128)(2,1)S(1)}, bf16[512,1024]{1,0:T(8,128)(2,1)}, u32[]{:S(2)}) copy-start(bf16[512,1024]{1,0:T(8,128)(2,1)} %queries.1) | copy-start | bytes 3145732
  7.5 9.4 %collective-permute-start = (s16[64,1152]{1,0:T(8,128)(2,1)S(1)}, s16[64,1152]{1,0:T(8,128)(2,1)S(1)}, u32[]{:S(2)}, u32[]{:S(2)}) collective-permute-start(s16[64,1152]{1,0:T(8,128)(2,1)S(1)} %get-tuple-element.22), channel_id=1, source_target_pairs={{0,2},{1,3},{2,0},{3,1},{4,6},{5,7},{6,4},{7,5},{8,10},{9,11},{10,... | collective-permute-start | bytes 442376 | tf_op jit(solution)/shard_map/ppermute | solution.py:21
  17.0 9.2 %collective-permute-start.1 = (s16[64,1152]{1,0:T(8,128)(2,1)S(1)}, s16[64,1152]{1,0:T(8,128)(2,1)S(1)}, u32[]{:S(2)}, u32[]{:S(2)}) collective-permute-start(s16[64,1152]{1,0:T(8,128)(2,1)S(1)} %get-tuple-element.26), channel_id=1, source_target_pairs={{0,1},{1,0},{2,3},{3,2},{4,5},{5,4},{6,7},{7,6},{8,9},{9,8},{10,11... | collective-permute-start | bytes 442376 | tf_op jit(solution)/shard_map/ppermute | solution.py:21
  17.8 8.3 %collective-permute-start.2 = (s16[16,1152]{1,0:T(8,128)(2,1)S(1)}, s16[16,1152]{1,0:T(8,128)(2,1)S(1)}, u32[]{:S(2)}, u32[]{:S(2)}) collective-permute-start(s16[16,1152]{1,0:T(8,128)(2,1)S(1)} %get-tuple-element.28), channel_id=1, source_target_pairs={{0,3},{1,2},{2,1},{3,0},{4,7},{5,6},{6,5},{7,4},{8,11},{9,10},{10,... | collective-permute-start | bytes 110600 | tf_op jit(solution)/shard_map/ppermute | solution.py:21
  20.7 5.6 %collective-permute-start.3 = (s16[16,1152]{1,0:T(8,128)(2,1)S(1)}, s16[16,1152]{1,0:T(8,128)(2,1)S(1)}, u32[]{:S(2)}, u32[]{:S(2)}) collective-permute-start(s16[16,1152]{1,0:T(8,128)(2,1)S(1)} %get-tuple-element.29), channel_id=1, source_target_pairs={{0,2},{1,3},{2,0},{3,1},{4,6},{5,7},{6,4},{7,5},{8,10},{9,11},{10,... | collective-permute-start | bytes 110600 | tf_op jit(solution)/shard_map/ppermute | solution.py:21
  21.1 5.1 %collective-permute-start.4 = (s16[16,1152]{1,0:T(8,128)(2,1)S(1)}, s16[16,1152]{1,0:T(8,128)(2,1)S(1)}, u32[]{:S(2)}, u32[]{:S(2)}) collective-permute-start(s16[16,1152]{1,0:T(8,128)(2,1)S(1)} %get-tuple-element.30), channel_id=1, source_target_pairs={{0,1},{1,0},{2,3},{3,2},{4,5},{5,4},{6,7},{7,6},{8,9},{9,8},{10,11... | collective-permute-start | bytes 110600 | tf_op jit(solution)/shard_map/ppermute | solution.py:21
  26.8 1.2 %collective-permute-start.5 = (bf16[16,512]{1,0:T(8,128)(2,1)S(1)}, bf16[16,512]{1,0:T(8,128)(2,1)S(1)}, u32[]{:S(2)}, u32[]{:S(2)}) collective-permute-start(bf16[16,512]{1,0:T(8,128)(2,1)S(1)} %train.1.mine), channel_id=1, source_target_pairs={{0,4},{4,0},{8,12},{12,8},{1,5},{5,1},{9,13},{13,9},{2,6},{6,2},{1... | collective-permute-start | bytes 49160 | tf_op jit(solution)/shard_map/ppermute | solution.py:21
  28.8 5.0 %collective-permute-start.7 = (f32[32,128]{1,0:T(8,128)S(1)}, f32[32,128]{1,0:T(8,128)S(1)}, u32[]{:S(2)}, u32[]{:S(2)}) collective-permute-start(f32[32,128]{1,0:T(8,128)S(1)} %get-tuple-element.31), channel_id=1, source_target_pairs={{0,7},{1,6},{2,5},{3,4},{4,3},{5,2},{6,1},{7,0},{8,15},{9,14},{10,... | collective-permute-start | bytes 49160 | tf_op jit(solution)/shard_map/ppermute | solution.py:27
  31.1 4.1 %collective-permute-start.8 = (f32[32,128]{1,0:T(8,128)S(1)}, f32[32,128]{1,0:T(8,128)S(1)}, u32[]{:S(2)}, u32[]{:S(2)}) collective-permute-start(f32[32,128]{1,0:T(8,128)S(1)} %get-tuple-element.32), channel_id=1, source_target_pairs={{0,6},{1,7},{2,4},{3,5},{4,2},{5,3},{6,0},{7,1},{8,14},{9,15},{10,... | collective-permute-start | bytes 49160 | tf_op jit(solution)/shard_map/ppermute | solution.py:27
  31.1 4.1 %collective-permute-start.9 = (f32[32,128]{1,0:T(8,128)S(1)}, f32[32,128]{1,0:T(8,128)S(1)}, u32[]{:S(2)}, u32[]{:S(2)}) collective-permute-start(f32[32,128]{1,0:T(8,128)S(1)} %get-tuple-element.33), channel_id=1, source_target_pairs={{0,5},{1,4},{2,7},{3,6},{4,1},{5,0},{6,3},{7,2},{8,13},{9,12},{10,... | collective-permute-start | bytes 49160 | tf_op jit(solution)/shard_map/ppermute | solution.py:27
  32.7 2.4 %collective-permute-start.10 = (f32[32,128]{1,0:T(8,128)S(1)}, f32[32,128]{1,0:T(8,128)S(1)}, u32[]{:S(2)}, u32[]{:S(2)}) collective-permute-start(f32[32,128]{1,0:T(8,128)S(1)} %get-tuple-element.34), channel_id=1, source_target_pairs={{0,4},{1,5},{2,6},{3,7},{4,0},{5,1},{6,2},{7,3},{8,12},{9,13},{10,... | collective-permute-start | bytes 49160 | tf_op jit(solution)/shard_map/ppermute | solution.py:27
  35.1 1.2 %collective-permute-start.11 = (f32[2,8,128]{2,1,0:T(8,128)S(1)}, f32[2,8,128]{2,1,0:T(8,128)S(1)}, u32[]{:S(2)}, u32[]{:S(2)}) collective-permute-start(f32[2,8,128]{2,1,0:T(8,128)S(1)} %get-tuple-element.36), channel_id=1, source_target_pairs={{0,4},{4,0},{8,12},{12,8},{1,5},{5,1},{9,13},{13,9},{2,6},{6,2},{1... | collective-permute-start | bytes 24584 | tf_op jit(solution)/shard_map/ppermute | solution.py:21

commit v5 on v4

--- a/solution.py
+++ b/solution.py
@@ -12,9 +12,14 @@
 BF16 = jnp.bfloat16
 NT = (((1,), (1,)), ((), ()))
 VMEM = pl.BlockSpec(memory_space=pltpu.VMEM)
+ANY = pl.BlockSpec(memory_space=pl.ANY)
+STREAM = pltpu.CompilerParams(vmem_limit_bytes=int(53.5 * 2**20))
 SMALL = pltpu.CompilerParams(vmem_limit_bytes=8 * 2**20)
 STEPS = 32000.0
 LANES = 128
+ROW_STEPS = 4
+X_PIECES, X_AHEAD = 1, 4
+G_PIECES, G_AHEAD = 1, 2
 
 
 def swapped(block, axis, flip):
@@ -44,15 +49,6 @@
 
 def unfolded(e):
     return jnp.concatenate([e[a : a + 1] for a in range(e.shape[0])], axis=1)
-
-
-def projected(rows, weights):
-    step = 256
-    parts = [
-        lax.dot_general(rows[a : a + step, :], weights[...], NT, preferred_element_type=F32).T
-        for a in range(0, rows.shape[0], step)
-    ]
-    return jnp.concatenate(parts, axis=1)
 
 
 def write_message(sent, v):
@@ -70,10 +66,62 @@
     return decoded(sent[:, :tokens], unfolded(tail[: tokens // LANES]))
 
 
-def inputs_kernel(x, px, own, sent):
-    v = projected(x, px)
-    own[...] = v
-    write_message(sent, v)
+def stream_copies(hbm, buffer, sems, pieces):
+    rows, columns = buffer.shape[0] // ROW_STEPS, buffer.shape[1] // pieces
+    return [
+        pltpu.make_async_copy(
+            hbm.at[pl.ds(a * rows, rows), pl.ds(c * columns, columns)],
+            buffer.at[pl.ds(a * rows, rows), pl.ds(c * columns, columns)],
+            sems.at[a * pieces + c],
+        )
+        for a in range(ROW_STEPS)
+        for c in range(pieces)
+    ]
+
+
+def streamed(hbm, weights_hbm, buffer, weights, acc, out, sems, pieces, ahead):
+    me = lax.axis_index("tensor")
+    rows, columns = buffer.shape[0] // ROW_STEPS, buffer.shape[1] // pieces
+    copies = stream_copies(hbm, buffer, sems, pieces)
+    first = pltpu.make_async_copy(weights_hbm, weights, sems.at[len(copies)])
+    first.start()
+    for copy in copies[:ahead]:
+        copy.start()
+    first.wait()
+    for t, copy in enumerate(copies):
+        copy.wait()
+        if t + ahead < len(copies):
+            copies[t + ahead].start()
+        a, c = t // pieces, t % pieces
+
+        @pl.when(me >= 0)
+        def _():
+            d = lax.dot_general(
+                buffer[a * rows : (a + 1) * rows, c * columns : (c + 1) * columns],
+                weights[:, c * columns : (c + 1) * columns],
+                NT,
+                preferred_element_type=F32,
+            )
+            if c > 0:
+                d = d + acc[...]
+            if c < pieces - 1:
+                acc[...] = d
+            else:
+                out[:, a * rows : (a + 1) * rows] = d.T
+
+
+def stream_scratch(rows, proj_t, pieces):
+    return [
+        pltpu.VMEM((rows, proj_t.shape[1]), BF16),
+        pltpu.VMEM(proj_t.shape, BF16),
+        pltpu.VMEM((rows // ROW_STEPS, proj_t.shape[0]), F32),
+        pltpu.SemaphoreType.DMA((ROW_STEPS * pieces + 1,)),
+    ]
+
+
+def inputs_kernel(x_hbm, px_hbm, own, sent, x, px, acc, sems):
+    streamed(x_hbm, px_hbm, x, px, acc, own, sems, X_PIECES, X_AHEAD)
+    write_message(sent, own[...])
 
 
 def fold_in_kernel(own, arrived, total, sent):
@@ -101,18 +149,19 @@
             jax.ShapeDtypeStruct((rank, tokens), F32),
             jax.ShapeDtypeStruct((rank, tokens + LANES), jnp.int16),
         ],
-        in_specs=[VMEM] * 2,
+        in_specs=[ANY] * 2,
         out_specs=[VMEM] * 2,
-        compiler_params=SMALL,
-        cost_estimate=pl.CostEstimate(flops=20_000_000_000, bytes_accessed=4_000_000, transcendentals=0),
+        scratch_shapes=stream_scratch(tokens, proj_t, X_PIECES),
+        compiler_params=STREAM,
         name="inputs",
     )(inputs, proj_t)
 
 
-def grads_kernel(shares, g, pg, own, *rest):
-    outs, held = rest[:-1], rest[-1]
+def grads_kernel(shares, g_hbm, pg_hbm, own, *rest):
+    outs, (held, full, g, pg, acc, sems) = rest[: shares - 1], rest[shares - 1 :]
+    streamed(g_hbm, pg_hbm, g, pg, acc, full, sems, G_PIECES, G_AHEAD)
     me = lax.axis_index("tensor")
-    v = projected(g, pg)
+    v = full[...]
     rank, tokens = v.shape
     rows = rank // shares
     steps, e = coded(v)
@@ -135,10 +184,11 @@
         functools.partial(grads_kernel, shares),
         out_shape=[jax.ShapeDtypeStruct((rows, tokens), F32)]
         + [jax.ShapeDtypeStruct((rows, tokens + LANES), jnp.int16)] * (shares - 1),
-        in_specs=[VMEM] * 2,
+        in_specs=[ANY] * 2,
         out_specs=[VMEM] * shares,
-        scratch_shapes=[pltpu.VMEM((shares, rows, tokens), F32)],
-        compiler_params=SMALL,
+        scratch_shapes=[pltpu.VMEM((shares, rows, tokens), F32), pltpu.VMEM((rank, tokens), F32)]
+        + stream_scratch(tokens, proj_t, G_PIECES),
+        compiler_params=STREAM,
         name="grads",
     )(grads, proj_t)
 

time: 37.2 us -> 36.4 us (0.978)
  Pallas kernels: 7.43 us -> 12.5 us
  local copies, waits for them, and re-layouts: 4.49 us -> 0.01 us
  waiting for transfers between devices: 9.56 us -> 7.14 us
  starting transfers between devices: 15.5 us -> 16.6 us
    unnamed x12 -> x4, local copies, waits for them, and re-layouts: 4.49 us -> 0.01 us
    pallas_call x1, Pallas kernels: 4.06 us -> 7.14 us  [project_grads(): pl.pallas_call(functools.partial(grads_kernel, shares), out_shape=[jax.Sh...]
    ppermute x8, waiting for transfers between devices: 7.48 us -> 4.81 us  [swapped(): lax.ppermute(block, axis, [(i, i ^ flip) for i in range(lax.axis_size(axi...]
    pallas_call x1, Pallas kernels: 1.34 us -> 3.32 us  [project_inputs(): pl.pallas_call(inputs_kernel, out_shape=[jax.ShapeDtypeStruct((rank, toke...]
    ppermute x8, starting transfers between devices: 11.2 us -> 12.3 us  [swapped(): lax.ppermute(block, axis, [(i, i ^ flip) for i in range(lax.axis_size(axi...]
  transfers between devices with their start and end apart: 12 -> 12, of which waited for: 7 -> 6; matrix products, arithmetic and copies ran while one was open for 0% -> 0% of each run, Pallas kernels for 17% -> 32%
where the time goes in v5:
time: 36.4 us; the launch traced here: 36.3 us
  starting transfers between devices  16.6 us (46%)
  Pallas kernels  12.5 us (34%)
  waiting for transfers between devices  7.14 us (20%)
    ppermute x8, starting transfers between devices, swapped(): lax.ppermute(block, axis, [(i, i ^ flip) for i in range(lax.axis_size(axi...  12.3 us
    pallas_call x1, Pallas kernels, project_grads(): pl.pallas_call(functools.partial(grads_kernel, shares), out_shape=[jax.Sh...  7.14 us
    ppermute x8, waiting for transfers between devices, swapped(): lax.ppermute(block, axis, [(i, i ^ flip) for i in range(lax.axis_size(axi...  4.81 us
    ppermute x4, starting transfers between devices, crossed(): return lax.ppermute(block, ('docs', 'tensor'), pairs)  4.24 us
    pallas_call x1, Pallas kernels, project_inputs(): pl.pallas_call(inputs_kernel, out_shape=[jax.ShapeDtypeStruct((rank, toke...  3.32 us
    ppermute x4, waiting for transfers between devices, crossed(): return lax.ppermute(block, ('docs', 'tensor'), pairs)  2.33 us
  transfers between devices with their start and end apart: 12, of which 6 were waited for; matrix products, arithmetic and copies ran while one was open for 0% of the time, Pallas kernels for 32%

profile of v5, /device:TPU:0, one launch (start us, length us, event | category | flops | bytes accessed | tf_op | source)
XLA Modules:
  0.0 36.3 jit_solution(16761945581026077354)
XLA Ops:
  0.0 3.0 %collective-permute-start.6 = (bf16[512,1024]{1,0:T(8,128)(2,1)}, bf16[512,1024]{1,0:T(8,128)(2,1)S(1)}, u32[]{:S(2)}, u32[]{:S(2)}) collective-permute-start(bf16[512,1024]{1,0:T(8,128)(2,1)} %queries.1), channel_id=1, source_target_pairs={{0,8},{4,12},{8,0},{12,4},{1,9},{5,13},{9,1},{13,5},{2,10},{6,14},... | collective-permute-start | bytes 3145736 | tf_op jit(solution)/shard_map/ppermute | solution.py:26
  3.0 3.3 %inputs.1 = (f32[64,1024]{1,0:T(8,128)S(1)}, s16[64,1152]{1,0:T(8,128)(2,1)S(1)}) custom-call(bf16[1024,2048]{1,0:T(8,128)(2,1)} %x_hbm.1, bf16[64,2048]{1,0:T(8,128)(2,1)} %bitcast.3), custom_call_target="tpu_custom_call" | custom-call | tf_op jit(solution)/shard_map/inputs/pallas_call | solution.py:146
  6.3 2.7 %collective-permute-start = (s16[64,1152]{1,0:T(8,128)(2,1)S(1)}, s16[64,1152]{1,0:T(8,128)(2,1)S(1)}, u32[]{:S(2)}, u32[]{:S(2)}) collective-permute-start(s16[64,1152]{1,0:T(8,128)(2,1)S(1)} %get-tuple-element.22), channel_id=1, source_target_pairs={{0,2},{1,3},{2,0},{3,1},{4,6},{5,7},{6,4},{7,5},{8,10},{9,11},{10,... | collective-permute-start | bytes 442376 | tf_op jit(solution)/shard_map/ppermute | solution.py:26
  9.0 7.1 %grads.1 = (f32[16,1024]{1,0:T(8,128)S(1)}, s16[16,1152]{1,0:T(8,128)(2,1)S(1)}, s16[16,1152]{1,0:T(8,128)(2,1)S(1)}, s16[16,1152]{1,0:T(8,128)(2,1)S(1)}) custom-call(bf16[1024,7168]{1,0:T(8,128)(2,1)} %g_hbm.1, bf16[64,7168]{1,0:T(8,128)(2,1)} %bitcast.2), custom_call_target="tpu_custom_call" | custom-call | tf_op jit(solution)/shard_map/grads/pallas_call | solution.py:183
  16.1 0.0 collective-permute-done.arrived
  16.1 0.1 fold_in.1
  16.2 1.6 %collective-permute-start.1 = (s16[64,1152]{1,0:T(8,128)(2,1)S(1)}, s16[64,1152]{1,0:T(8,128)(2,1)S(1)}, u32[]{:S(2)}, u32[]{:S(2)}) collective-permute-start(s16[64,1152]{1,0:T(8,128)(2,1)S(1)} %get-tuple-element.26), channel_id=1, source_target_pairs={{0,1},{1,0},{2,3},{3,2},{4,5},{5,4},{6,7},{7,6},{8,9},{9,8},{10,11... | collective-permute-start | bytes 442376 | tf_op jit(solution)/shard_map/ppermute | solution.py:26
  17.9 1.6 %collective-permute-start.2 = (s16[16,1152]{1,0:T(8,128)(2,1)S(1)}, s16[16,1152]{1,0:T(8,128)(2,1)S(1)}, u32[]{:S(2)}, u32[]{:S(2)}) collective-permute-start(s16[16,1152]{1,0:T(8,128)(2,1)S(1)} %get-tuple-element.28), channel_id=1, source_target_pairs={{0,3},{1,2},{2,1},{3,0},{4,7},{5,6},{6,5},{7,4},{8,11},{9,10},{10,... | collective-permute-start | bytes 110600 | tf_op jit(solution)/shard_map/ppermute | solution.py:26
  19.5 0.5 %collective-permute-start.3 = (s16[16,1152]{1,0:T(8,128)(2,1)S(1)}, s16[16,1152]{1,0:T(8,128)(2,1)S(1)}, u32[]{:S(2)}, u32[]{:S(2)}) collective-permute-start(s16[16,1152]{1,0:T(8,128)(2,1)S(1)} %get-tuple-element.29), channel_id=1, source_target_pairs={{0,2},{1,3},{2,0},{3,1},{4,6},{5,7},{6,4},{7,5},{8,10},{9,11},{10,... | collective-permute-start | bytes 110600 | tf_op jit(solution)/shard_map/ppermute | solution.py:26
  20.0 2.3 %collective-permute-start.4 = (s16[16,1152]{1,0:T(8,128)(2,1)S(1)}, s16[16,1152]{1,0:T(8,128)(2,1)S(1)}, u32[]{:S(2)}, u32[]{:S(2)}) collective-permute-start(s16[16,1152]{1,0:T(8,128)(2,1)S(1)} %get-tuple-element.30), channel_id=1, source_target_pairs={{0,1},{1,0},{2,3},{3,2},{4,5},{5,4},{6,7},{7,6},{8,9},{9,8},{10,11... | collective-permute-start | bytes 110600 | tf_op jit(solution)/shard_map/ppermute | solution.py:26
  22.3 2.6 %collective-permute-done.2.refs_0_ = s16[16,1152]{1,0:T(8,128)(2,1)S(1)} collective-permute-done((s16[16,1152]{1,0:T(8,128)(2,1)S(1)}, s16[16,1152]{1,0:T(8,128)(2,1)S(1)}, u32[]{:S(2)}, u32[]{:S(2)}) %collective-permute-start.2) | collective-permute-done | bytes 36896 | tf_op jit(solution)/shard_map/ppermute | solution.py:26
  24.9 0.2 collective-permute-done.3.refs_1_
  25.1 0.0 collective-permute-done.4.refs_2_
  25.1 0.0 collective-permute-done.1.x_sent
  25.1 0.0 copy-done.1
  25.1 0.5 %train.1.mine = bf16[16,512]{1,0:T(8,128)(2,1)S(1)} custom-call(s32[1,1024]{1,0:T(1,128)S(1)} %copy-done.1, f32[64,1024]{1,0:T(8,128)S(1)} %get-tuple-element.25.x_own, s16[64,1152]{1,0:T(8,128)(2,1)S(1)} %collective-permute-done.1.x_sent, f32[16,1024]{1,0:T(8,128)S(1)} %get-tuple-element.27.g_own, s16[16,1152]{1,0:T(8,128)(2,1)S(1)} %collective-permute-done.2.refs_0_, ...), custom_call_target="tpu_custom_call" | custom-call | tf_op jit(solution)/shard_map/train/pallas_call | solution.py:218
  25.6 0.1 collective-permute-start.5
  25.7 1.2 %collective-permute-done.5.sibling = bf16[16,512]{1,0:T(8,128)(2,1)S(1)} collective-permute-done((bf16[16,512]{1,0:T(8,128)(2,1)S(1)}, bf16[16,512]{1,0:T(8,128)(2,1)S(1)}, u32[]{:S(2)}, u32[]{:S(2)}) %collective-permute-start.5) | collective-permute-done | bytes 16416 | tf_op jit(solution)/shard_map/ppermute | solution.py:26
  26.9 0.4 %near.1 = f32[16,512]{1,0:T(8,128)S(1)} custom-call(bf16[16,512]{1,0:T(8,128)(2,1)S(1)} %train.1.mine, bf16[16,512]{1,0:T(8,128)(2,1)S(1)} %collective-permute-done.5.sibling, bf16[512,1024]{1,0:T(8,128)(2,1)S(1)} %copy-done), custom_call_target="tpu_custom_call" | custom-call | tf_op jit(solution)/shard_map/near/pallas_call | solution.py:255
  27.2 0.0 collective-permute-done.6.refs_0_
  27.2 0.4 %score.1 = (f32[32,128]{1,0:T(8,128)S(1)}, f32[32,128]{1,0:T(8,128)S(1)}, f32[32,128]{1,0:T(8,128)S(1)}, f32[32,128]{1,0:T(8,128)S(1)}) custom-call(bf16[16,512]{1,0:T(8,128)(2,1)S(1)} %train.1.mine, bf16[16,512]{1,0:T(8,128)(2,1)S(1)} %collective-permute-done.5.sibling, f32[16,512]{1,0:T(8,128)S(1)} %near.1, ...), custom_call_target="tpu_custom_call" | custom-call | tf_op jit(solution)/shard_map/score/pallas_call | solution.py:264
  27.6 2.3 %collective-permute-start.7 = (f32[32,128]{1,0:T(8,128)S(1)}, f32[32,128]{1,0:T(8,128)S(1)}, u32[]{:S(2)}, u32[]{:S(2)}) collective-permute-start(f32[32,128]{1,0:T(8,128)S(1)} %get-tuple-element.31), channel_id=1, source_target_pairs={{0,7},{1,6},{2,5},{3,4},{4,3},{5,2},{6,1},{7,0},{8,15},{9,14},{10,... | collective-permute-start | bytes 49160 | tf_op jit(solution)/shard_map/ppermute | solution.py:32
  29.9 0.1 collective-permute-start.8
  30.0 1.6 %collective-permute-start.9 = (f32[32,128]{1,0:T(8,128)S(1)}, f32[32,128]{1,0:T(8,128)S(1)}, u32[]{:S(2)}, u32[]{:S(2)}) collective-permute-start(f32[32,128]{1,0:T(8,128)S(1)} %get-tuple-element.33), channel_id=1, source_target_pairs={{0,5},{1,4},{2,7},{3,6},{4,1},{5,0},{6,3},{7,2},{8,13},{9,12},{10,... | collective-permute-start | bytes 49160 | tf_op jit(solution)/shard_map/ppermute | solution.py:32
  31.5 0.3 collective-permute-start.10
  31.9 0.7 %collective-permute-done.7.refs_0_ = f32[32,128]{1,0:T(8,128)S(1)} collective-permute-done((f32[32,128]{1,0:T(8,128)S(1)}, f32[32,128]{1,0:T(8,128)S(1)}, u32[]{:S(2)}, u32[]{:S(2)}) %collective-permute-start.7) | collective-permute-done | bytes 16416 | tf_op jit(solution)/shard_map/ppermute | solution.py:32
  32.6 1.6 %collective-permute-done.8.refs_1_ = f32[32,128]{1,0:T(8,128)S(1)} collective-permute-done((f32[32,128]{1,0:T(8,128)S(1)}, f32[32,128]{1,0:T(8,128)S(1)}, u32[]{:S(2)}, u32[]{:S(2)}) %collective-permute-start.8) | collective-permute-done | bytes 16416 | tf_op jit(solution)/shard_map/ppermute | solution.py:32
  34.2 0.0 collective-permute-done.9.refs_2_
  34.2 0.0 collective-permute-done.10.refs_3_
  34.2 0.6 %collective-permute-start.11 = (f32[2,8,128]{2,1,0:T(8,128)S(1)}, f32[2,8,128]{2,1,0:T(8,128)S(1)}, u32[]{:S(2)}, u32[]{:S(2)}) collective-permute-start(f32[2,8,128]{2,1,0:T(8,128)S(1)} %get-tuple-element.36), channel_id=1, source_target_pairs={{0,4},{4,0},{8,12},{12,8},{1,5},{5,1},{9,13},{13,9},{2,6},{6,2},{1... | collective-permute-start | bytes 24584 | tf_op jit(solution)/shard_map/ppermute | solution.py:26
  34.8 0.8 %collective-permute-done.11.far = f32[2,8,128]{2,1,0:T(8,128)S(1)} collective-permute-done((f32[2,8,128]{2,1,0:T(8,128)S(1)}, f32[2,8,128]{2,1,0:T(8,128)S(1)}, u32[]{:S(2)}, u32[]{:S(2)}) %collective-permute-start.11) | collective-permute-done | bytes 8224 | tf_op jit(solution)/shard_map/ppermute | solution.py:26
  35.7 0.6 %place.1 = f32[8,4,128]{2,1,0:T(4,128)} custom-call(f32[2,8,128]{2,1,0:T(8,128)S(1)} %get-tuple-element.35.near, f32[2,8,128]{2,1,0:T(8,128)S(1)} %collective-permute-done.11.far), custom_call_target="tpu_custom_call" | custom-call | tf_op jit(solution)/shard_map/place/pallas_call | solution.py:306
  (4 shorter events, 0.0 us)
Async XLA Ops:
  0.0 26.9 %copy-start = (bf16[512,1024]{1,0:T(8,128)(2,1)S(1)}, bf16[512,1024]{1,0:T(8,128)(2,1)}, u32[]{:S(2)}) copy-start(bf16[512,1024]{1,0:T(8,128)(2,1)} %queries.1) | copy-start | bytes 3145732
  0.0 25.1 %copy-start.1 = (s32[1,1024]{1,0:T(1,128)S(1)}, s32[1,1024]{1,0:T(1,128)}, u32[]{:S(2)}) copy-start(s32[1,1024]{1,0:T(1,128)} %ids.1) | copy-start | bytes 12292
  0.0 27.2 %collective-permute-start.6 = (bf16[512,1024]{1,0:T(8,128)(2,1)}, bf16[512,1024]{1,0:T(8,128)(2,1)S(1)}, u32[]{:S(2)}, u32[]{:S(2)}) collective-permute-start(bf16[512,1024]{1,0:T(8,128)(2,1)} %queries.1), channel_id=1, source_target_pairs={{0,8},{4,12},{8,0},{12,4},{1,9},{5,13},{9,1},{13,5},{2,10},{6,14},... | collective-permute-start | bytes 3145736 | tf_op jit(solution)/shard_map/ppermute | solution.py:26
  6.3 9.8 %collective-permute-start = (s16[64,1152]{1,0:T(8,128)(2,1)S(1)}, s16[64,1152]{1,0:T(8,128)(2,1)S(1)}, u32[]{:S(2)}, u32[]{:S(2)}) collective-permute-start(s16[64,1152]{1,0:T(8,128)(2,1)S(1)} %get-tuple-element.22), channel_id=1, source_target_pairs={{0,2},{1,3},{2,0},{3,1},{4,6},{5,7},{6,4},{7,5},{8,10},{9,11},{10,... | collective-permute-start | bytes 442376 | tf_op jit(solution)/shard_map/ppermute | solution.py:26
  16.2 8.8 %collective-permute-start.1 = (s16[64,1152]{1,0:T(8,128)(2,1)S(1)}, s16[64,1152]{1,0:T(8,128)(2,1)S(1)}, u32[]{:S(2)}, u32[]{:S(2)}) collective-permute-start(s16[64,1152]{1,0:T(8,128)(2,1)S(1)} %get-tuple-element.26), channel_id=1, source_target_pairs={{0,1},{1,0},{2,3},{3,2},{4,5},{5,4},{6,7},{7,6},{8,9},{9,8},{10,11... | collective-permute-start | bytes 442376 | tf_op jit(solution)/shard_map/ppermute | solution.py:26
  17.9 7.0 %collective-permute-start.2 = (s16[16,1152]{1,0:T(8,128)(2,1)S(1)}, s16[16,1152]{1,0:T(8,128)(2,1)S(1)}, u32[]{:S(2)}, u32[]{:S(2)}) collective-permute-start(s16[16,1152]{1,0:T(8,128)(2,1)S(1)} %get-tuple-element.28), channel_id=1, source_target_pairs={{0,3},{1,2},{2,1},{3,0},{4,7},{5,6},{6,5},{7,4},{8,11},{9,10},{10,... | collective-permute-start | bytes 110600 | tf_op jit(solution)/shard_map/ppermute | solution.py:26
  19.5 5.6 %collective-permute-start.3 = (s16[16,1152]{1,0:T(8,128)(2,1)S(1)}, s16[16,1152]{1,0:T(8,128)(2,1)S(1)}, u32[]{:S(2)}, u32[]{:S(2)}) collective-permute-start(s16[16,1152]{1,0:T(8,128)(2,1)S(1)} %get-tuple-element.29), channel_id=1, source_target_pairs={{0,2},{1,3},{2,0},{3,1},{4,6},{5,7},{6,4},{7,5},{8,10},{9,11},{10,... | collective-permute-start | bytes 110600 | tf_op jit(solution)/shard_map/ppermute | solution.py:26
  20.0 5.1 %collective-permute-start.4 = (s16[16,1152]{1,0:T(8,128)(2,1)S(1)}, s16[16,1152]{1,0:T(8,128)(2,1)S(1)}, u32[]{:S(2)}, u32[]{:S(2)}) collective-permute-start(s16[16,1152]{1,0:T(8,128)(2,1)S(1)} %get-tuple-element.30), channel_id=1, source_target_pairs={{0,1},{1,0},{2,3},{3,2},{4,5},{5,4},{6,7},{7,6},{8,9},{9,8},{10,11... | collective-permute-start | bytes 110600 | tf_op jit(solution)/shard_map/ppermute | solution.py:26
  25.6 1.2 %collective-permute-start.5 = (bf16[16,512]{1,0:T(8,128)(2,1)S(1)}, bf16[16,512]{1,0:T(8,128)(2,1)S(1)}, u32[]{:S(2)}, u32[]{:S(2)}) collective-permute-start(bf16[16,512]{1,0:T(8,128)(2,1)S(1)} %train.1.mine), channel_id=1, source_target_pairs={{0,4},{4,0},{8,12},{12,8},{1,5},{5,1},{9,13},{13,9},{2,6},{6,2},{1... | collective-permute-start | bytes 49160 | tf_op jit(solution)/shard_map/ppermute | solution.py:26
  27.6 5.0 %collective-permute-start.7 = (f32[32,128]{1,0:T(8,128)S(1)}, f32[32,128]{1,0:T(8,128)S(1)}, u32[]{:S(2)}, u32[]{:S(2)}) collective-permute-start(f32[32,128]{1,0:T(8,128)S(1)} %get-tuple-element.31), channel_id=1, source_target_pairs={{0,7},{1,6},{2,5},{3,4},{4,3},{5,2},{6,1},{7,0},{8,15},{9,14},{10,... | collective-permute-start | bytes 49160 | tf_op jit(solution)/shard_map/ppermute | solution.py:32
  29.9 4.3 %collective-permute-start.8 = (f32[32,128]{1,0:T(8,128)S(1)}, f32[32,128]{1,0:T(8,128)S(1)}, u32[]{:S(2)}, u32[]{:S(2)}) collective-permute-start(f32[32,128]{1,0:T(8,128)S(1)} %get-tuple-element.32), channel_id=1, source_target_pairs={{0,6},{1,7},{2,4},{3,5},{4,2},{5,3},{6,0},{7,1},{8,14},{9,15},{10,... | collective-permute-start | bytes 49160 | tf_op jit(solution)/shard_map/ppermute | solution.py:32
  30.0 4.2 %collective-permute-start.9 = (f32[32,128]{1,0:T(8,128)S(1)}, f32[32,128]{1,0:T(8,128)S(1)}, u32[]{:S(2)}, u32[]{:S(2)}) collective-permute-start(f32[32,128]{1,0:T(8,128)S(1)} %get-tuple-element.33), channel_id=1, source_target_pairs={{0,5},{1,4},{2,7},{3,6},{4,1},{5,0},{6,3},{7,2},{8,13},{9,12},{10,... | collective-permute-start | bytes 49160 | tf_op jit(solution)/shard_map/ppermute | solution.py:32
  31.5 2.7 %collective-permute-start.10 = (f32[32,128]{1,0:T(8,128)S(1)}, f32[32,128]{1,0:T(8,128)S(1)}, u32[]{:S(2)}, u32[]{:S(2)}) collective-permute-start(f32[32,128]{1,0:T(8,128)S(1)} %get-tuple-element.34), channel_id=1, source_target_pairs={{0,4},{1,5},{2,6},{3,7},{4,0},{5,1},{6,2},{7,3},{8,12},{9,13},{10,... | collective-permute-start | bytes 49160 | tf_op jit(solution)/shard_map/ppermute | solution.py:32
  34.2 1.4 %collective-permute-start.11 = (f32[2,8,128]{2,1,0:T(8,128)S(1)}, f32[2,8,128]{2,1,0:T(8,128)S(1)}, u32[]{:S(2)}, u32[]{:S(2)}) collective-permute-start(f32[2,8,128]{2,1,0:T(8,128)S(1)} %get-tuple-element.36), channel_id=1, source_target_pairs={{0,4},{4,0},{8,12},{12,8},{1,5},{5,1},{9,13},{13,9},{2,6},{6,2},{1... | collective-permute-start | bytes 24584 | tf_op jit(solution)/shard_map/ppermute | solution.py:26

commit v6 on v5

--- a/solution.py
+++ b/solution.py
@@ -53,17 +53,18 @@
 
 def write_message(sent, v):
     steps, e = coded(v)
-    tokens = v.shape[1]
-    sent[:, :tokens] = steps.astype(jnp.int16)
+    rows, tokens = v.shape
     tail = folded(e)
-    blank = jnp.zeros((v.shape[0] - tail.shape[0], LANES), jnp.int32)
-    sent[:, tokens:] = jnp.concatenate([tail, blank], axis=0).astype(jnp.int16)
-
-
-def read_message(sent):
+    if rows > tail.shape[0]:
+        tail = jnp.concatenate([tail, jnp.zeros((rows - tail.shape[0], LANES), jnp.int32)], axis=0)
+    sent[:rows, :tokens] = steps.astype(jnp.int16)
+    sent[:rows, tokens:] = tail.astype(jnp.int16)
+
+
+def read_message(sent, first, rows):
     tokens = sent.shape[1] - LANES
-    tail = sent[:, tokens:].astype(jnp.int32)
-    return decoded(sent[:, :tokens], unfolded(tail[: tokens // LANES]))
+    tail = sent[first : first + rows, tokens:].astype(jnp.int32)
+    return decoded(sent[first : first + rows, :tokens], unfolded(tail[: tokens // LANES]))
 
 
 def stream_copies(hbm, buffer, sems, pieces):
@@ -79,7 +80,7 @@
     ]
 
 
-def streamed(hbm, weights_hbm, buffer, weights, acc, out, sems, pieces, ahead):
+def streamed(hbm, weights_hbm, buffer, weights, acc, out, sems, pieces, ahead, between=None):
     me = lax.axis_index("tensor")
     rows, columns = buffer.shape[0] // ROW_STEPS, buffer.shape[1] // pieces
     copies = stream_copies(hbm, buffer, sems, pieces)
@@ -87,11 +88,15 @@
     first.start()
     for copy in copies[:ahead]:
         copy.start()
+    if between:
+        between(-1)
     first.wait()
     for t, copy in enumerate(copies):
         copy.wait()
         if t + ahead < len(copies):
             copies[t + ahead].start()
+        if between:
+            between(t)
         a, c = t // pieces, t % pieces
 
         @pl.when(me >= 0)
@@ -119,13 +124,35 @@
     ]
 
 
-def inputs_kernel(x_hbm, px_hbm, own, sent, x, px, acc, sems):
-    streamed(x_hbm, px_hbm, x, px, acc, own, sems, X_PIECES, X_AHEAD)
+def inputs_kernel(flips, x_hbm, px_hbm, queries, own, sent, early, late, x, px, acc, sems, staged, cuts):
+    me = lax.axis_index("tensor")
+    width = late.shape[0]
+    staging = pltpu.make_async_copy(queries, staged, cuts.at[len(flips) + 1])
+    pieces = [
+        pltpu.make_async_copy(
+            staged.at[pl.ds(pl.multiple_of((me ^ k) * width, width), width)],
+            early.at[pl.ds(i * width, width)] if k else late,
+            cuts.at[i],
+        )
+        for i, k in enumerate(flips + [0])
+    ]
+
+    def hand_on(step):
+        if step < 0:
+            staging.start()
+        if step == 2:
+            staging.wait()
+            for piece in pieces:
+                piece.start()
+
+    streamed(x_hbm, px_hbm, x, px, acc, own, sems, X_PIECES, X_AHEAD, hand_on)
     write_message(sent, own[...])
+    for piece in pieces:
+        piece.wait()
 
 
 def fold_in_kernel(own, arrived, total, sent):
-    v = own[...] + read_message(arrived)
+    v = own[...] + read_message(arrived, 0, own.shape[0])
     total[...] = v
     write_message(sent, v)
 
@@ -137,24 +164,29 @@
         in_specs=[VMEM] * 2,
         out_specs=[VMEM] * 2,
         compiler_params=SMALL,
+        cost_estimate=pl.CostEstimate(flops=20_000_000_000, bytes_accessed=0, transcendentals=0),
         name="fold_in",
     )(own, arrived)
 
 
-def project_inputs(inputs, proj_t):
+def project_inputs(inputs, proj_t, queries, flips):
     rank, tokens = proj_t.shape[0], inputs.shape[0]
-    return pl.pallas_call(
-        inputs_kernel,
+    rows, width = queries.shape[0] // (len(flips) + 1), queries.shape[1]
+    return pl.pallas_call(
+        functools.partial(inputs_kernel, flips),
         out_shape=[
             jax.ShapeDtypeStruct((rank, tokens), F32),
             jax.ShapeDtypeStruct((rank, tokens + LANES), jnp.int16),
+            jax.ShapeDtypeStruct((rows * len(flips), width), BF16),
+            jax.ShapeDtypeStruct((rows, width), BF16),
         ],
-        in_specs=[ANY] * 2,
-        out_specs=[VMEM] * 2,
-        scratch_shapes=stream_scratch(tokens, proj_t, X_PIECES),
+        in_specs=[ANY] * 3,
+        out_specs=[VMEM] * 2 + [ANY] * 2,
+        scratch_shapes=stream_scratch(tokens, proj_t, X_PIECES)
+        + [pltpu.VMEM(queries.shape, BF16), pltpu.SemaphoreType.DMA((len(flips) + 2,))],
         compiler_params=STREAM,
         name="inputs",
-    )(inputs, proj_t)
+    )(inputs, proj_t, queries)
 
 
 def grads_kernel(shares, g_hbm, pg_hbm, own, *rest):
@@ -188,17 +220,18 @@
         out_specs=[VMEM] * shares,
         scratch_shapes=[pltpu.VMEM((shares, rows, tokens), F32), pltpu.VMEM((rank, tokens), F32)]
         + stream_scratch(tokens, proj_t, G_PIECES),
-        compiler_params=STREAM,
+        compiler_params=pltpu.CompilerParams(vmem_limit_bytes=int(53.5 * 2**20)),
         name="grads",
     )(grads, proj_t)
 
 
-def train_kernel(ids, x_own, x_sent, g_own, *refs):
+def train_kernel(ids, x_own, g_own, x_sent, *refs):
     g_sent, out = refs[:-1], refs[-1]
-    x, g = x_own[...] + read_message(x_sent), g_own[...]
+    rank, rows = x_own.shape[0], g_own.shape[0]
+    x, g = x_own[...] + read_message(x_sent, 0, rank), g_own[...]
     for sent in g_sent:
-        g = g + read_message(sent)
-    rows, tokens = g.shape
+        g = g + read_message(sent, 0, rows)
+    tokens = g.shape[1]
     mask = ids[...] == lax.broadcasted_iota(jnp.int32, (DOC_DEV, tokens), 0)
     counts = jnp.sum(mask.astype(F32), axis=1, keepdims=True)
     picked = jnp.concatenate([jnp.where(mask, g[i : i + 1], 0.0) for i in range(rows)], axis=0)
@@ -213,7 +246,7 @@
     out[...] = jnp.concatenate([train[:, :half], train[:, half:]], axis=0).astype(BF16)
 
 
-def mean_gradients(ids, x_own, x_sent, g_own, g_sent):
+def mean_gradients(ids, x_own, g_own, x_sent, g_sent):
     width = g_own.shape[0] * x_own.shape[0]
     return pl.pallas_call(
         train_kernel,
@@ -222,7 +255,7 @@
         out_specs=VMEM,
         compiler_params=SMALL,
         name="train",
-    )(ids, x_own, x_sent, g_own, *g_sent)
+    )(ids, x_own, g_own, x_sent, *g_sent)
 
 
 def scores_of(trains, queries):
@@ -235,102 +268,119 @@
 
 
 def near_kernel(mine, sibling, queries, out):
-    out[...] = scores_of((mine, sibling), queries)
-
-
-def score_kernel(shares, mine, sibling, near, *refs):
-    blocks, outs, held = refs[: -shares - 1], refs[-shares - 1 : -1], refs[-1]
-    me = lax.axis_index("tensor")
-    count, width = near.shape[0], near.shape[1] // shares
-    for m in range(len(blocks) + 1):
-        scores = scores_of((mine, sibling), blocks[m - 1]) if m else near[...]
-        for j in range(shares):
-            held[j, m * count : (m + 1) * count, :] = scores[:, j * width : (j + 1) * width]
-    for k in range(shares):
-        outs[k][...] = held[me ^ k]
-
-
-def score(mine, sibling, blocks, shares):
-    rows, width = 2 * DOC_DEV, blocks[0].shape[0]
-    near = pl.pallas_call(
+    width = out.shape[2]
+    scores = scores_of((mine, sibling), queries)
+    for j in range(out.shape[0]):
+        out[j] = scores[:, j * width : (j + 1) * width]
+
+
+def near_scores(mine, sibling, queries, shares):
+    return pl.pallas_call(
         near_kernel,
-        out_shape=jax.ShapeDtypeStruct((rows, width), F32),
+        out_shape=jax.ShapeDtypeStruct((shares, 2 * DOC_DEV, queries.shape[0] // shares), F32),
         in_specs=[VMEM] * 3,
         out_specs=VMEM,
         compiler_params=SMALL,
+        cost_estimate=pl.CostEstimate(flops=3_000_000_000, bytes_accessed=0, transcendentals=0),
         name="near",
-    )(mine, sibling, blocks[0])
-    shape = (rows * len(blocks), width // shares)
-    return pl.pallas_call(
-        functools.partial(score_kernel, shares),
-        out_shape=[jax.ShapeDtypeStruct(shape, F32)] * shares,
-        in_specs=[VMEM] * (2 + len(blocks)),
-        out_specs=[VMEM] * shares,
-        scratch_shapes=[pltpu.VMEM((shares, *shape), F32)],
+    )(mine, sibling, queries)
+
+
+def score_kernel(flips, mine, sibling, near, *refs):
+    blocks, outs = refs[: -len(flips)], refs[-len(flips) :]
+    me = lax.axis_index("tensor")
+    _, count, width = near.shape
+    for i, k in enumerate(flips):
+        outs[i][:count, :] = near[me ^ k]
+    for m, queries in enumerate(blocks, 1):
+        scores = scores_of((mine, sibling), queries)
+        for i in range(len(flips)):
+            outs[i][m * count : (m + 1) * count, :] = scores[:, i * width : (i + 1) * width]
+
+
+def score(mine, sibling, near, blocks, flips):
+    _, count, width = near.shape
+    return pl.pallas_call(
+        functools.partial(score_kernel, flips),
+        out_shape=[jax.ShapeDtypeStruct((count * (1 + len(blocks)), width), F32)] * len(flips),
+        in_specs=[VMEM] * (3 + len(blocks)),
+        out_specs=[VMEM] * len(flips),
         compiler_params=SMALL,
         name="score",
-    )(mine, sibling, near, *blocks[1:])
-
-
-def add_kernel(shares, *refs):
-    parts, outs = refs[:shares], refs[shares:]
+    )(mine, sibling, near, *blocks)
+
+
+def add_kernel(chips, mine, sibling, near, *refs):
+    blocks, parts, (kept_own, kept_sum, given) = refs[: chips - 1], refs[chips - 1 : -3], refs[-3:]
+    me = lax.axis_index("tensor")
     total = parts[0][...]
     for part in parts[1:]:
         total = total + part[...]
-    both = total.reshape(-1, 2, DOC_DEV, total.shape[1])
-    for core, out in enumerate(outs):
-        out[...] = both[:, 1 - core]
-
-
-def add(parts):
-    rows, width = parts[0].shape
-    return pl.pallas_call(
-        functools.partial(add_kernel, len(parts)),
-        out_shape=[jax.ShapeDtypeStruct((rows // (2 * DOC_DEV), DOC_DEV, width), F32)] * 2,
-        in_specs=[VMEM] * len(parts),
-        out_specs=[VMEM] * 2,
+    own = jnp.concatenate([near[me]] + [scores_of((mine, sibling), queries) for queries in blocks], axis=0)
+    own = own.reshape(chips, 2, DOC_DEV, total.shape[1])
+    summed = total.reshape(chips, 2, DOC_DEV, total.shape[1])
+    kept_own[...] = own[:, 0]
+    kept_sum[...] = summed[:, 1]
+    given[0] = own[:, 1]
+    given[1] = summed[:, 0]
+
+
+def add(mine, sibling, near, blocks, parts):
+    chips, width = 1 + len(blocks), near.shape[2]
+    shape = (chips, DOC_DEV, width)
+    return pl.pallas_call(
+        functools.partial(add_kernel, chips),
+        out_shape=[jax.ShapeDtypeStruct(s, F32) for s in (shape, shape, (2, *shape))],
+        in_specs=[VMEM] * (3 + len(blocks) + len(parts)),
+        out_specs=[VMEM] * 3,
         compiler_params=SMALL,
         name="add",
-    )(*parts)
-
-
-def place_kernel(near, far, out):
+    )(mine, sibling, near, *blocks, *parts)
+
+
+def place_kernel(kept_own, kept_sum, taken, out):
     me = lax.axis_index("docs")
-    for m in range(near.shape[0]):
-        out[:, pl.ds(me ^ (2 * m + 1), 1), :] = near[m][:, None, :]
-        out[:, pl.ds(me ^ (2 * m), 1), :] = far[m][:, None, :]
-
-
-def place(near, far):
-    chips, docs, width = near.shape
+    for m in range(kept_own.shape[0]):
+        out[:, pl.ds(me ^ (2 * m), 1), :] = (kept_own[m] + taken[1, m])[:, None, :]
+        out[:, pl.ds(me ^ (2 * m + 1), 1), :] = (kept_sum[m] + taken[0, m])[:, None, :]
+
+
+def place(kept_own, kept_sum, taken):
+    chips, docs, width = kept_own.shape
     return pl.pallas_call(
         place_kernel,
         out_shape=jax.ShapeDtypeStruct((docs, 2 * chips, width), F32),
-        in_specs=[VMEM] * 2,
+        in_specs=[VMEM] * 3,
         out_specs=VMEM,
         compiler_params=SMALL,
         name="place",
-    )(near, far)
+    )(kept_own, kept_sum, taken)
 
 
 def per_device(inputs, grads, proj_in, proj_out, queries, ids):
     shares, ndev = lax.axis_size("tensor"), lax.axis_size("docs")
-    blocks = [queries] + [swapped(queries, "docs", 2 * m) for m in range(1, ndev // 2)]
+    chips = range(1, ndev // 2)
     flips = list(range(shares - 1, 0, -1))
-    x, x_sent = project_inputs(inputs, proj_in.T)
+    x, x_coded, early, late = project_inputs(inputs, proj_in.T, queries, flips)
     flip = shares // 2
-    x_sent = swapped(x_sent, "tensor", flip)
+    x_sent = swapped(x_coded, "tensor", flip)
+    early = [swapped(early, "docs", 2 * m) for m in chips]
     g_own, *g_coded = project_grads(grads, proj_out.T, shares)
     x_sent, g_own = lax.optimization_barrier((x_sent, g_own))
+    g_sent = [swapped(g, "tensor", k) for k, g in zip(flips, g_coded)]
     while flip > 1:
         flip //= 2
         x, x_sent = fold_in(x, x_sent)
         x_sent = swapped(x_sent, "tensor", flip)
-    g_sent = [swapped(g, "tensor", k) for k, g in zip(flips, g_coded)]
-    train = mean_gradients(ids, x, x_sent, g_own, g_sent)
-    scores = score(train, swapped(train, "docs", 1), blocks, shares)
-    mine, sibling = add([crossed(scores[k], 1, k) for k in flips + [0]])
-    return place(mine, swapped(sibling, "docs", 1))
+    mine = mean_gradients(ids, x, g_own, x_sent, g_sent)
+    late, mine = lax.optimization_barrier((late, mine))
+    late = [swapped(late, "docs", 2 * m) for m in chips]
+    sibling = swapped(mine, "docs", 1)
+    near = near_scores(mine, sibling, queries, shares)
+    scores = score(mine, sibling, near, early, flips)
+    arrived = [crossed(s, 1, k) for k, s in zip(flips, scores)]
+    kept_own, kept_sum, given = add(mine, sibling, near, late, arrived)
+    return place(kept_own, kept_sum, swapped(given, "docs", 1))
 
 
 def solution(mesh):

time: 36.4 us -> 36.1 us (level)
  waiting for transfers between devices: 7.14 us -> 5.85 us
  Pallas kernels: 12.5 us -> 12.9 us
  starting transfers between devices: 16.6 us -> 17 us
    ppermute x4 -> x3, waiting for transfers between devices: 2.33 us -> 0.01 us  [crossed(): return lax.ppermute(block, ('docs', 'tensor'), pairs)]
    ppermute x8 -> x9, waiting for transfers between devices: 4.81 us -> 5.84 us  [swapped(): lax.ppermute(block, axis, [(i, i ^ flip) for i in range(lax.axis_size(axi...]
    ppermute x8 -> x9, starting transfers between devices: 12.3 us -> 13.3 us  [swapped(): lax.ppermute(block, axis, [(i, i ^ flip) for i in range(lax.axis_size(axi...]
    ppermute x4 -> x3, starting transfers between devices: 4.24 us -> 3.79 us  [crossed(): return lax.ppermute(block, ('docs', 'tensor'), pairs)]
    pallas_call x4, Pallas kernels: 4.09 us -> 4.52 us  [the longest x1 3.68 us: project_inputs(): pl.pallas_call(functools.partial(inputs_kernel, flips), out_shape=[jax.Sh...]
  transfers between devices with their start and end apart: 12 -> 12, of which waited for: 6 -> 5; matrix products, arithmetic and copies ran while one was open for 0% -> 0% of each run, Pallas kernels for 32% -> 24%
where the time goes in v6:
time: 36.1 us; the launch traced here: 35.9 us
  starting transfers between devices  17 us (47%)
  Pallas kernels  12.9 us (36%)
  waiting for transfers between devices  5.85 us (16%)
    ppermute x9, starting transfers between devices, swapped(): lax.ppermute(block, axis, [(i, i ^ flip) for i in range(lax.axis_size(axi...  13.3 us
    pallas_call x1, Pallas kernels, project_grads(): pl.pallas_call(functools.partial(grads_kernel, shares), out_shape=[jax.Sh...  7.15 us
    ppermute x9, waiting for transfers between devices, swapped(): lax.ppermute(block, axis, [(i, i ^ flip) for i in range(lax.axis_size(axi...  5.84 us
    ppermute x3, starting transfers between devices, crossed(): return lax.ppermute(block, ('docs', 'tensor'), pairs)  3.79 us
    pallas_call x1, Pallas kernels, project_inputs(): pl.pallas_call(functools.partial(inputs_kernel, flips), out_shape=[jax.Sh...  3.68 us
  transfers between devices with their start and end apart: 12, of which 5 were waited for; matrix products, arithmetic and copies ran while one was open for 0% of the time, Pallas kernels for 24%

profile of v6, /device:TPU:0, one launch (start us, length us, event | category | flops | bytes accessed | tf_op | source)
XLA Modules:
  0.0 35.9 jit_solution(12840212359166842572)
XLA Ops:
  0.0 3.7 %inputs.1 = (f32[64,1024]{1,0:T(8,128)S(1)}, s16[64,1152]{1,0:T(8,128)(2,1)S(1)}, bf16[384,1024]{1,0:T(8,128)(2,1)}, bf16[128,1024]{1,0:T(8,128)(2,1)}) custom-call(bf16[1024,2048]{1,0:T(8,128)(2,1)} %x_hbm.1, bf16[64,2048]{1,0:T(8,128)(2,1)} %bitcast.3, bf16[512,1024]{1,0:T(8,128)(2,1)} %queries.3), custom_call_target="tpu_custom_call" | custom-call | tf_op jit(solution)/shard_map/inputs/pallas_call | solution.py:175
  3.7 4.1 %collective-permute-start = (s16[64,1152]{1,0:T(8,128)(2,1)S(1)}, s16[64,1152]{1,0:T(8,128)(2,1)S(1)}, u32[]{:S(2)}, u32[]{:S(2)}) collective-permute-start(s16[64,1152]{1,0:T(8,128)(2,1)S(1)} %get-tuple-element.27), channel_id=1, source_target_pairs={{0,2},{1,3},{2,0},{3,1},{4,6},{5,7},{6,4},{7,5},{8,10},{9,11},{10,... | collective-permute-start | bytes 442376 | tf_op jit(solution)/shard_map/ppermute | solution.py:26
  7.8 1.5 %collective-permute-start.7 = (bf16[384,1024]{1,0:T(8,128)(2,1)}, bf16[384,1024]{1,0:T(8,128)(2,1)S(1)}, u32[]{:S(2)}, u32[]{:S(2)}) collective-permute-start(bf16[384,1024]{1,0:T(8,128)(2,1)} %get-tuple-element.38), channel_id=1, source_target_pairs={{0,8},{4,12},{8,0},{12,4},{1,9},{5,13},{9,1},{13,5},{2,10},{6,14},... | collective-permute-start | bytes 2359304 | tf_op jit(solution)/shard_map/ppermute | solution.py:26
  9.3 7.1 %grads.1 = (f32[16,1024]{1,0:T(8,128)S(1)}, s16[16,1152]{1,0:T(8,128)(2,1)S(1)}, s16[16,1152]{1,0:T(8,128)(2,1)S(1)}, s16[16,1152]{1,0:T(8,128)(2,1)S(1)}) custom-call(bf16[1024,7168]{1,0:T(8,128)(2,1)} %g_hbm.1, bf16[64,7168]{1,0:T(8,128)(2,1)} %bitcast.2), custom_call_target="tpu_custom_call" | custom-call | tf_op jit(solution)/shard_map/grads/pallas_call | solution.py:215
  16.5 0.0 collective-permute-done.arrived
  16.5 0.0 copy-start.1
  16.5 0.0 copy-start
  16.5 0.1 fold_in.1
  16.6 1.6 %collective-permute-start.1 = (s16[64,1152]{1,0:T(8,128)(2,1)S(1)}, s16[64,1152]{1,0:T(8,128)(2,1)S(1)}, u32[]{:S(2)}, u32[]{:S(2)}) collective-permute-start(s16[64,1152]{1,0:T(8,128)(2,1)S(1)} %get-tuple-element.32), channel_id=1, source_target_pairs={{0,1},{1,0},{2,3},{3,2},{4,5},{5,4},{6,7},{7,6},{8,9},{9,8},{10,11... | collective-permute-start | bytes 442376 | tf_op jit(solution)/shard_map/ppermute | solution.py:26
  18.3 0.3 collective-permute-start.2
  18.6 1.6 %collective-permute-start.3 = (s16[16,1152]{1,0:T(8,128)(2,1)S(1)}, s16[16,1152]{1,0:T(8,128)(2,1)S(1)}, u32[]{:S(2)}, u32[]{:S(2)}) collective-permute-start(s16[16,1152]{1,0:T(8,128)(2,1)S(1)} %get-tuple-element.34), channel_id=1, source_target_pairs={{0,2},{1,3},{2,0},{3,1},{4,6},{5,7},{6,4},{7,5},{8,10},{9,11},{10,... | collective-permute-start | bytes 110600 | tf_op jit(solution)/shard_map/ppermute | solution.py:26
  20.2 2.5 %collective-permute-start.4 = (s16[16,1152]{1,0:T(8,128)(2,1)S(1)}, s16[16,1152]{1,0:T(8,128)(2,1)S(1)}, u32[]{:S(2)}, u32[]{:S(2)}) collective-permute-start(s16[16,1152]{1,0:T(8,128)(2,1)S(1)} %get-tuple-element.35), channel_id=1, source_target_pairs={{0,1},{1,0},{2,3},{3,2},{4,5},{5,4},{6,7},{7,6},{8,9},{9,8},{10,11... | collective-permute-start | bytes 110600 | tf_op jit(solution)/shard_map/ppermute | solution.py:26
  22.7 1.5 %collective-permute-done.2.refs_0_ = s16[16,1152]{1,0:T(8,128)(2,1)S(1)} collective-permute-done((s16[16,1152]{1,0:T(8,128)(2,1)S(1)}, s16[16,1152]{1,0:T(8,128)(2,1)S(1)}, u32[]{:S(2)}, u32[]{:S(2)}) %collective-permute-start.2) | collective-permute-done | bytes 36896 | tf_op jit(solution)/shard_map/ppermute | solution.py:26
  24.1 0.0 collective-permute-done.3.refs_1_
  24.1 0.5 %collective-permute-done.4.refs_2_ = s16[16,1152]{1,0:T(8,128)(2,1)S(1)} collective-permute-done((s16[16,1152]{1,0:T(8,128)(2,1)S(1)}, s16[16,1152]{1,0:T(8,128)(2,1)S(1)}, u32[]{:S(2)}, u32[]{:S(2)}) %collective-permute-start.4) | collective-permute-done | bytes 36896 | tf_op jit(solution)/shard_map/ppermute | solution.py:26
  24.6 0.0 collective-permute-done.1.x_sent
  24.6 0.5 %train.1.mine = bf16[16,512]{1,0:T(8,128)(2,1)S(1)} custom-call(s32[1,1024]{1,0:T(1,128)S(1)} %copy-done.1, f32[64,1024]{1,0:T(8,128)S(1)} %get-tuple-element.30.x_own, f32[16,1024]{1,0:T(8,128)S(1)} %get-tuple-element.31.g_own, s16[64,1152]{1,0:T(8,128)(2,1)S(1)} %collective-permute-done.1.x_sent, s16[16,1152]{1,0:T(8,128)(2,1)S(1)} %collective-permute-done.2.refs_0_, ...), custom_call_target="tpu_custom_call" | custom-call | tf_op jit(solution)/shard_map/train/pallas_call | solution.py:251
  25.1 0.1 collective-permute-start.5
  25.2 1.3 %collective-permute-start.6 = (bf16[128,1024]{1,0:T(8,128)(2,1)S(1)}, bf16[128,1024]{1,0:T(8,128)(2,1)S(1)}, u32[]{:S(2)}, u32[]{:S(2)}) collective-permute-start(bf16[128,1024]{1,0:T(8,128)(2,1)S(1)} %copy-done.2), channel_id=1, source_target_pairs={{0,8},{4,12},{8,0},{12,4},{1,9},{5,13},{9,1},{13,5},{2,10},{6,14},... | collective-permute-start | bytes 786440 | tf_op jit(solution)/shard_map/ppermute | solution.py:26
  26.5 0.0 collective-permute-done.5.sibling
  26.5 0.4 %near.1 = f32[4,16,128]{2,1,0:T(8,128)S(1)} custom-call(bf16[16,512]{1,0:T(8,128)(2,1)S(1)} %train.1.mine, bf16[16,512]{1,0:T(8,128)(2,1)S(1)} %collective-permute-done.5.sibling, bf16[512,1024]{1,0:T(8,128)(2,1)S(1)} %copy-done), custom_call_target="tpu_custom_call" | custom-call | flops 3000000000 | tf_op jit(solution)/shard_map/near/pallas_call | solution.py:278
  26.9 0.1 collective-permute-done.7.refs_0_
  27.0 0.3 score.1
  27.3 2.4 %collective-permute-start.8 = (f32[32,128]{1,0:T(8,128)S(1)}, f32[32,128]{1,0:T(8,128)S(1)}, u32[]{:S(2)}, u32[]{:S(2)}) collective-permute-start(f32[32,128]{1,0:T(8,128)S(1)} %get-tuple-element.39), channel_id=1, source_target_pairs={{0,7},{1,6},{2,5},{3,4},{4,3},{5,2},{6,1},{7,0},{8,15},{9,14},{10,... | collective-permute-start | bytes 49160 | tf_op jit(solution)/shard_map/ppermute | solution.py:32
  29.7 0.6 %collective-permute-start.9 = (f32[32,128]{1,0:T(8,128)S(1)}, f32[32,128]{1,0:T(8,128)S(1)}, u32[]{:S(2)}, u32[]{:S(2)}) collective-permute-start(f32[32,128]{1,0:T(8,128)S(1)} %get-tuple-element.40), channel_id=1, source_target_pairs={{0,6},{1,7},{2,4},{3,5},{4,2},{5,3},{6,0},{7,1},{8,14},{9,15},{10,... | collective-permute-start | bytes 49160 | tf_op jit(solution)/shard_map/ppermute | solution.py:32
  30.3 0.8 %collective-permute-start.10 = (f32[32,128]{1,0:T(8,128)S(1)}, f32[32,128]{1,0:T(8,128)S(1)}, u32[]{:S(2)}, u32[]{:S(2)}) collective-permute-start(f32[32,128]{1,0:T(8,128)S(1)} %get-tuple-element.41), channel_id=1, source_target_pairs={{0,5},{1,4},{2,7},{3,6},{4,1},{5,0},{6,3},{7,2},{8,13},{9,12},{10,... | collective-permute-start | bytes 49160 | tf_op jit(solution)/shard_map/ppermute | solution.py:32
  31.1 2.8 %collective-permute-done.6.refs_0_ = bf16[128,1024]{1,0:T(8,128)(2,1)S(1)} collective-permute-done((bf16[128,1024]{1,0:T(8,128)(2,1)S(1)}, bf16[128,1024]{1,0:T(8,128)(2,1)S(1)}, u32[]{:S(2)}, u32[]{:S(2)}) %collective-permute-start.6) | collective-permute-done | bytes 262176 | tf_op jit(solution)/shard_map/ppermute | solution.py:26
  33.9 0.0 collective-permute-done.8.refs_1_
  33.9 0.2 add.1
  34.1 0.2 collective-permute-start.11
  34.3 1.0 %collective-permute-done.11.taken = f32[2,2,8,128]{3,2,1,0:T(8,128)S(1)} collective-permute-done((f32[2,2,8,128]{3,2,1,0:T(8,128)S(1)}, f32[2,2,8,128]{3,2,1,0:T(8,128)S(1)}, u32[]{:S(2)}, u32[]{:S(2)}) %collective-permute-start.11) | collective-permute-done | bytes 16416 | tf_op jit(solution)/shard_map/ppermute | solution.py:26
  35.3 0.6 %place.1 = f32[8,4,128]{2,1,0:T(4,128)} custom-call(f32[2,8,128]{2,1,0:T(8,128)S(1)} %get-tuple-element.42.kept_own, f32[2,8,128]{2,1,0:T(8,128)S(1)} %get-tuple-element.43.kept_sum, f32[2,2,8,128]{3,2,1,0:T(8,128)S(1)} %collective-permute-done.11.taken), custom_call_target="tpu_custom_call" | custom-call | tf_op jit(solution)/shard_map/place/pallas_call | solution.py:350
  (6 shorter events, 0.0 us)
Async XLA Ops:
  3.7 12.8 %collective-permute-start = (s16[64,1152]{1,0:T(8,128)(2,1)S(1)}, s16[64,1152]{1,0:T(8,128)(2,1)S(1)}, u32[]{:S(2)}, u32[]{:S(2)}) collective-permute-start(s16[64,1152]{1,0:T(8,128)(2,1)S(1)} %get-tuple-element.27), channel_id=1, source_target_pairs={{0,2},{1,3},{2,0},{3,1},{4,6},{5,7},{6,4},{7,5},{8,10},{9,11},{10,... | collective-permute-start | bytes 442376 | tf_op jit(solution)/shard_map/ppermute | solution.py:26
  7.8 19.2 %collective-permute-start.7 = (bf16[384,1024]{1,0:T(8,128)(2,1)}, bf16[384,1024]{1,0:T(8,128)(2,1)S(1)}, u32[]{:S(2)}, u32[]{:S(2)}) collective-permute-start(bf16[384,1024]{1,0:T(8,128)(2,1)} %get-tuple-element.38), channel_id=1, source_target_pairs={{0,8},{4,12},{8,0},{12,4},{1,9},{5,13},{9,1},{13,5},{2,10},{6,14},... | collective-permute-start | bytes 2359304 | tf_op jit(solution)/shard_map/ppermute | solution.py:26
  16.5 8.1 %copy-start.1 = (s32[1,1024]{1,0:T(1,128)S(1)}, s32[1,1024]{1,0:T(1,128)}, u32[]{:S(2)}) copy-start(s32[1,1024]{1,0:T(1,128)} %ids.1) | copy-start | bytes 12292
  16.5 8.7 %copy-start.2 = (bf16[128,1024]{1,0:T(8,128)(2,1)S(1)}, bf16[128,1024]{1,0:T(8,128)(2,1)}, u32[]{:S(2)}) copy-start(bf16[128,1024]{1,0:T(8,128)(2,1)} %get-tuple-element.37) | copy-start | bytes 786436
  16.5 10.0 %copy-start = (bf16[512,1024]{1,0:T(8,128)(2,1)S(1)}, bf16[512,1024]{1,0:T(8,128)(2,1)}, u32[]{:S(2)}) copy-start(bf16[512,1024]{1,0:T(8,128)(2,1)} %queries.3) | copy-start | bytes 3145732
  16.6 8.0 %collective-permute-start.1 = (s16[64,1152]{1,0:T(8,128)(2,1)S(1)}, s16[64,1152]{1,0:T(8,128)(2,1)S(1)}, u32[]{:S(2)}, u32[]{:S(2)}) collective-permute-start(s16[64,1152]{1,0:T(8,128)(2,1)S(1)} %get-tuple-element.32), channel_id=1, source_target_pairs={{0,1},{1,0},{2,3},{3,2},{4,5},{5,4},{6,7},{7,6},{8,9},{9,8},{10,11... | collective-permute-start | bytes 442376 | tf_op jit(solution)/shard_map/ppermute | solution.py:26
  18.3 5.9 %collective-permute-start.2 = (s16[16,1152]{1,0:T(8,128)(2,1)S(1)}, s16[16,1152]{1,0:T(8,128)(2,1)S(1)}, u32[]{:S(2)}, u32[]{:S(2)}) collective-permute-start(s16[16,1152]{1,0:T(8,128)(2,1)S(1)} %get-tuple-element.33), channel_id=1, source_target_pairs={{0,3},{1,2},{2,1},{3,0},{4,7},{5,6},{6,5},{7,4},{8,11},{9,10},{10,... | collective-permute-start | bytes 110600 | tf_op jit(solution)/shard_map/ppermute | solution.py:26
  18.6 5.5 %collective-permute-start.3 = (s16[16,1152]{1,0:T(8,128)(2,1)S(1)}, s16[16,1152]{1,0:T(8,128)(2,1)S(1)}, u32[]{:S(2)}, u32[]{:S(2)}) collective-permute-start(s16[16,1152]{1,0:T(8,128)(2,1)S(1)} %get-tuple-element.34), channel_id=1, source_target_pairs={{0,2},{1,3},{2,0},{3,1},{4,6},{5,7},{6,4},{7,5},{8,10},{9,11},{10,... | collective-permute-start | bytes 110600 | tf_op jit(solution)/shard_map/ppermute | solution.py:26
  20.2 4.4 %collective-permute-start.4 = (s16[16,1152]{1,0:T(8,128)(2,1)S(1)}, s16[16,1152]{1,0:T(8,128)(2,1)S(1)}, u32[]{:S(2)}, u32[]{:S(2)}) collective-permute-start(s16[16,1152]{1,0:T(8,128)(2,1)S(1)} %get-tuple-element.35), channel_id=1, source_target_pairs={{0,1},{1,0},{2,3},{3,2},{4,5},{5,4},{6,7},{7,6},{8,9},{9,8},{10,11... | collective-permute-start | bytes 110600 | tf_op jit(solution)/shard_map/ppermute | solution.py:26
  25.1 1.4 %collective-permute-start.5 = (bf16[16,512]{1,0:T(8,128)(2,1)S(1)}, bf16[16,512]{1,0:T(8,128)(2,1)S(1)}, u32[]{:S(2)}, u32[]{:S(2)}) collective-permute-start(bf16[16,512]{1,0:T(8,128)(2,1)S(1)} %train.1.mine), channel_id=1, source_target_pairs={{0,4},{4,0},{8,12},{12,8},{1,5},{5,1},{9,13},{13,9},{2,6},{6,2},{1... | collective-permute-start | bytes 49160 | tf_op jit(solution)/shard_map/ppermute | solution.py:26
  25.2 8.7 %collective-permute-start.6 = (bf16[128,1024]{1,0:T(8,128)(2,1)S(1)}, bf16[128,1024]{1,0:T(8,128)(2,1)S(1)}, u32[]{:S(2)}, u32[]{:S(2)}) collective-permute-start(bf16[128,1024]{1,0:T(8,128)(2,1)S(1)} %copy-done.2), channel_id=1, source_target_pairs={{0,8},{4,12},{8,0},{12,4},{1,9},{5,13},{9,1},{13,5},{2,10},{6,14},... | collective-permute-start | bytes 786440 | tf_op jit(solution)/shard_map/ppermute | solution.py:26
  27.3 6.6 %collective-permute-start.8 = (f32[32,128]{1,0:T(8,128)S(1)}, f32[32,128]{1,0:T(8,128)S(1)}, u32[]{:S(2)}, u32[]{:S(2)}) collective-permute-start(f32[32,128]{1,0:T(8,128)S(1)} %get-tuple-element.39), channel_id=1, source_target_pairs={{0,7},{1,6},{2,5},{3,4},{4,3},{5,2},{6,1},{7,0},{8,15},{9,14},{10,... | collective-permute-start | bytes 49160 | tf_op jit(solution)/shard_map/ppermute | solution.py:32
  29.7 4.2 %collective-permute-start.9 = (f32[32,128]{1,0:T(8,128)S(1)}, f32[32,128]{1,0:T(8,128)S(1)}, u32[]{:S(2)}, u32[]{:S(2)}) collective-permute-start(f32[32,128]{1,0:T(8,128)S(1)} %get-tuple-element.40), channel_id=1, source_target_pairs={{0,6},{1,7},{2,4},{3,5},{4,2},{5,3},{6,0},{7,1},{8,14},{9,15},{10,... | collective-permute-start | bytes 49160 | tf_op jit(solution)/shard_map/ppermute | solution.py:32
  30.3 3.6 %collective-permute-start.10 = (f32[32,128]{1,0:T(8,128)S(1)}, f32[32,128]{1,0:T(8,128)S(1)}, u32[]{:S(2)}, u32[]{:S(2)}) collective-permute-start(f32[32,128]{1,0:T(8,128)S(1)} %get-tuple-element.41), channel_id=1, source_target_pairs={{0,5},{1,4},{2,7},{3,6},{4,1},{5,0},{6,3},{7,2},{8,13},{9,12},{10,... | collective-permute-start | bytes 49160 | tf_op jit(solution)/shard_map/ppermute | solution.py:32
  34.1 1.2 %collective-permute-start.11 = (f32[2,2,8,128]{3,2,1,0:T(8,128)S(1)}, f32[2,2,8,128]{3,2,1,0:T(8,128)S(1)}, u32[]{:S(2)}, u32[]{:S(2)}) collective-permute-start(f32[2,2,8,128]{3,2,1,0:T(8,128)S(1)} %get-tuple-element.44), channel_id=1, source_target_pairs={{0,4},{4,0},{8,12},{12,8},{1,5},{5,1},{9,13},{13,9},{2,6},{6,2},{1... | collective-permute-start | bytes 49160 | tf_op jit(solution)/shard_map/ppermute | solution.py:26

commit v7 on v6

--- a/solution.py
+++ b/solution.py
@@ -17,8 +17,9 @@
 SMALL = pltpu.CompilerParams(vmem_limit_bytes=8 * 2**20)
 STEPS = 32000.0
 LANES = 128
+MESSAGE_ROWS = 16
 ROW_STEPS = 4
-X_PIECES, X_AHEAD = 1, 4
+X_PIECES, X_AHEAD = 1, 3
 G_PIECES, G_AHEAD = 1, 2
 
 
@@ -53,18 +54,19 @@
 
 def write_message(sent, v):
     steps, e = coded(v)
-    rows, tokens = v.shape
+    height, tokens = sent.shape[0], v.shape[1]
+    for i, at in enumerate(range(0, v.shape[0], height)):
+        sent[:, i * tokens : (i + 1) * tokens] = steps[at : at + height].astype(jnp.int16)
     tail = folded(e)
-    if rows > tail.shape[0]:
-        tail = jnp.concatenate([tail, jnp.zeros((rows - tail.shape[0], LANES), jnp.int32)], axis=0)
-    sent[:rows, :tokens] = steps.astype(jnp.int16)
-    sent[:rows, tokens:] = tail.astype(jnp.int16)
-
-
-def read_message(sent, first, rows):
-    tokens = sent.shape[1] - LANES
-    tail = sent[first : first + rows, tokens:].astype(jnp.int32)
-    return decoded(sent[first : first + rows, :tokens], unfolded(tail[: tokens // LANES]))
+    if height > tail.shape[0]:
+        tail = jnp.concatenate([tail, jnp.zeros((height - tail.shape[0], LANES), jnp.int32)], axis=0)
+    sent[:, sent.shape[1] - LANES :] = tail.astype(jnp.int16)
+
+
+def read_message(sent, tokens):
+    last = sent.shape[1] - LANES
+    steps = jnp.concatenate([sent[:, at : at + tokens] for at in range(0, last, tokens)], axis=0)
+    return decoded(steps, unfolded(sent[:, last:].astype(jnp.int32)[: tokens // LANES]))
 
 
 def stream_copies(hbm, buffer, sems, pieces):
@@ -152,7 +154,7 @@
 
 
 def fold_in_kernel(own, arrived, total, sent):
-    v = own[...] + read_message(arrived, 0, own.shape[0])
+    v = own[...] + read_message(arrived, own.shape[1])
     total[...] = v
     write_message(sent, v)
 
@@ -176,7 +178,7 @@
         functools.partial(inputs_kernel, flips),
         out_shape=[
             jax.ShapeDtypeStruct((rank, tokens), F32),
-            jax.ShapeDtypeStruct((rank, tokens + LANES), jnp.int16),
+            jax.ShapeDtypeStruct((MESSAGE_ROWS, rank // MESSAGE_ROWS * tokens + LANES), jnp.int16),
             jax.ShapeDtypeStruct((rows * len(flips), width), BF16),
             jax.ShapeDtypeStruct((rows, width), BF16),
         ],
@@ -228,9 +230,9 @@
 def train_kernel(ids, x_own, g_own, x_sent, *refs):
     g_sent, out = refs[:-1], refs[-1]
     rank, rows = x_own.shape[0], g_own.shape[0]
-    x, g = x_own[...] + read_message(x_sent, 0, rank), g_own[...]
+    x, g = x_own[...] + read_message(x_sent, g_own.shape[1]), g_own[...]
     for sent in g_sent:
-        g = g + read_message(sent, 0, rows)
+        g = g + read_message(sent, g_own.shape[1])
     tokens = g.shape[1]
     mask = ids[...] == lax.broadcasted_iota(jnp.int32, (DOC_DEV, tokens), 0)
     counts = jnp.sum(mask.astype(F32), axis=1, keepdims=True)

time: 36.1 us -> 35.8 us (level)
  waiting for transfers between devices: 5.85 us -> 6.79 us
  starting transfers between devices: 17 us -> 16.1 us
    ppermute x9, waiting for transfers between devices: 5.84 us -> 6.78 us  [swapped(): lax.ppermute(block, axis, [(i, i ^ flip) for i in range(lax.axis_size(axi...]
    ppermute x9, starting transfers between devices: 13.3 us -> 12.5 us  [swapped(): lax.ppermute(block, axis, [(i, i ^ flip) for i in range(lax.axis_size(axi...]
  transfers between devices with their start and end apart: 12 -> 12, of which waited for: 5 -> 6; matrix products, arithmetic and copies ran while one was open for 0% -> 0% of each run, Pallas kernels for 24% -> 24%
where the time goes in v7:
time: 35.8 us; the launch traced here: 35.7 us
  starting transfers between devices  16.1 us (45%)
  Pallas kernels  12.7 us (35%)
  waiting for transfers between devices  6.79 us (19%)
    ppermute x9, starting transfers between devices, swapped(): lax.ppermute(block, axis, [(i, i ^ flip) for i in range(lax.axis_size(axi...  12.5 us
    pallas_call x1, Pallas kernels, project_grads(): pl.pallas_call(functools.partial(grads_kernel, shares), out_shape=[jax.Sh...  7.14 us
    ppermute x9, waiting for transfers between devices, swapped(): lax.ppermute(block, axis, [(i, i ^ flip) for i in range(lax.axis_size(axi...  6.78 us
    ppermute x3, starting transfers between devices, crossed(): return lax.ppermute(block, ('docs', 'tensor'), pairs)  3.66 us
    pallas_call x1, Pallas kernels, project_inputs(): pl.pallas_call(functools.partial(inputs_kernel, flips), out_shape=[jax.Sh...  3.42 us
  transfers between devices with their start and end apart: 12, of which 6 were waited for; matrix products, arithmetic and copies ran while one was open for 0% of the time, Pallas kernels for 24%

profile of v7, /device:TPU:0, one launch (start us, length us, event | category | flops | bytes accessed | tf_op | source)
XLA Modules:
  0.0 35.7 jit_solution(3443446412409325071)
XLA Ops:
  0.0 3.4 %inputs.1 = (f32[64,1024]{1,0:T(8,128)S(1)}, s16[16,4224]{1,0:T(8,128)(2,1)S(1)}, bf16[384,1024]{1,0:T(8,128)(2,1)}, bf16[128,1024]{1,0:T(8,128)(2,1)}) custom-call(bf16[1024,2048]{1,0:T(8,128)(2,1)} %x_hbm.1, bf16[64,2048]{1,0:T(8,128)(2,1)} %bitcast.3, bf16[512,1024]{1,0:T(8,128)(2,1)} %queries.3), custom_call_target="tpu_custom_call" | custom-call | tf_op jit(solution)/shard_map/inputs/pallas_call | solution.py:177
  3.4 4.1 %collective-permute-start = (s16[16,4224]{1,0:T(8,128)(2,1)S(1)}, s16[16,4224]{1,0:T(8,128)(2,1)S(1)}, u32[]{:S(2)}, u32[]{:S(2)}) collective-permute-start(s16[16,4224]{1,0:T(8,128)(2,1)S(1)} %get-tuple-element.27), channel_id=1, source_target_pairs={{0,2},{1,3},{2,0},{3,1},{4,6},{5,7},{6,4},{7,5},{8,10},{9,11},{10,... | collective-permute-start | bytes 405512 | tf_op jit(solution)/shard_map/ppermute | solution.py:27
  7.5 1.5 %collective-permute-start.7 = (bf16[384,1024]{1,0:T(8,128)(2,1)}, bf16[384,1024]{1,0:T(8,128)(2,1)S(1)}, u32[]{:S(2)}, u32[]{:S(2)}) collective-permute-start(bf16[384,1024]{1,0:T(8,128)(2,1)} %get-tuple-element.38), channel_id=1, source_target_pairs={{0,8},{4,12},{8,0},{12,4},{1,9},{5,13},{9,1},{13,5},{2,10},{6,14},... | collective-permute-start | bytes 2359304 | tf_op jit(solution)/shard_map/ppermute | solution.py:27
  9.1 7.1 %grads.1 = (f32[16,1024]{1,0:T(8,128)S(1)}, s16[16,1152]{1,0:T(8,128)(2,1)S(1)}, s16[16,1152]{1,0:T(8,128)(2,1)S(1)}, s16[16,1152]{1,0:T(8,128)(2,1)S(1)}) custom-call(bf16[1024,7168]{1,0:T(8,128)(2,1)} %g_hbm.1, bf16[64,7168]{1,0:T(8,128)(2,1)} %bitcast.2), custom_call_target="tpu_custom_call" | custom-call | tf_op jit(solution)/shard_map/grads/pallas_call | solution.py:217
  16.2 0.0 collective-permute-done.arrived
  16.2 0.0 copy-start.1
  16.2 0.0 copy-start
  16.3 0.1 fold_in.1
  16.4 1.6 %collective-permute-start.1 = (s16[16,4224]{1,0:T(8,128)(2,1)S(1)}, s16[16,4224]{1,0:T(8,128)(2,1)S(1)}, u32[]{:S(2)}, u32[]{:S(2)}) collective-permute-start(s16[16,4224]{1,0:T(8,128)(2,1)S(1)} %get-tuple-element.32), channel_id=1, source_target_pairs={{0,1},{1,0},{2,3},{3,2},{4,5},{5,4},{6,7},{7,6},{8,9},{9,8},{10,11... | collective-permute-start | bytes 405512 | tf_op jit(solution)/shard_map/ppermute | solution.py:27
  18.0 0.2 collective-permute-start.2
  18.2 1.7 %collective-permute-start.3 = (s16[16,1152]{1,0:T(8,128)(2,1)S(1)}, s16[16,1152]{1,0:T(8,128)(2,1)S(1)}, u32[]{:S(2)}, u32[]{:S(2)}) collective-permute-start(s16[16,1152]{1,0:T(8,128)(2,1)S(1)} %get-tuple-element.34), channel_id=1, source_target_pairs={{0,2},{1,3},{2,0},{3,1},{4,6},{5,7},{6,4},{7,5},{8,10},{9,11},{10,... | collective-permute-start | bytes 110600 | tf_op jit(solution)/shard_map/ppermute | solution.py:27
  19.9 2.5 %collective-permute-start.4 = (s16[16,1152]{1,0:T(8,128)(2,1)S(1)}, s16[16,1152]{1,0:T(8,128)(2,1)S(1)}, u32[]{:S(2)}, u32[]{:S(2)}) collective-permute-start(s16[16,1152]{1,0:T(8,128)(2,1)S(1)} %get-tuple-element.35), channel_id=1, source_target_pairs={{0,1},{1,0},{2,3},{3,2},{4,5},{5,4},{6,7},{7,6},{8,9},{9,8},{10,11... | collective-permute-start | bytes 110600 | tf_op jit(solution)/shard_map/ppermute | solution.py:27
  22.4 1.4 %collective-permute-done.2.refs_0_ = s16[16,1152]{1,0:T(8,128)(2,1)S(1)} collective-permute-done((s16[16,1152]{1,0:T(8,128)(2,1)S(1)}, s16[16,1152]{1,0:T(8,128)(2,1)S(1)}, u32[]{:S(2)}, u32[]{:S(2)}) %collective-permute-start.2) | collective-permute-done | bytes 36896 | tf_op jit(solution)/shard_map/ppermute | solution.py:27
  23.8 0.0 collective-permute-done.3.refs_1_
  23.8 0.6 %collective-permute-done.4.refs_2_ = s16[16,1152]{1,0:T(8,128)(2,1)S(1)} collective-permute-done((s16[16,1152]{1,0:T(8,128)(2,1)S(1)}, s16[16,1152]{1,0:T(8,128)(2,1)S(1)}, u32[]{:S(2)}, u32[]{:S(2)}) %collective-permute-start.4) | collective-permute-done | bytes 36896 | tf_op jit(solution)/shard_map/ppermute | solution.py:27
  24.3 0.0 collective-permute-done.1.x_sent
  24.3 0.5 %train.1.mine = bf16[16,512]{1,0:T(8,128)(2,1)S(1)} custom-call(s32[1,1024]{1,0:T(1,128)S(1)} %copy-done.1, f32[64,1024]{1,0:T(8,128)S(1)} %get-tuple-element.30.x_own, f32[16,1024]{1,0:T(8,128)S(1)} %get-tuple-element.31.g_own, s16[16,4224]{1,0:T(8,128)(2,1)S(1)} %collective-permute-done.1.x_sent, s16[16,1152]{1,0:T(8,128)(2,1)S(1)} %collective-permute-done.2.refs_0_, ...), custom_call_target="tpu_custom_call" | custom-call | tf_op jit(solution)/shard_map/train/pallas_call | solution.py:253
  24.9 0.1 collective-permute-start.5
  25.0 0.7 %collective-permute-start.6 = (bf16[128,1024]{1,0:T(8,128)(2,1)S(1)}, bf16[128,1024]{1,0:T(8,128)(2,1)S(1)}, u32[]{:S(2)}, u32[]{:S(2)}) collective-permute-start(bf16[128,1024]{1,0:T(8,128)(2,1)S(1)} %copy-done.2), channel_id=1, source_target_pairs={{0,8},{4,12},{8,0},{12,4},{1,9},{5,13},{9,1},{13,5},{2,10},{6,14},... | collective-permute-start | bytes 786440 | tf_op jit(solution)/shard_map/ppermute | solution.py:27
  25.7 0.4 %collective-permute-done.5.sibling = bf16[16,512]{1,0:T(8,128)(2,1)S(1)} collective-permute-done((bf16[16,512]{1,0:T(8,128)(2,1)S(1)}, bf16[16,512]{1,0:T(8,128)(2,1)S(1)}, u32[]{:S(2)}, u32[]{:S(2)}) %collective-permute-start.5) | collective-permute-done | bytes 16416 | tf_op jit(solution)/shard_map/ppermute | solution.py:27
  26.1 0.4 %near.1 = f32[4,16,128]{2,1,0:T(8,128)S(1)} custom-call(bf16[16,512]{1,0:T(8,128)(2,1)S(1)} %train.1.mine, bf16[16,512]{1,0:T(8,128)(2,1)S(1)} %collective-permute-done.5.sibling, bf16[512,1024]{1,0:T(8,128)(2,1)S(1)} %copy-done), custom_call_target="tpu_custom_call" | custom-call | flops 3000000000 | tf_op jit(solution)/shard_map/near/pallas_call | solution.py:280
  26.5 0.3 collective-permute-done.7.refs_0_
  26.8 0.3 score.1
  27.1 2.2 %collective-permute-start.8 = (f32[32,128]{1,0:T(8,128)S(1)}, f32[32,128]{1,0:T(8,128)S(1)}, u32[]{:S(2)}, u32[]{:S(2)}) collective-permute-start(f32[32,128]{1,0:T(8,128)S(1)} %get-tuple-element.39), channel_id=1, source_target_pairs={{0,7},{1,6},{2,5},{3,4},{4,3},{5,2},{6,1},{7,0},{8,15},{9,14},{10,... | collective-permute-start | bytes 49160 | tf_op jit(solution)/shard_map/ppermute | solution.py:33
  29.2 0.8 %collective-permute-start.9 = (f32[32,128]{1,0:T(8,128)S(1)}, f32[32,128]{1,0:T(8,128)S(1)}, u32[]{:S(2)}, u32[]{:S(2)}) collective-permute-start(f32[32,128]{1,0:T(8,128)S(1)} %get-tuple-element.40), channel_id=1, source_target_pairs={{0,6},{1,7},{2,4},{3,5},{4,2},{5,3},{6,0},{7,1},{8,14},{9,15},{10,... | collective-permute-start | bytes 49160 | tf_op jit(solution)/shard_map/ppermute | solution.py:33
  30.0 0.7 %collective-permute-start.10 = (f32[32,128]{1,0:T(8,128)S(1)}, f32[32,128]{1,0:T(8,128)S(1)}, u32[]{:S(2)}, u32[]{:S(2)}) collective-permute-start(f32[32,128]{1,0:T(8,128)S(1)} %get-tuple-element.41), channel_id=1, source_target_pairs={{0,5},{1,4},{2,7},{3,6},{4,1},{5,0},{6,3},{7,2},{8,13},{9,12},{10,... | collective-permute-start | bytes 49160 | tf_op jit(solution)/shard_map/ppermute | solution.py:33
  30.7 3.0 %collective-permute-done.6.refs_0_ = bf16[128,1024]{1,0:T(8,128)(2,1)S(1)} collective-permute-done((bf16[128,1024]{1,0:T(8,128)(2,1)S(1)}, bf16[128,1024]{1,0:T(8,128)(2,1)S(1)}, u32[]{:S(2)}, u32[]{:S(2)}) %collective-permute-start.6) | collective-permute-done | bytes 262176 | tf_op jit(solution)/shard_map/ppermute | solution.py:27
  33.7 0.0 collective-permute-done.8.refs_1_
  33.7 0.2 add.1
  33.8 0.0 collective-permute-start.11
  33.8 1.2 %collective-permute-done.11.taken = f32[2,2,8,128]{3,2,1,0:T(8,128)S(1)} collective-permute-done((f32[2,2,8,128]{3,2,1,0:T(8,128)S(1)}, f32[2,2,8,128]{3,2,1,0:T(8,128)S(1)}, u32[]{:S(2)}, u32[]{:S(2)}) %collective-permute-start.11) | collective-permute-done | bytes 16416 | tf_op jit(solution)/shard_map/ppermute | solution.py:27
  35.1 0.6 %place.1 = f32[8,4,128]{2,1,0:T(4,128)} custom-call(f32[2,8,128]{2,1,0:T(8,128)S(1)} %get-tuple-element.42.kept_own, f32[2,8,128]{2,1,0:T(8,128)S(1)} %get-tuple-element.43.kept_sum, f32[2,2,8,128]{3,2,1,0:T(8,128)S(1)} %collective-permute-done.11.taken), custom_call_target="tpu_custom_call" | custom-call | tf_op jit(solution)/shard_map/place/pallas_call | solution.py:352
  (6 shorter events, 0.0 us)
Async XLA Ops:
  3.4 12.8 %collective-permute-start = (s16[16,4224]{1,0:T(8,128)(2,1)S(1)}, s16[16,4224]{1,0:T(8,128)(2,1)S(1)}, u32[]{:S(2)}, u32[]{:S(2)}) collective-permute-start(s16[16,4224]{1,0:T(8,128)(2,1)S(1)} %get-tuple-element.27), channel_id=1, source_target_pairs={{0,2},{1,3},{2,0},{3,1},{4,6},{5,7},{6,4},{7,5},{8,10},{9,11},{10,... | collective-permute-start | bytes 405512 | tf_op jit(solution)/shard_map/ppermute | solution.py:27
  7.5 19.2 %collective-permute-start.7 = (bf16[384,1024]{1,0:T(8,128)(2,1)}, bf16[384,1024]{1,0:T(8,128)(2,1)S(1)}, u32[]{:S(2)}, u32[]{:S(2)}) collective-permute-start(bf16[384,1024]{1,0:T(8,128)(2,1)} %get-tuple-element.38), channel_id=1, source_target_pairs={{0,8},{4,12},{8,0},{12,4},{1,9},{5,13},{9,1},{13,5},{2,10},{6,14},... | collective-permute-start | bytes 2359304 | tf_op jit(solution)/shard_map/ppermute | solution.py:27
  16.2 8.1 %copy-start.1 = (s32[1,1024]{1,0:T(1,128)S(1)}, s32[1,1024]{1,0:T(1,128)}, u32[]{:S(2)}) copy-start(s32[1,1024]{1,0:T(1,128)} %ids.1) | copy-start | bytes 12292
  16.2 8.7 %copy-start.2 = (bf16[128,1024]{1,0:T(8,128)(2,1)S(1)}, bf16[128,1024]{1,0:T(8,128)(2,1)}, u32[]{:S(2)}) copy-start(bf16[128,1024]{1,0:T(8,128)(2,1)} %get-tuple-element.37) | copy-start | bytes 786436
  16.2 9.9 %copy-start = (bf16[512,1024]{1,0:T(8,128)(2,1)S(1)}, bf16[512,1024]{1,0:T(8,128)(2,1)}, u32[]{:S(2)}) copy-start(bf16[512,1024]{1,0:T(8,128)(2,1)} %queries.3) | copy-start | bytes 3145732
  16.4 8.0 %collective-permute-start.1 = (s16[16,4224]{1,0:T(8,128)(2,1)S(1)}, s16[16,4224]{1,0:T(8,128)(2,1)S(1)}, u32[]{:S(2)}, u32[]{:S(2)}) collective-permute-start(s16[16,4224]{1,0:T(8,128)(2,1)S(1)} %get-tuple-element.32), channel_id=1, source_target_pairs={{0,1},{1,0},{2,3},{3,2},{4,5},{5,4},{6,7},{7,6},{8,9},{9,8},{10,11... | collective-permute-start | bytes 405512 | tf_op jit(solution)/shard_map/ppermute | solution.py:27
  18.0 5.8 %collective-permute-start.2 = (s16[16,1152]{1,0:T(8,128)(2,1)S(1)}, s16[16,1152]{1,0:T(8,128)(2,1)S(1)}, u32[]{:S(2)}, u32[]{:S(2)}) collective-permute-start(s16[16,1152]{1,0:T(8,128)(2,1)S(1)} %get-tuple-element.33), channel_id=1, source_target_pairs={{0,3},{1,2},{2,1},{3,0},{4,7},{5,6},{6,5},{7,4},{8,11},{9,10},{10,... | collective-permute-start | bytes 110600 | tf_op jit(solution)/shard_map/ppermute | solution.py:27
  18.2 5.5 %collective-permute-start.3 = (s16[16,1152]{1,0:T(8,128)(2,1)S(1)}, s16[16,1152]{1,0:T(8,128)(2,1)S(1)}, u32[]{:S(2)}, u32[]{:S(2)}) collective-permute-start(s16[16,1152]{1,0:T(8,128)(2,1)S(1)} %get-tuple-element.34), channel_id=1, source_target_pairs={{0,2},{1,3},{2,0},{3,1},{4,6},{5,7},{6,4},{7,5},{8,10},{9,11},{10,... | collective-permute-start | bytes 110600 | tf_op jit(solution)/shard_map/ppermute | solution.py:27
  19.9 4.4 %collective-permute-start.4 = (s16[16,1152]{1,0:T(8,128)(2,1)S(1)}, s16[16,1152]{1,0:T(8,128)(2,1)S(1)}, u32[]{:S(2)}, u32[]{:S(2)}) collective-permute-start(s16[16,1152]{1,0:T(8,128)(2,1)S(1)} %get-tuple-element.35), channel_id=1, source_target_pairs={{0,1},{1,0},{2,3},{3,2},{4,5},{5,4},{6,7},{7,6},{8,9},{9,8},{10,11... | collective-permute-start | bytes 110600 | tf_op jit(solution)/shard_map/ppermute | solution.py:27
  24.9 1.2 %collective-permute-start.5 = (bf16[16,512]{1,0:T(8,128)(2,1)S(1)}, bf16[16,512]{1,0:T(8,128)(2,1)S(1)}, u32[]{:S(2)}, u32[]{:S(2)}) collective-permute-start(bf16[16,512]{1,0:T(8,128)(2,1)S(1)} %train.1.mine), channel_id=1, source_target_pairs={{0,4},{4,0},{8,12},{12,8},{1,5},{5,1},{9,13},{13,9},{2,6},{6,2},{1... | collective-permute-start | bytes 49160 | tf_op jit(solution)/shard_map/ppermute | solution.py:27
  25.0 8.7 %collective-permute-start.6 = (bf16[128,1024]{1,0:T(8,128)(2,1)S(1)}, bf16[128,1024]{1,0:T(8,128)(2,1)S(1)}, u32[]{:S(2)}, u32[]{:S(2)}) collective-permute-start(bf16[128,1024]{1,0:T(8,128)(2,1)S(1)} %copy-done.2), channel_id=1, source_target_pairs={{0,8},{4,12},{8,0},{12,4},{1,9},{5,13},{9,1},{13,5},{2,10},{6,14},... | collective-permute-start | bytes 786440 | tf_op jit(solution)/shard_map/ppermute | solution.py:27
  27.1 6.6 %collective-permute-start.8 = (f32[32,128]{1,0:T(8,128)S(1)}, f32[32,128]{1,0:T(8,128)S(1)}, u32[]{:S(2)}, u32[]{:S(2)}) collective-permute-start(f32[32,128]{1,0:T(8,128)S(1)} %get-tuple-element.39), channel_id=1, source_target_pairs={{0,7},{1,6},{2,5},{3,4},{4,3},{5,2},{6,1},{7,0},{8,15},{9,14},{10,... | collective-permute-start | bytes 49160 | tf_op jit(solution)/shard_map/ppermute | solution.py:33
  29.2 4.5 %collective-permute-start.9 = (f32[32,128]{1,0:T(8,128)S(1)}, f32[32,128]{1,0:T(8,128)S(1)}, u32[]{:S(2)}, u32[]{:S(2)}) collective-permute-start(f32[32,128]{1,0:T(8,128)S(1)} %get-tuple-element.40), channel_id=1, source_target_pairs={{0,6},{1,7},{2,4},{3,5},{4,2},{5,3},{6,0},{7,1},{8,14},{9,15},{10,... | collective-permute-start | bytes 49160 | tf_op jit(solution)/shard_map/ppermute | solution.py:33
  30.0 3.6 %collective-permute-start.10 = (f32[32,128]{1,0:T(8,128)S(1)}, f32[32,128]{1,0:T(8,128)S(1)}, u32[]{:S(2)}, u32[]{:S(2)}) collective-permute-start(f32[32,128]{1,0:T(8,128)S(1)} %get-tuple-element.41), channel_id=1, source_target_pairs={{0,5},{1,4},{2,7},{3,6},{4,1},{5,0},{6,3},{7,2},{8,13},{9,12},{10,... | collective-permute-start | bytes 49160 | tf_op jit(solution)/shard_map/ppermute | solution.py:33
  33.8 1.2 %collective-permute-start.11 = (f32[2,2,8,128]{3,2,1,0:T(8,128)S(1)}, f32[2,2,8,128]{3,2,1,0:T(8,128)S(1)}, u32[]{:S(2)}, u32[]{:S(2)}) collective-permute-start(f32[2,2,8,128]{3,2,1,0:T(8,128)S(1)} %get-tuple-element.44), channel_id=1, source_target_pairs={{0,4},{4,0},{8,12},{12,8},{1,5},{5,1},{9,13},{13,9},{2,6},{6,2},{1... | collective-permute-start | bytes 49160 | tf_op jit(solution)/shard_map/ppermute | solution.py:27

commit v8 on v7

--- a/solution.py
+++ b/solution.py
@@ -20,7 +20,7 @@
 MESSAGE_ROWS = 16
 ROW_STEPS = 4
 X_PIECES, X_AHEAD = 1, 3
-G_PIECES, G_AHEAD = 1, 2
+G_PIECES, G_AHEAD = 1, 3
 
 
 def swapped(block, axis, flip):
@@ -266,78 +266,56 @@
         t = train[...].astype(F32)
         rows.append(jnp.concatenate([t[:DOC_DEV], t[DOC_DEV:]], axis=1))
     docs = jnp.concatenate(rows, axis=0).astype(BF16)
-    return lax.dot_general(docs, queries[...], NT, preferred_element_type=F32)
-
-
-def near_kernel(mine, sibling, queries, out):
-    width = out.shape[2]
-    scores = scores_of((mine, sibling), queries)
-    for j in range(out.shape[0]):
-        out[j] = scores[:, j * width : (j + 1) * width]
-
-
-def near_scores(mine, sibling, queries, shares):
-    return pl.pallas_call(
-        near_kernel,
-        out_shape=jax.ShapeDtypeStruct((shares, 2 * DOC_DEV, queries.shape[0] // shares), F32),
-        in_specs=[VMEM] * 3,
+    return lax.dot_general(docs, queries, NT, preferred_element_type=F32)
+
+
+def score_kernel(flip, at, mine, sibling, queries, *refs):
+    blocks, out = refs[:-1], refs[-1]
+    me = lax.axis_index("tensor")
+    count, width = 2 * DOC_DEV, out.shape[1]
+    own = queries[pl.ds(pl.multiple_of((me ^ flip) * width, width), width), :]
+    rows = [own] + [block[at * width : (at + 1) * width, :] for block in blocks]
+    for m, part in enumerate(rows):
+        out[m * count : (m + 1) * count, :] = scores_of((mine, sibling), part)
+
+
+def score(mine, sibling, queries, blocks, flip, at, shares):
+    width = queries.shape[0] // shares
+    return pl.pallas_call(
+        functools.partial(score_kernel, flip, at),
+        out_shape=jax.ShapeDtypeStruct((2 * DOC_DEV * (1 + len(blocks)), width), F32),
+        in_specs=[VMEM] * (3 + len(blocks)),
         out_specs=VMEM,
         compiler_params=SMALL,
-        cost_estimate=pl.CostEstimate(flops=3_000_000_000, bytes_accessed=0, transcendentals=0),
-        name="near",
-    )(mine, sibling, queries)
-
-
-def score_kernel(flips, mine, sibling, near, *refs):
-    blocks, outs = refs[: -len(flips)], refs[-len(flips) :]
-    me = lax.axis_index("tensor")
-    _, count, width = near.shape
-    for i, k in enumerate(flips):
-        outs[i][:count, :] = near[me ^ k]
-    for m, queries in enumerate(blocks, 1):
-        scores = scores_of((mine, sibling), queries)
-        for i in range(len(flips)):
-            outs[i][m * count : (m + 1) * count, :] = scores[:, i * width : (i + 1) * width]
-
-
-def score(mine, sibling, near, blocks, flips):
-    _, count, width = near.shape
-    return pl.pallas_call(
-        functools.partial(score_kernel, flips),
-        out_shape=[jax.ShapeDtypeStruct((count * (1 + len(blocks)), width), F32)] * len(flips),
-        in_specs=[VMEM] * (3 + len(blocks)),
-        out_specs=[VMEM] * len(flips),
-        compiler_params=SMALL,
+        cost_estimate=pl.CostEstimate(flops=1_000_000_000, bytes_accessed=0, transcendentals=0),
         name="score",
-    )(mine, sibling, near, *blocks)
-
-
-def add_kernel(chips, mine, sibling, near, *refs):
-    blocks, parts, (kept_own, kept_sum, given) = refs[: chips - 1], refs[chips - 1 : -3], refs[-3:]
-    me = lax.axis_index("tensor")
+    )(mine, sibling, queries, *blocks)
+
+
+def add_kernel(chips, own, *refs):
+    parts, (kept_own, kept_sum, given) = refs[:-3], refs[-3:]
     total = parts[0][...]
     for part in parts[1:]:
         total = total + part[...]
-    own = jnp.concatenate([near[me]] + [scores_of((mine, sibling), queries) for queries in blocks], axis=0)
-    own = own.reshape(chips, 2, DOC_DEV, total.shape[1])
+    mine = own[...].reshape(chips, 2, DOC_DEV, total.shape[1])
     summed = total.reshape(chips, 2, DOC_DEV, total.shape[1])
-    kept_own[...] = own[:, 0]
+    kept_own[...] = mine[:, 0]
     kept_sum[...] = summed[:, 1]
-    given[0] = own[:, 1]
+    given[0] = mine[:, 1]
     given[1] = summed[:, 0]
 
 
-def add(mine, sibling, near, blocks, parts):
-    chips, width = 1 + len(blocks), near.shape[2]
+def add(own, parts):
+    chips, width = own.shape[0] // (2 * DOC_DEV), own.shape[1]
     shape = (chips, DOC_DEV, width)
     return pl.pallas_call(
         functools.partial(add_kernel, chips),
         out_shape=[jax.ShapeDtypeStruct(s, F32) for s in (shape, shape, (2, *shape))],
-        in_specs=[VMEM] * (3 + len(blocks) + len(parts)),
+        in_specs=[VMEM] * (1 + len(parts)),
         out_specs=[VMEM] * 3,
         compiler_params=SMALL,
         name="add",
-    )(mine, sibling, near, *blocks, *parts)
+    )(own, *parts)
 
 
 def place_kernel(kept_own, kept_sum, taken, out):
@@ -378,10 +356,12 @@
     late, mine = lax.optimization_barrier((late, mine))
     late = [swapped(late, "docs", 2 * m) for m in chips]
     sibling = swapped(mine, "docs", 1)
-    near = near_scores(mine, sibling, queries, shares)
-    scores = score(mine, sibling, near, early, flips)
-    arrived = [crossed(s, 1, k) for k, s in zip(flips, scores)]
-    kept_own, kept_sum, given = add(mine, sibling, near, late, arrived)
+    arrived = []
+    for at, k in enumerate(flips):
+        part = score(mine, sibling, queries, early, k, at, shares)
+        arrived.append(crossed(part, 1, k))
+    own = score(mine, sibling, queries, late, 0, 0, shares)
+    kept_own, kept_sum, given = add(own, arrived)
     return place(kept_own, kept_sum, swapped(given, "docs", 1))
 
 

time: 35.8 us -> 35.9 us (level)
    ppermute x3, starting transfers between devices: 3.66 us -> 3.25 us  [crossed(): return lax.ppermute(block, ('docs', 'tensor'), pairs)]
    pallas_call x2 -> x4, Pallas kernels: 0.68 us -> 0.95 us  [score(): pl.pallas_call(functools.partial(score_kernel, flip, at), out_shape=jax.S...]
where the time goes in v8:
time: 35.9 us; the launch traced here: 35.8 us
  starting transfers between devices  15.9 us (44%)
  Pallas kernels  12.7 us (35%)
  waiting for transfers between devices  7.06 us (20%)
    ppermute x9, starting transfers between devices, swapped(): lax.ppermute(block, axis, [(i, i ^ flip) for i in range(lax.axis_size(axi...  12.6 us
    pallas_call x1, Pallas kernels, project_grads(): pl.pallas_call(functools.partial(grads_kernel, shares), out_shape=[jax.Sh...  7.07 us
    ppermute x9, waiting for transfers between devices, swapped(): lax.ppermute(block, axis, [(i, i ^ flip) for i in range(lax.axis_size(axi...  7.04 us
    pallas_call x1, Pallas kernels, project_inputs(): pl.pallas_call(functools.partial(inputs_kernel, flips), out_shape=[jax.Sh...  3.42 us
    ppermute x3, starting transfers between devices, crossed(): return lax.ppermute(block, ('docs', 'tensor'), pairs)  3.25 us
    pallas_call x4, Pallas kernels, score(): pl.pallas_call(functools.partial(score_kernel, flip, at), out_shape=jax.S...  0.95 us
  transfers between devices with their start and end apart: 12, of which 6 were waited for; matrix products, arithmetic and copies ran while one was open for 0% of the time, Pallas kernels for 24%

profile of v8, /device:TPU:0, one launch (start us, length us, event | category | flops | bytes accessed | tf_op | source)
XLA Modules:
  0.0 35.8 jit_solution(3315801354990115714)
XLA Ops:
  0.0 3.4 %inputs.1 = (f32[64,1024]{1,0:T(8,128)S(1)}, s16[16,4224]{1,0:T(8,128)(2,1)S(1)}, bf16[384,1024]{1,0:T(8,128)(2,1)}, bf16[128,1024]{1,0:T(8,128)(2,1)}) custom-call(bf16[1024,2048]{1,0:T(8,128)(2,1)} %x_hbm.1, bf16[64,2048]{1,0:T(8,128)(2,1)} %bitcast.3, bf16[512,1024]{1,0:T(8,128)(2,1)} %queries.9), custom_call_target="tpu_custom_call" | custom-call | tf_op jit(solution)/shard_map/inputs/pallas_call | solution.py:177
  3.4 4.1 %collective-permute-start = (s16[16,4224]{1,0:T(8,128)(2,1)S(1)}, s16[16,4224]{1,0:T(8,128)(2,1)S(1)}, u32[]{:S(2)}, u32[]{:S(2)}) collective-permute-start(s16[16,4224]{1,0:T(8,128)(2,1)S(1)} %get-tuple-element.24), channel_id=1, source_target_pairs={{0,2},{1,3},{2,0},{3,1},{4,6},{5,7},{6,4},{7,5},{8,10},{9,11},{10,... | collective-permute-start | bytes 405512 | tf_op jit(solution)/shard_map/ppermute | solution.py:27
  7.5 1.5 %collective-permute-start.7 = (bf16[384,1024]{1,0:T(8,128)(2,1)}, bf16[384,1024]{1,0:T(8,128)(2,1)S(1)}, u32[]{:S(2)}, u32[]{:S(2)}) collective-permute-start(bf16[384,1024]{1,0:T(8,128)(2,1)} %get-tuple-element.35), channel_id=1, source_target_pairs={{0,8},{4,12},{8,0},{12,4},{1,9},{5,13},{9,1},{13,5},{2,10},{6,14},... | collective-permute-start | bytes 2359304 | tf_op jit(solution)/shard_map/ppermute | solution.py:27
  9.1 7.1 %grads.1 = (f32[16,1024]{1,0:T(8,128)S(1)}, s16[16,1152]{1,0:T(8,128)(2,1)S(1)}, s16[16,1152]{1,0:T(8,128)(2,1)S(1)}, s16[16,1152]{1,0:T(8,128)(2,1)S(1)}) custom-call(bf16[1024,7168]{1,0:T(8,128)(2,1)} %g_hbm.1, bf16[64,7168]{1,0:T(8,128)(2,1)} %bitcast.2), custom_call_target="tpu_custom_call" | custom-call | tf_op jit(solution)/shard_map/grads/pallas_call | solution.py:217
  16.1 0.0 collective-permute-done.arrived
  16.1 0.0 copy-start.1
  16.2 0.0 copy-start
  16.2 0.1 fold_in.1
  16.3 1.6 %collective-permute-start.1 = (s16[16,4224]{1,0:T(8,128)(2,1)S(1)}, s16[16,4224]{1,0:T(8,128)(2,1)S(1)}, u32[]{:S(2)}, u32[]{:S(2)}) collective-permute-start(s16[16,4224]{1,0:T(8,128)(2,1)S(1)} %get-tuple-element.29), channel_id=1, source_target_pairs={{0,1},{1,0},{2,3},{3,2},{4,5},{5,4},{6,7},{7,6},{8,9},{9,8},{10,11... | collective-permute-start | bytes 405512 | tf_op jit(solution)/shard_map/ppermute | solution.py:27
  17.9 0.2 collective-permute-start.2
  18.2 1.7 %collective-permute-start.3 = (s16[16,1152]{1,0:T(8,128)(2,1)S(1)}, s16[16,1152]{1,0:T(8,128)(2,1)S(1)}, u32[]{:S(2)}, u32[]{:S(2)}) collective-permute-start(s16[16,1152]{1,0:T(8,128)(2,1)S(1)} %get-tuple-element.31), channel_id=1, source_target_pairs={{0,2},{1,3},{2,0},{3,1},{4,6},{5,7},{6,4},{7,5},{8,10},{9,11},{10,... | collective-permute-start | bytes 110600 | tf_op jit(solution)/shard_map/ppermute | solution.py:27
  19.8 2.5 %collective-permute-start.4 = (s16[16,1152]{1,0:T(8,128)(2,1)S(1)}, s16[16,1152]{1,0:T(8,128)(2,1)S(1)}, u32[]{:S(2)}, u32[]{:S(2)}) collective-permute-start(s16[16,1152]{1,0:T(8,128)(2,1)S(1)} %get-tuple-element.32), channel_id=1, source_target_pairs={{0,1},{1,0},{2,3},{3,2},{4,5},{5,4},{6,7},{7,6},{8,9},{9,8},{10,11... | collective-permute-start | bytes 110600 | tf_op jit(solution)/shard_map/ppermute | solution.py:27
  22.3 1.4 %collective-permute-done.2.refs_0_ = s16[16,1152]{1,0:T(8,128)(2,1)S(1)} collective-permute-done((s16[16,1152]{1,0:T(8,128)(2,1)S(1)}, s16[16,1152]{1,0:T(8,128)(2,1)S(1)}, u32[]{:S(2)}, u32[]{:S(2)}) %collective-permute-start.2) | collective-permute-done | bytes 36896 | tf_op jit(solution)/shard_map/ppermute | solution.py:27
  23.7 0.6 %collective-permute-done.4.refs_2_ = s16[16,1152]{1,0:T(8,128)(2,1)S(1)} collective-permute-done((s16[16,1152]{1,0:T(8,128)(2,1)S(1)}, s16[16,1152]{1,0:T(8,128)(2,1)S(1)}, u32[]{:S(2)}, u32[]{:S(2)}) %collective-permute-start.4) | collective-permute-done | bytes 36896 | tf_op jit(solution)/shard_map/ppermute | solution.py:27
  24.3 0.5 %train.1.mine = bf16[16,512]{1,0:T(8,128)(2,1)S(1)} custom-call(s32[1,1024]{1,0:T(1,128)S(1)} %copy-done.1, f32[64,1024]{1,0:T(8,128)S(1)} %get-tuple-element.27.x_own, f32[16,1024]{1,0:T(8,128)S(1)} %get-tuple-element.28.g_own, s16[16,4224]{1,0:T(8,128)(2,1)S(1)} %collective-permute-done.1.x_sent, s16[16,1152]{1,0:T(8,128)(2,1)S(1)} %collective-permute-done.2.refs_0_, ...), custom_call_target="tpu_custom_call" | custom-call | tf_op jit(solution)/shard_map/train/pallas_call | solution.py:253
  24.8 0.1 collective-permute-start.5
  24.9 0.8 %collective-permute-start.6 = (bf16[128,1024]{1,0:T(8,128)(2,1)S(1)}, bf16[128,1024]{1,0:T(8,128)(2,1)S(1)}, u32[]{:S(2)}, u32[]{:S(2)}) collective-permute-start(bf16[128,1024]{1,0:T(8,128)(2,1)S(1)} %copy-done.2), channel_id=1, source_target_pairs={{0,8},{4,12},{8,0},{12,4},{1,9},{5,13},{9,1},{13,5},{2,10},{6,14},... | collective-permute-start | bytes 786440 | tf_op jit(solution)/shard_map/ppermute | solution.py:27
  25.7 0.3 collective-permute-done.5.sibling
  26.0 0.7 %collective-permute-done.7.refs_0_ = bf16[384,1024]{1,0:T(8,128)(2,1)S(1)} collective-permute-done((bf16[384,1024]{1,0:T(8,128)(2,1)}, bf16[384,1024]{1,0:T(8,128)(2,1)S(1)}, u32[]{:S(2)}, u32[]{:S(2)}) %collective-permute-start.7) | collective-permute-done | bytes 786464 | tf_op jit(solution)/shard_map/ppermute | solution.py:27
  26.8 0.2 score.5
  27.0 1.7 %collective-permute-start.8 = (f32[32,128]{1,0:T(8,128)S(1)}, f32[32,128]{1,0:T(8,128)S(1)}, u32[]{:S(2)}, u32[]{:S(2)}) collective-permute-start(f32[32,128]{1,0:T(8,128)S(1)} %score.5), channel_id=1, source_target_pairs={{0,7},{1,6},{2,5},{3,4},{4,3},{5,2},{6,1},{7,0},{8,15},{9,14},{10,... | collective-permute-start | bytes 49160 | tf_op jit(solution)/shard_map/ppermute | solution.py:33
  28.7 0.2 score.6
  28.9 1.1 %collective-permute-start.9 = (f32[32,128]{1,0:T(8,128)S(1)}, f32[32,128]{1,0:T(8,128)S(1)}, u32[]{:S(2)}, u32[]{:S(2)}) collective-permute-start(f32[32,128]{1,0:T(8,128)S(1)} %score.6), channel_id=1, source_target_pairs={{0,6},{1,7},{2,4},{3,5},{4,2},{5,3},{6,0},{7,1},{8,14},{9,15},{10,... | collective-permute-start | bytes 49160 | tf_op jit(solution)/shard_map/ppermute | solution.py:33
  30.0 0.2 score.7
  30.3 0.4 %collective-permute-start.10 = (f32[32,128]{1,0:T(8,128)S(1)}, f32[32,128]{1,0:T(8,128)S(1)}, u32[]{:S(2)}, u32[]{:S(2)}) collective-permute-start(f32[32,128]{1,0:T(8,128)S(1)} %score.7), channel_id=1, source_target_pairs={{0,5},{1,4},{2,7},{3,6},{4,1},{5,0},{6,3},{7,2},{8,13},{9,12},{10,... | collective-permute-start | bytes 49160 | tf_op jit(solution)/shard_map/ppermute | solution.py:33
  30.7 2.9 %collective-permute-done.6.refs_0_ = bf16[128,1024]{1,0:T(8,128)(2,1)S(1)} collective-permute-done((bf16[128,1024]{1,0:T(8,128)(2,1)S(1)}, bf16[128,1024]{1,0:T(8,128)(2,1)S(1)}, u32[]{:S(2)}, u32[]{:S(2)}) %collective-permute-start.6) | collective-permute-done | bytes 262176 | tf_op jit(solution)/shard_map/ppermute | solution.py:27
  33.6 0.2 score.4.own
  33.8 0.0 collective-permute-done.9.refs_1_
  33.9 0.0 collective-permute-done.10.refs_2_
  33.9 0.1 collective-permute-start.11
  34.0 1.2 %collective-permute-done.11.taken = f32[2,2,8,128]{3,2,1,0:T(8,128)S(1)} collective-permute-done((f32[2,2,8,128]{3,2,1,0:T(8,128)S(1)}, f32[2,2,8,128]{3,2,1,0:T(8,128)S(1)}, u32[]{:S(2)}, u32[]{:S(2)}) %collective-permute-start.11) | collective-permute-done | bytes 16416 | tf_op jit(solution)/shard_map/ppermute | solution.py:27
  35.1 0.6 %place.1 = f32[8,4,128]{2,1,0:T(4,128)} custom-call(f32[2,8,128]{2,1,0:T(8,128)S(1)} %get-tuple-element.36.kept_own, f32[2,8,128]{2,1,0:T(8,128)S(1)} %get-tuple-element.37.kept_sum, f32[2,2,8,128]{3,2,1,0:T(8,128)S(1)} %collective-permute-done.11.taken), custom_call_target="tpu_custom_call" | custom-call | tf_op jit(solution)/shard_map/place/pallas_call | solution.py:330
  (8 shorter events, 0.0 us)
Async XLA Ops:
  3.4 12.7 %collective-permute-start = (s16[16,4224]{1,0:T(8,128)(2,1)S(1)}, s16[16,4224]{1,0:T(8,128)(2,1)S(1)}, u32[]{:S(2)}, u32[]{:S(2)}) collective-permute-start(s16[16,4224]{1,0:T(8,128)(2,1)S(1)} %get-tuple-element.24), channel_id=1, source_target_pairs={{0,2},{1,3},{2,0},{3,1},{4,6},{5,7},{6,4},{7,5},{8,10},{9,11},{10,... | collective-permute-start | bytes 405512 | tf_op jit(solution)/shard_map/ppermute | solution.py:27
  7.5 19.2 %collective-permute-start.7 = (bf16[384,1024]{1,0:T(8,128)(2,1)}, bf16[384,1024]{1,0:T(8,128)(2,1)S(1)}, u32[]{:S(2)}, u32[]{:S(2)}) collective-permute-start(bf16[384,1024]{1,0:T(8,128)(2,1)} %get-tuple-element.35), channel_id=1, source_target_pairs={{0,8},{4,12},{8,0},{12,4},{1,9},{5,13},{9,1},{13,5},{2,10},{6,14},... | collective-permute-start | bytes 2359304 | tf_op jit(solution)/shard_map/ppermute | solution.py:27
  16.1 8.1 %copy-start.1 = (s32[1,1024]{1,0:T(1,128)S(1)}, s32[1,1024]{1,0:T(1,128)}, u32[]{:S(2)}) copy-start(s32[1,1024]{1,0:T(1,128)} %ids.1) | copy-start | bytes 12292
  16.2 8.7 %copy-start.2 = (bf16[128,1024]{1,0:T(8,128)(2,1)S(1)}, bf16[128,1024]{1,0:T(8,128)(2,1)}, u32[]{:S(2)}) copy-start(bf16[128,1024]{1,0:T(8,128)(2,1)} %get-tuple-element.34) | copy-start | bytes 786436
  16.2 10.6 %copy-start = (bf16[512,1024]{1,0:T(8,128)(2,1)S(1)}, bf16[512,1024]{1,0:T(8,128)(2,1)}, u32[]{:S(2)}) copy-start(bf16[512,1024]{1,0:T(8,128)(2,1)} %queries.9) | copy-start | bytes 3145732
  16.3 8.0 %collective-permute-start.1 = (s16[16,4224]{1,0:T(8,128)(2,1)S(1)}, s16[16,4224]{1,0:T(8,128)(2,1)S(1)}, u32[]{:S(2)}, u32[]{:S(2)}) collective-permute-start(s16[16,4224]{1,0:T(8,128)(2,1)S(1)} %get-tuple-element.29), channel_id=1, source_target_pairs={{0,1},{1,0},{2,3},{3,2},{4,5},{5,4},{6,7},{7,6},{8,9},{9,8},{10,11... | collective-permute-start | bytes 405512 | tf_op jit(solution)/shard_map/ppermute | solution.py:27
  17.9 5.8 %collective-permute-start.2 = (s16[16,1152]{1,0:T(8,128)(2,1)S(1)}, s16[16,1152]{1,0:T(8,128)(2,1)S(1)}, u32[]{:S(2)}, u32[]{:S(2)}) collective-permute-start(s16[16,1152]{1,0:T(8,128)(2,1)S(1)} %get-tuple-element.30), channel_id=1, source_target_pairs={{0,3},{1,2},{2,1},{3,0},{4,7},{5,6},{6,5},{7,4},{8,11},{9,10},{10,... | collective-permute-start | bytes 110600 | tf_op jit(solution)/shard_map/ppermute | solution.py:27
  18.2 5.5 %collective-permute-start.3 = (s16[16,1152]{1,0:T(8,128)(2,1)S(1)}, s16[16,1152]{1,0:T(8,128)(2,1)S(1)}, u32[]{:S(2)}, u32[]{:S(2)}) collective-permute-start(s16[16,1152]{1,0:T(8,128)(2,1)S(1)} %get-tuple-element.31), channel_id=1, source_target_pairs={{0,2},{1,3},{2,0},{3,1},{4,6},{5,7},{6,4},{7,5},{8,10},{9,11},{10,... | collective-permute-start | bytes 110600 | tf_op jit(solution)/shard_map/ppermute | solution.py:27
  19.8 4.4 %collective-permute-start.4 = (s16[16,1152]{1,0:T(8,128)(2,1)S(1)}, s16[16,1152]{1,0:T(8,128)(2,1)S(1)}, u32[]{:S(2)}, u32[]{:S(2)}) collective-permute-start(s16[16,1152]{1,0:T(8,128)(2,1)S(1)} %get-tuple-element.32), channel_id=1, source_target_pairs={{0,1},{1,0},{2,3},{3,2},{4,5},{5,4},{6,7},{7,6},{8,9},{9,8},{10,11... | collective-permute-start | bytes 110600 | tf_op jit(solution)/shard_map/ppermute | solution.py:27
  24.8 1.2 %collective-permute-start.5 = (bf16[16,512]{1,0:T(8,128)(2,1)S(1)}, bf16[16,512]{1,0:T(8,128)(2,1)S(1)}, u32[]{:S(2)}, u32[]{:S(2)}) collective-permute-start(bf16[16,512]{1,0:T(8,128)(2,1)S(1)} %train.1.mine), channel_id=1, source_target_pairs={{0,4},{4,0},{8,12},{12,8},{1,5},{5,1},{9,13},{13,9},{2,6},{6,2},{1... | collective-permute-start | bytes 49160 | tf_op jit(solution)/shard_map/ppermute | solution.py:27
  24.9 8.7 %collective-permute-start.6 = (bf16[128,1024]{1,0:T(8,128)(2,1)S(1)}, bf16[128,1024]{1,0:T(8,128)(2,1)S(1)}, u32[]{:S(2)}, u32[]{:S(2)}) collective-permute-start(bf16[128,1024]{1,0:T(8,128)(2,1)S(1)} %copy-done.2), channel_id=1, source_target_pairs={{0,8},{4,12},{8,0},{12,4},{1,9},{5,13},{9,1},{13,5},{2,10},{6,14},... | collective-permute-start | bytes 786440 | tf_op jit(solution)/shard_map/ppermute | solution.py:27
  27.0 6.8 %collective-permute-start.8 = (f32[32,128]{1,0:T(8,128)S(1)}, f32[32,128]{1,0:T(8,128)S(1)}, u32[]{:S(2)}, u32[]{:S(2)}) collective-permute-start(f32[32,128]{1,0:T(8,128)S(1)} %score.5), channel_id=1, source_target_pairs={{0,7},{1,6},{2,5},{3,4},{4,3},{5,2},{6,1},{7,0},{8,15},{9,14},{10,... | collective-permute-start | bytes 49160 | tf_op jit(solution)/shard_map/ppermute | solution.py:33
  28.9 4.9 %collective-permute-start.9 = (f32[32,128]{1,0:T(8,128)S(1)}, f32[32,128]{1,0:T(8,128)S(1)}, u32[]{:S(2)}, u32[]{:S(2)}) collective-permute-start(f32[32,128]{1,0:T(8,128)S(1)} %score.6), channel_id=1, source_target_pairs={{0,6},{1,7},{2,4},{3,5},{4,2},{5,3},{6,0},{7,1},{8,14},{9,15},{10,... | collective-permute-start | bytes 49160 | tf_op jit(solution)/shard_map/ppermute | solution.py:33
  30.3 3.6 %collective-permute-start.10 = (f32[32,128]{1,0:T(8,128)S(1)}, f32[32,128]{1,0:T(8,128)S(1)}, u32[]{:S(2)}, u32[]{:S(2)}) collective-permute-start(f32[32,128]{1,0:T(8,128)S(1)} %score.7), channel_id=1, source_target_pairs={{0,5},{1,4},{2,7},{3,6},{4,1},{5,0},{6,3},{7,2},{8,13},{9,12},{10,... | collective-permute-start | bytes 49160 | tf_op jit(solution)/shard_map/ppermute | solution.py:33
  33.9 1.2 %collective-permute-start.11 = (f32[2,2,8,128]{3,2,1,0:T(8,128)S(1)}, f32[2,2,8,128]{3,2,1,0:T(8,128)S(1)}, u32[]{:S(2)}, u32[]{:S(2)}) collective-permute-start(f32[2,2,8,128]{3,2,1,0:T(8,128)S(1)} %get-tuple-element.38), channel_id=1, source_target_pairs={{0,4},{4,0},{8,12},{12,8},{1,5},{5,1},{9,13},{13,9},{2,6},{6,2},{1... | collective-permute-start | bytes 49160 | tf_op jit(solution)/shard_map/ppermute | solution.py:27

commit v9 on v7

--- a/solution.py
+++ b/solution.py
@@ -20,7 +20,7 @@
 MESSAGE_ROWS = 16
 ROW_STEPS = 4
 X_PIECES, X_AHEAD = 1, 3
-G_PIECES, G_AHEAD = 1, 2
+G_PIECES, G_AHEAD = 2, 2
 
 
 def swapped(block, axis, flip):
@@ -69,23 +69,23 @@
     return decoded(steps, unfolded(sent[:, last:].astype(jnp.int32)[: tokens // LANES]))
 
 
-def stream_copies(hbm, buffer, sems, pieces):
-    rows, columns = buffer.shape[0] // ROW_STEPS, buffer.shape[1] // pieces
+def stream_copies(hbm, buffer, sems, pieces, blocks):
+    rows, columns = buffer.shape[0] // blocks, buffer.shape[1] // pieces
     return [
         pltpu.make_async_copy(
             hbm.at[pl.ds(a * rows, rows), pl.ds(c * columns, columns)],
             buffer.at[pl.ds(a * rows, rows), pl.ds(c * columns, columns)],
             sems.at[a * pieces + c],
         )
-        for a in range(ROW_STEPS)
+        for a in range(blocks)
         for c in range(pieces)
     ]
 
 
 def streamed(hbm, weights_hbm, buffer, weights, acc, out, sems, pieces, ahead, between=None):
     me = lax.axis_index("tensor")
-    rows, columns = buffer.shape[0] // ROW_STEPS, buffer.shape[1] // pieces
-    copies = stream_copies(hbm, buffer, sems, pieces)
+    rows, columns = acc.shape[0], buffer.shape[1] // pieces
+    copies = stream_copies(hbm, buffer, sems, pieces, buffer.shape[0] // rows)
     first = pltpu.make_async_copy(weights_hbm, weights, sems.at[len(copies)])
     first.start()
     for copy in copies[:ahead]:
@@ -117,12 +117,12 @@
                 out[:, a * rows : (a + 1) * rows] = d.T
 
 
-def stream_scratch(rows, proj_t, pieces):
+def stream_scratch(rows, proj_t, pieces, blocks):
     return [
         pltpu.VMEM((rows, proj_t.shape[1]), BF16),
         pltpu.VMEM(proj_t.shape, BF16),
-        pltpu.VMEM((rows // ROW_STEPS, proj_t.shape[0]), F32),
-        pltpu.SemaphoreType.DMA((ROW_STEPS * pieces + 1,)),
+        pltpu.VMEM((rows // blocks, proj_t.shape[0]), F32),
+        pltpu.SemaphoreType.DMA((blocks * pieces + 1,)),
     ]
 
 
@@ -184,7 +184,7 @@
         ],
         in_specs=[ANY] * 3,
         out_specs=[VMEM] * 2 + [ANY] * 2,
-        scratch_shapes=stream_scratch(tokens, proj_t, X_PIECES)
+        scratch_shapes=stream_scratch(tokens, proj_t, X_PIECES, ROW_STEPS)
         + [pltpu.VMEM(queries.shape, BF16), pltpu.SemaphoreType.DMA((len(flips) + 2,))],
         compiler_params=STREAM,
         name="inputs",
@@ -221,7 +221,7 @@
         in_specs=[ANY] * 2,
         out_specs=[VMEM] * shares,
         scratch_shapes=[pltpu.VMEM((shares, rows, tokens), F32), pltpu.VMEM((rank, tokens), F32)]
-        + stream_scratch(tokens, proj_t, G_PIECES),
+        + stream_scratch(tokens, proj_t, G_PIECES, ROW_STEPS // 2),
         compiler_params=pltpu.CompilerParams(vmem_limit_bytes=int(53.5 * 2**20)),
         name="grads",
     )(grads, proj_t)

time: 35.8 us -> 35.8 us (level)
  no operation moved by 1% of the time
where the time goes in v9:
time: 35.8 us; the launch traced here: 35.6 us
  starting transfers between devices  16.1 us (45%)
  Pallas kernels  12.6 us (35%)
  waiting for transfers between devices  6.79 us (19%)
    ppermute x9, starting transfers between devices, swapped(): lax.ppermute(block, axis, [(i, i ^ flip) for i in range(lax.axis_size(axi...  12.5 us
    pallas_call x1, Pallas kernels, project_grads(): pl.pallas_call(functools.partial(grads_kernel, shares), out_shape=[jax.Sh...  7.1 us
    ppermute x9, waiting for transfers between devices, swapped(): lax.ppermute(block, axis, [(i, i ^ flip) for i in range(lax.axis_size(axi...  6.79 us
    ppermute x3, starting transfers between devices, crossed(): return lax.ppermute(block, ('docs', 'tensor'), pairs)  3.61 us
    pallas_call x1, Pallas kernels, project_inputs(): pl.pallas_call(functools.partial(inputs_kernel, flips), out_shape=[jax.Sh...  3.42 us
  transfers between devices with their start and end apart: 12, of which 6 were waited for; matrix products, arithmetic and copies ran while one was open for 0% of the time, Pallas kernels for 24%

profile of v9, /device:TPU:0, one launch (start us, length us, event | category | flops | bytes accessed | tf_op | source)
XLA Modules:
  0.0 35.6 jit_solution(13224567790227070085)
XLA Ops:
  0.0 3.4 %inputs.1 = (f32[64,1024]{1,0:T(8,128)S(1)}, s16[16,4224]{1,0:T(8,128)(2,1)S(1)}, bf16[384,1024]{1,0:T(8,128)(2,1)}, bf16[128,1024]{1,0:T(8,128)(2,1)}) custom-call(bf16[1024,2048]{1,0:T(8,128)(2,1)} %x_hbm.1, bf16[64,2048]{1,0:T(8,128)(2,1)} %bitcast.3, bf16[512,1024]{1,0:T(8,128)(2,1)} %queries.3), custom_call_target="tpu_custom_call" | custom-call | tf_op jit(solution)/shard_map/inputs/pallas_call | solution.py:177
  3.4 4.1 %collective-permute-start = (s16[16,4224]{1,0:T(8,128)(2,1)S(1)}, s16[16,4224]{1,0:T(8,128)(2,1)S(1)}, u32[]{:S(2)}, u32[]{:S(2)}) collective-permute-start(s16[16,4224]{1,0:T(8,128)(2,1)S(1)} %get-tuple-element.27), channel_id=1, source_target_pairs={{0,2},{1,3},{2,0},{3,1},{4,6},{5,7},{6,4},{7,5},{8,10},{9,11},{10,... | collective-permute-start | bytes 405512 | tf_op jit(solution)/shard_map/ppermute | solution.py:27
  7.5 1.5 %collective-permute-start.7 = (bf16[384,1024]{1,0:T(8,128)(2,1)}, bf16[384,1024]{1,0:T(8,128)(2,1)S(1)}, u32[]{:S(2)}, u32[]{:S(2)}) collective-permute-start(bf16[384,1024]{1,0:T(8,128)(2,1)} %get-tuple-element.38), channel_id=1, source_target_pairs={{0,8},{4,12},{8,0},{12,4},{1,9},{5,13},{9,1},{13,5},{2,10},{6,14},... | collective-permute-start | bytes 2359304 | tf_op jit(solution)/shard_map/ppermute | solution.py:27
  9.1 7.1 %grads.1 = (f32[16,1024]{1,0:T(8,128)S(1)}, s16[16,1152]{1,0:T(8,128)(2,1)S(1)}, s16[16,1152]{1,0:T(8,128)(2,1)S(1)}, s16[16,1152]{1,0:T(8,128)(2,1)S(1)}) custom-call(bf16[1024,7168]{1,0:T(8,128)(2,1)} %g_hbm.1, bf16[64,7168]{1,0:T(8,128)(2,1)} %bitcast.2), custom_call_target="tpu_custom_call" | custom-call | tf_op jit(solution)/shard_map/grads/pallas_call | solution.py:217
  16.2 0.0 collective-permute-done.arrived
  16.2 0.0 copy-start.1
  16.2 0.0 copy-start
  16.2 0.1 fold_in.1
  16.3 1.6 %collective-permute-start.1 = (s16[16,4224]{1,0:T(8,128)(2,1)S(1)}, s16[16,4224]{1,0:T(8,128)(2,1)S(1)}, u32[]{:S(2)}, u32[]{:S(2)}) collective-permute-start(s16[16,4224]{1,0:T(8,128)(2,1)S(1)} %get-tuple-element.32), channel_id=1, source_target_pairs={{0,1},{1,0},{2,3},{3,2},{4,5},{5,4},{6,7},{7,6},{8,9},{9,8},{10,11... | collective-permute-start | bytes 405512 | tf_op jit(solution)/shard_map/ppermute | solution.py:27
  18.0 0.2 collective-permute-start.2
  18.2 1.7 %collective-permute-start.3 = (s16[16,1152]{1,0:T(8,128)(2,1)S(1)}, s16[16,1152]{1,0:T(8,128)(2,1)S(1)}, u32[]{:S(2)}, u32[]{:S(2)}) collective-permute-start(s16[16,1152]{1,0:T(8,128)(2,1)S(1)} %get-tuple-element.34), channel_id=1, source_target_pairs={{0,2},{1,3},{2,0},{3,1},{4,6},{5,7},{6,4},{7,5},{8,10},{9,11},{10,... | collective-permute-start | bytes 110600 | tf_op jit(solution)/shard_map/ppermute | solution.py:27
  19.9 2.5 %collective-permute-start.4 = (s16[16,1152]{1,0:T(8,128)(2,1)S(1)}, s16[16,1152]{1,0:T(8,128)(2,1)S(1)}, u32[]{:S(2)}, u32[]{:S(2)}) collective-permute-start(s16[16,1152]{1,0:T(8,128)(2,1)S(1)} %get-tuple-element.35), channel_id=1, source_target_pairs={{0,1},{1,0},{2,3},{3,2},{4,5},{5,4},{6,7},{7,6},{8,9},{9,8},{10,11... | collective-permute-start | bytes 110600 | tf_op jit(solution)/shard_map/ppermute | solution.py:27
  22.4 1.4 %collective-permute-done.2.refs_0_ = s16[16,1152]{1,0:T(8,128)(2,1)S(1)} collective-permute-done((s16[16,1152]{1,0:T(8,128)(2,1)S(1)}, s16[16,1152]{1,0:T(8,128)(2,1)S(1)}, u32[]{:S(2)}, u32[]{:S(2)}) %collective-permute-start.2) | collective-permute-done | bytes 36896 | tf_op jit(solution)/shard_map/ppermute | solution.py:27
  23.7 0.6 %collective-permute-done.4.refs_2_ = s16[16,1152]{1,0:T(8,128)(2,1)S(1)} collective-permute-done((s16[16,1152]{1,0:T(8,128)(2,1)S(1)}, s16[16,1152]{1,0:T(8,128)(2,1)S(1)}, u32[]{:S(2)}, u32[]{:S(2)}) %collective-permute-start.4) | collective-permute-done | bytes 36896 | tf_op jit(solution)/shard_map/ppermute | solution.py:27
  24.3 0.0 collective-permute-done.1.x_sent
  24.3 0.5 %train.1.mine = bf16[16,512]{1,0:T(8,128)(2,1)S(1)} custom-call(s32[1,1024]{1,0:T(1,128)S(1)} %copy-done.1, f32[64,1024]{1,0:T(8,128)S(1)} %get-tuple-element.30.x_own, f32[16,1024]{1,0:T(8,128)S(1)} %get-tuple-element.31.g_own, s16[16,4224]{1,0:T(8,128)(2,1)S(1)} %collective-permute-done.1.x_sent, s16[16,1152]{1,0:T(8,128)(2,1)S(1)} %collective-permute-done.2.refs_0_, ...), custom_call_target="tpu_custom_call" | custom-call | tf_op jit(solution)/shard_map/train/pallas_call | solution.py:253
  24.8 0.1 collective-permute-start.5
  24.9 0.8 %collective-permute-start.6 = (bf16[128,1024]{1,0:T(8,128)(2,1)S(1)}, bf16[128,1024]{1,0:T(8,128)(2,1)S(1)}, u32[]{:S(2)}, u32[]{:S(2)}) collective-permute-start(bf16[128,1024]{1,0:T(8,128)(2,1)S(1)} %copy-done.2), channel_id=1, source_target_pairs={{0,8},{4,12},{8,0},{12,4},{1,9},{5,13},{9,1},{13,5},{2,10},{6,14},... | collective-permute-start | bytes 786440 | tf_op jit(solution)/shard_map/ppermute | solution.py:27
  25.7 0.4 %collective-permute-done.5.sibling = bf16[16,512]{1,0:T(8,128)(2,1)S(1)} collective-permute-done((bf16[16,512]{1,0:T(8,128)(2,1)S(1)}, bf16[16,512]{1,0:T(8,128)(2,1)S(1)}, u32[]{:S(2)}, u32[]{:S(2)}) %collective-permute-start.5) | collective-permute-done | bytes 16416 | tf_op jit(solution)/shard_map/ppermute | solution.py:27
  26.1 0.4 %near.1 = f32[4,16,128]{2,1,0:T(8,128)S(1)} custom-call(bf16[16,512]{1,0:T(8,128)(2,1)S(1)} %train.1.mine, bf16[16,512]{1,0:T(8,128)(2,1)S(1)} %collective-permute-done.5.sibling, bf16[512,1024]{1,0:T(8,128)(2,1)S(1)} %copy-done), custom_call_target="tpu_custom_call" | custom-call | flops 3000000000 | tf_op jit(solution)/shard_map/near/pallas_call | solution.py:280
  26.4 0.3 collective-permute-done.7.refs_0_
  26.8 0.3 score.1
  27.1 2.1 %collective-permute-start.8 = (f32[32,128]{1,0:T(8,128)S(1)}, f32[32,128]{1,0:T(8,128)S(1)}, u32[]{:S(2)}, u32[]{:S(2)}) collective-permute-start(f32[32,128]{1,0:T(8,128)S(1)} %get-tuple-element.39), channel_id=1, source_target_pairs={{0,7},{1,6},{2,5},{3,4},{4,3},{5,2},{6,1},{7,0},{8,15},{9,14},{10,... | collective-permute-start | bytes 49160 | tf_op jit(solution)/shard_map/ppermute | solution.py:33
  29.2 0.8 %collective-permute-start.9 = (f32[32,128]{1,0:T(8,128)S(1)}, f32[32,128]{1,0:T(8,128)S(1)}, u32[]{:S(2)}, u32[]{:S(2)}) collective-permute-start(f32[32,128]{1,0:T(8,128)S(1)} %get-tuple-element.40), channel_id=1, source_target_pairs={{0,6},{1,7},{2,4},{3,5},{4,2},{5,3},{6,0},{7,1},{8,14},{9,15},{10,... | collective-permute-start | bytes 49160 | tf_op jit(solution)/shard_map/ppermute | solution.py:33
  30.0 0.7 %collective-permute-start.10 = (f32[32,128]{1,0:T(8,128)S(1)}, f32[32,128]{1,0:T(8,128)S(1)}, u32[]{:S(2)}, u32[]{:S(2)}) collective-permute-start(f32[32,128]{1,0:T(8,128)S(1)} %get-tuple-element.41), channel_id=1, source_target_pairs={{0,5},{1,4},{2,7},{3,6},{4,1},{5,0},{6,3},{7,2},{8,13},{9,12},{10,... | collective-permute-start | bytes 49160 | tf_op jit(solution)/shard_map/ppermute | solution.py:33
  30.7 3.0 %collective-permute-done.6.refs_0_ = bf16[128,1024]{1,0:T(8,128)(2,1)S(1)} collective-permute-done((bf16[128,1024]{1,0:T(8,128)(2,1)S(1)}, bf16[128,1024]{1,0:T(8,128)(2,1)S(1)}, u32[]{:S(2)}, u32[]{:S(2)}) %collective-permute-start.6) | collective-permute-done | bytes 262176 | tf_op jit(solution)/shard_map/ppermute | solution.py:27
  33.6 0.0 collective-permute-done.8.refs_1_
  33.6 0.0 collective-permute-done.9.refs_2_
  33.6 0.0 collective-permute-done.10.refs_3_
  33.6 0.2 add.1
  33.8 1.2 %collective-permute-done.11.taken = f32[2,2,8,128]{3,2,1,0:T(8,128)S(1)} collective-permute-done((f32[2,2,8,128]{3,2,1,0:T(8,128)S(1)}, f32[2,2,8,128]{3,2,1,0:T(8,128)S(1)}, u32[]{:S(2)}, u32[]{:S(2)}) %collective-permute-start.11) | collective-permute-done | bytes 16416 | tf_op jit(solution)/shard_map/ppermute | solution.py:27
  35.0 0.6 %place.1 = f32[8,4,128]{2,1,0:T(4,128)} custom-call(f32[2,8,128]{2,1,0:T(8,128)S(1)} %get-tuple-element.42.kept_own, f32[2,8,128]{2,1,0:T(8,128)S(1)} %get-tuple-element.43.kept_sum, f32[2,2,8,128]{3,2,1,0:T(8,128)S(1)} %collective-permute-done.11.taken), custom_call_target="tpu_custom_call" | custom-call | tf_op jit(solution)/shard_map/place/pallas_call | solution.py:352
  (6 shorter events, 0.0 us)
Async XLA Ops:
  3.4 12.7 %collective-permute-start = (s16[16,4224]{1,0:T(8,128)(2,1)S(1)}, s16[16,4224]{1,0:T(8,128)(2,1)S(1)}, u32[]{:S(2)}, u32[]{:S(2)}) collective-permute-start(s16[16,4224]{1,0:T(8,128)(2,1)S(1)} %get-tuple-element.27), channel_id=1, source_target_pairs={{0,2},{1,3},{2,0},{3,1},{4,6},{5,7},{6,4},{7,5},{8,10},{9,11},{10,... | collective-permute-start | bytes 405512 | tf_op jit(solution)/shard_map/ppermute | solution.py:27
  7.5 19.2 %collective-permute-start.7 = (bf16[384,1024]{1,0:T(8,128)(2,1)}, bf16[384,1024]{1,0:T(8,128)(2,1)S(1)}, u32[]{:S(2)}, u32[]{:S(2)}) collective-permute-start(bf16[384,1024]{1,0:T(8,128)(2,1)} %get-tuple-element.38), channel_id=1, source_target_pairs={{0,8},{4,12},{8,0},{12,4},{1,9},{5,13},{9,1},{13,5},{2,10},{6,14},... | collective-permute-start | bytes 2359304 | tf_op jit(solution)/shard_map/ppermute | solution.py:27
  16.2 8.1 %copy-start.1 = (s32[1,1024]{1,0:T(1,128)S(1)}, s32[1,1024]{1,0:T(1,128)}, u32[]{:S(2)}) copy-start(s32[1,1024]{1,0:T(1,128)} %ids.1) | copy-start | bytes 12292
  16.2 8.7 %copy-start.2 = (bf16[128,1024]{1,0:T(8,128)(2,1)S(1)}, bf16[128,1024]{1,0:T(8,128)(2,1)}, u32[]{:S(2)}) copy-start(bf16[128,1024]{1,0:T(8,128)(2,1)} %get-tuple-element.37) | copy-start | bytes 786436
  16.2 9.9 %copy-start = (bf16[512,1024]{1,0:T(8,128)(2,1)S(1)}, bf16[512,1024]{1,0:T(8,128)(2,1)}, u32[]{:S(2)}) copy-start(bf16[512,1024]{1,0:T(8,128)(2,1)} %queries.3) | copy-start | bytes 3145732
  16.3 8.0 %collective-permute-start.1 = (s16[16,4224]{1,0:T(8,128)(2,1)S(1)}, s16[16,4224]{1,0:T(8,128)(2,1)S(1)}, u32[]{:S(2)}, u32[]{:S(2)}) collective-permute-start(s16[16,4224]{1,0:T(8,128)(2,1)S(1)} %get-tuple-element.32), channel_id=1, source_target_pairs={{0,1},{1,0},{2,3},{3,2},{4,5},{5,4},{6,7},{7,6},{8,9},{9,8},{10,11... | collective-permute-start | bytes 405512 | tf_op jit(solution)/shard_map/ppermute | solution.py:27
  18.0 5.8 %collective-permute-start.2 = (s16[16,1152]{1,0:T(8,128)(2,1)S(1)}, s16[16,1152]{1,0:T(8,128)(2,1)S(1)}, u32[]{:S(2)}, u32[]{:S(2)}) collective-permute-start(s16[16,1152]{1,0:T(8,128)(2,1)S(1)} %get-tuple-element.33), channel_id=1, source_target_pairs={{0,3},{1,2},{2,1},{3,0},{4,7},{5,6},{6,5},{7,4},{8,11},{9,10},{10,... | collective-permute-start | bytes 110600 | tf_op jit(solution)/shard_map/ppermute | solution.py:27
  18.2 5.5 %collective-permute-start.3 = (s16[16,1152]{1,0:T(8,128)(2,1)S(1)}, s16[16,1152]{1,0:T(8,128)(2,1)S(1)}, u32[]{:S(2)}, u32[]{:S(2)}) collective-permute-start(s16[16,1152]{1,0:T(8,128)(2,1)S(1)} %get-tuple-element.34), channel_id=1, source_target_pairs={{0,2},{1,3},{2,0},{3,1},{4,6},{5,7},{6,4},{7,5},{8,10},{9,11},{10,... | collective-permute-start | bytes 110600 | tf_op jit(solution)/shard_map/ppermute | solution.py:27
  19.9 4.4 %collective-permute-start.4 = (s16[16,1152]{1,0:T(8,128)(2,1)S(1)}, s16[16,1152]{1,0:T(8,128)(2,1)S(1)}, u32[]{:S(2)}, u32[]{:S(2)}) collective-permute-start(s16[16,1152]{1,0:T(8,128)(2,1)S(1)} %get-tuple-element.35), channel_id=1, source_target_pairs={{0,1},{1,0},{2,3},{3,2},{4,5},{5,4},{6,7},{7,6},{8,9},{9,8},{10,11... | collective-permute-start | bytes 110600 | tf_op jit(solution)/shard_map/ppermute | solution.py:27
  24.8 1.2 %collective-permute-start.5 = (bf16[16,512]{1,0:T(8,128)(2,1)S(1)}, bf16[16,512]{1,0:T(8,128)(2,1)S(1)}, u32[]{:S(2)}, u32[]{:S(2)}) collective-permute-start(bf16[16,512]{1,0:T(8,128)(2,1)S(1)} %train.1.mine), channel_id=1, source_target_pairs={{0,4},{4,0},{8,12},{12,8},{1,5},{5,1},{9,13},{13,9},{2,6},{6,2},{1... | collective-permute-start | bytes 49160 | tf_op jit(solution)/shard_map/ppermute | solution.py:27
  24.9 8.7 %collective-permute-start.6 = (bf16[128,1024]{1,0:T(8,128)(2,1)S(1)}, bf16[128,1024]{1,0:T(8,128)(2,1)S(1)}, u32[]{:S(2)}, u32[]{:S(2)}) collective-permute-start(bf16[128,1024]{1,0:T(8,128)(2,1)S(1)} %copy-done.2), channel_id=1, source_target_pairs={{0,8},{4,12},{8,0},{12,4},{1,9},{5,13},{9,1},{13,5},{2,10},{6,14},... | collective-permute-start | bytes 786440 | tf_op jit(solution)/shard_map/ppermute | solution.py:27
  27.1 6.6 %collective-permute-start.8 = (f32[32,128]{1,0:T(8,128)S(1)}, f32[32,128]{1,0:T(8,128)S(1)}, u32[]{:S(2)}, u32[]{:S(2)}) collective-permute-start(f32[32,128]{1,0:T(8,128)S(1)} %get-tuple-element.39), channel_id=1, source_target_pairs={{0,7},{1,6},{2,5},{3,4},{4,3},{5,2},{6,1},{7,0},{8,15},{9,14},{10,... | collective-permute-start | bytes 49160 | tf_op jit(solution)/shard_map/ppermute | solution.py:33
  29.2 4.5 %collective-permute-start.9 = (f32[32,128]{1,0:T(8,128)S(1)}, f32[32,128]{1,0:T(8,128)S(1)}, u32[]{:S(2)}, u32[]{:S(2)}) collective-permute-start(f32[32,128]{1,0:T(8,128)S(1)} %get-tuple-element.40), channel_id=1, source_target_pairs={{0,6},{1,7},{2,4},{3,5},{4,2},{5,3},{6,0},{7,1},{8,14},{9,15},{10,... | collective-permute-start | bytes 49160 | tf_op jit(solution)/shard_map/ppermute | solution.py:33
  30.0 3.6 %collective-permute-start.10 = (f32[32,128]{1,0:T(8,128)S(1)}, f32[32,128]{1,0:T(8,128)S(1)}, u32[]{:S(2)}, u32[]{:S(2)}) collective-permute-start(f32[32,128]{1,0:T(8,128)S(1)} %get-tuple-element.41), channel_id=1, source_target_pairs={{0,5},{1,4},{2,7},{3,6},{4,1},{5,0},{6,3},{7,2},{8,13},{9,12},{10,... | collective-permute-start | bytes 49160 | tf_op jit(solution)/shard_map/ppermute | solution.py:33
  33.8 1.2 %collective-permute-start.11 = (f32[2,2,8,128]{3,2,1,0:T(8,128)S(1)}, f32[2,2,8,128]{3,2,1,0:T(8,128)S(1)}, u32[]{:S(2)}, u32[]{:S(2)}) collective-permute-start(f32[2,2,8,128]{3,2,1,0:T(8,128)S(1)} %get-tuple-element.44), channel_id=1, source_target_pairs={{0,4},{4,0},{8,12},{12,8},{1,5},{5,1},{9,13},{13,9},{2,6},{6,2},{1... | collective-permute-start | bytes 49160 | tf_op jit(solution)/shard_map/ppermute | solution.py:27
